TPU v7x, 32 devices: a whole 2x2x4 slice. The times are simulated.
32 devices in a mesh: narrow: 4 (over x, core), wide: 8 (over z, y).
Axes of the slice: x: 2, y: 2, z: 4, core: 2. Of those that a mesh axis runs over, the one named last changes fastest.
Arguments:
- tokens: bfloat16 [16384, 1024], P(('narrow', 'wide')), may hold values from -6 to 6
- lengths: int32 [32], P(('narrow', 'wide')), may hold values from 64 to 512, as said below
- buckets: int32 [512], replicated, may hold values from 0 to 31, as said below
- ln1_gain: bfloat16 [1024], P('wide'), may hold values from 0.099609375 to 1.8984375
- ln1_bias: bfloat16 [1024], P('wide'), may hold values from -3 to 3
- w_qkv: bfloat16 [1024, 3072], P('wide'), may hold values from -0.1875 to 0.1875
- rel_table: bfloat16 [512], P('wide'), may hold values from -4 to 4
- w_out: bfloat16 [1024, 1024], P('wide'), may hold values from -2 to 2
- ln2_gain: bfloat16 [1024], P('wide'), may hold values from 0.099609375 to 1.8984375
- ln2_bias: bfloat16 [1024], P('wide'), may hold values from -3 to 3
- w_up: bfloat16 [1024, 4096], P('wide'), may hold values from -0.1875 to 0.1875
- w_down: bfloat16 [4096, 1024], P('wide'), may hold values from -0.09375 to 0.09375
- cotangent: bfloat16 [16384, 1024], P(('narrow', 'wide')), may hold values from -6 to 6
Outputs:
- output: bfloat16 [16384, 1024], P(('narrow', 'wide'))
- grad_tokens: float32 [16384, 1024], P(('narrow', 'wide'))
- grad_ln1_gain: float32 [1024], P('wide')
- grad_ln1_bias: float32 [1024], P('wide')
- grad_w_qkv: float32 [1024, 3072], P('wide')
- grad_rel_table: float32 [512], P('wide')
- grad_w_out: float32 [1024, 1024], P('wide')
- grad_ln2_gain: float32 [1024], P('wide')
- grad_ln2_bias: float32 [1024], P('wide')
- grad_w_up: float32 [1024, 4096], P('wide')
- grad_w_down: float32 [4096, 1024], P('wide')
Inputs may be any that keep to these rules, and one draw needn't show every extreme that they name: `lengths`: in each aligned group of eight sequences exactly one has length 512. `buckets`: never falls as the distance grows; 0 at distance 0; every bucket occurs.
All inputs are finite; a program needn't handle non-finite values.
Results may differ from a plain program's by a relative error of at most 0.015.
Values may be sent and summed in bfloat16 or wider, within the bound.
No kernel may reach another device: no remote copies, remote signals or barrier semaphores. Data moves between devices by JAX's collectives and lax.ppermute only.
A program may use at most 320 MiB of HBM per device.

v0:
```python
import jax
import jax.numpy as jnp
from jax import lax
from jax.sharding import PartitionSpec as P

HEADS = 16
HEAD_DIM = 64
BUCKETS = 32


norm_eps = 1e-05
neg_large = -1e30


def layer_norm(values, gain, shift):
    center = values - jnp.mean(values, axis=-1, keepdims=True)
    spread = jnp.mean(center * center, axis=-1, keepdims=True)
    return center * lax.rsqrt(spread + norm_eps) * gain + shift


def diagonal_sums(grad_scores, row_start):
    head_count, row_count, col_count = grad_scores.shape
    flipped = grad_scores[:, :, ::-1]
    padded = jnp.pad(flipped, ((0, 0), (0, 0), (0, row_count)))
    flat_rows = padded.reshape(head_count, row_count * (col_count + row_count))
    sheared = flat_rows[:, : row_count * (col_count + row_count - 1)].reshape(
        head_count, row_count, col_count + row_count - 1
    )
    summed = jnp.pad(jnp.sum(sheared, axis=1), ((0, 0), (0, col_count)))
    offset = col_count - 1 - row_start
    return summed[:, offset : offset + col_count]


def local(
    tokens,
    lengths,
    buckets,
    ln1_gain,
    ln1_bias,
    w_qkv,
    rel_table,
    w_out,
    ln2_gain,
    ln2_bias,
    w_up,
    w_down,
    cotangent,
):
    slot_len, model_width = tokens.shape
    score_scale = HEAD_DIM ** (-0.5)
    attn_set = (
        lax.all_gather(ln1_gain, "wide", axis=0, tiled=True),
        lax.all_gather(ln1_bias, "wide", axis=0, tiled=True),
        lax.all_gather(w_qkv, "wide", axis=0, tiled=True),
        lax.all_gather(rel_table, "wide", axis=0, tiled=True),
        lax.all_gather(w_out, "wide", axis=0, tiled=True),
    )
    ffn_set = (
        lax.all_gather(ln2_gain, "wide", axis=0, tiled=True),
        lax.all_gather(ln2_bias, "wide", axis=0, tiled=True),
        lax.all_gather(w_up, "wide", axis=0, tiled=True),
        lax.all_gather(w_down, "wide", axis=0, tiled=True),
    )
    gain_first = attn_set[0].astype(jnp.float32)
    shift_first = attn_set[1].astype(jnp.float32)
    gain_second = ffn_set[0].astype(jnp.float32)
    shift_second = ffn_set[1].astype(jnp.float32)
    position = jnp.arange(slot_len, dtype=jnp.int32)
    seq_length = lengths[0]
    valid_rows = (position < seq_length).astype(jnp.float32)[:, None]
    onehot_bucket = (buckets[:, None] == jnp.arange(BUCKETS, dtype=jnp.int32)[None, :]).astype(
        jnp.float32
    )
    table_heads = attn_set[3].astype(jnp.float32).reshape(HEADS, BUCKETS)
    by_distance = jnp.dot(table_heads, onehot_bucket.T, precision=lax.Precision.HIGHEST)
    block_rows = min(512, slot_len)
    row_starts = list(range(0, slot_len, block_rows))

    def block_scores(row_start, query_rows, keys_all):
        rows_here = row_start + jnp.arange(block_rows, dtype=jnp.int32)
        distance = jnp.maximum(rows_here[:, None] - position[None, :], 0)
        allowed = (position[None, :] <= rows_here[:, None]) & (position[None, :] < seq_length)
        raw_scores = jnp.einsum(
            "rhd,shd->hrs", query_rows, keys_all, preferred_element_type=jnp.float32
        )
        scores = raw_scores * score_scale + jnp.take(by_distance, distance, axis=1)
        return jnp.where(allowed[None], scores, neg_large)

    inputs = tokens.astype(jnp.float32)
    normed_one = layer_norm(inputs, gain_first, shift_first).astype(jnp.bfloat16)
    packed = jnp.dot(normed_one, attn_set[2], preferred_element_type=jnp.float32).astype(
        jnp.bfloat16
    )
    queries = packed[:, :model_width].reshape(slot_len, HEADS, HEAD_DIM)
    keys_all = packed[:, model_width : 2 * model_width].reshape(slot_len, HEADS, HEAD_DIM)
    values_all = packed[:, 2 * model_width :].reshape(slot_len, HEADS, HEAD_DIM)
    mixed_blocks = []
    log_totals = []
    for row_start in row_starts:
        query_rows = queries
        scores = block_scores(row_start, query_rows, keys_all)
        row_max = jnp.max(scores, axis=-1, keepdims=True)
        weights_exp = jnp.exp(scores - row_max)
        row_total = jnp.sum(weights_exp, axis=-1, keepdims=True)
        probs = (weights_exp / row_total).astype(jnp.bfloat16)
        mixed = jnp.einsum("hrs,shd->rhd", probs, values_all, preferred_element_type=jnp.float32)
        mixed_blocks.append(mixed.reshape(block_rows, model_width))
        log_totals.append(row_max + jnp.log(row_total))
    attended = mixed_blocks[0].astype(jnp.bfloat16)
    attn_out = jnp.dot(attended, attn_set[4], preferred_element_type=jnp.float32)
    middle = inputs + valid_rows * attn_out
    normed_two = layer_norm(middle, gain_second, shift_second).astype(jnp.bfloat16)
    up_proj = jnp.dot(normed_two, ffn_set[2], preferred_element_type=jnp.float32)
    hidden = jax.nn.gelu(up_proj).astype(jnp.bfloat16)
    ffn_out = jnp.dot(hidden, ffn_set[3], preferred_element_type=jnp.float32)
    output = (middle + valid_rows * ffn_out).astype(jnp.bfloat16)
    ffn_back = (
        lax.all_gather(ln2_gain, "wide", axis=0, tiled=True),
        lax.all_gather(ln2_bias, "wide", axis=0, tiled=True),
        lax.all_gather(w_up, "wide", axis=0, tiled=True),
        lax.all_gather(w_down, "wide", axis=0, tiled=True),
    )
    attn_back = (
        lax.all_gather(ln1_gain, "wide", axis=0, tiled=True),
        lax.all_gather(ln1_bias, "wide", axis=0, tiled=True),
        lax.all_gather(w_qkv, "wide", axis=0, tiled=True),
        lax.all_gather(rel_table, "wide", axis=0, tiled=True),
        lax.all_gather(w_out, "wide", axis=0, tiled=True),
    )
    cotan = cotangent.astype(jnp.float32)
    grad_ffn = (valid_rows * cotan).astype(jnp.bfloat16)
    grad_down = jnp.dot(hidden.T, grad_ffn, preferred_element_type=jnp.float32)
    grad_hidden = jnp.dot(grad_ffn, ffn_back[3].T, preferred_element_type=jnp.float32)
    gelu_value, gelu_pull = jax.vjp(jax.nn.gelu, up_proj)
    grad_upproj = gelu_pull(grad_hidden)[0].astype(jnp.bfloat16)
    grad_up = jnp.dot(normed_two.T, grad_upproj, preferred_element_type=jnp.float32)
    grad_normtwo = jnp.dot(grad_upproj, ffn_back[2].T, preferred_element_type=jnp.float32)
    norm_value, norm_pull = jax.vjp(
        layer_norm, middle, ffn_back[0].astype(jnp.float32), ffn_back[1].astype(jnp.float32)
    )
    grad_from_norm, grad_gain_two, grad_shift_two = norm_pull(grad_normtwo)
    grad_middle = cotan + grad_from_norm
    ffn_shares = (
        lax.psum_scatter(grad_gain_two, "wide", scatter_dimension=0, tiled=True),
        lax.psum_scatter(grad_shift_two, "wide", scatter_dimension=0, tiled=True),
        lax.psum_scatter(grad_up, "wide", scatter_dimension=0, tiled=True),
        lax.psum_scatter(grad_down, "wide", scatter_dimension=0, tiled=True),
    )
    grad_branch = (valid_rows * grad_middle).astype(jnp.bfloat16)
    grad_out = jnp.dot(attended.T, grad_branch, preferred_element_type=jnp.float32)
    grad_attended = jnp.dot(grad_branch, attn_back[4].T, preferred_element_type=jnp.float32).astype(
        jnp.bfloat16
    )
    grad_attended = grad_attended.reshape(slot_len, HEADS, HEAD_DIM)
    grad_query_blocks = []
    grad_keys = jnp.zeros((slot_len, HEADS, HEAD_DIM), jnp.float32)
    grad_values = jnp.zeros((slot_len, HEADS, HEAD_DIM), jnp.float32)
    distance_sums = jnp.zeros((HEADS, slot_len), jnp.float32)
    for block_index, row_start in enumerate(row_starts):
        query_rows = queries
        scores = block_scores(row_start, query_rows, keys_all)
        probs = jnp.exp(scores - log_totals[block_index])
        probs_low = probs.astype(jnp.bfloat16)
        grad_probs = jnp.einsum(
            "rhd,shd->hrs", grad_attended, values_all, preferred_element_type=jnp.float32
        )
        row_inner = jnp.sum(probs * grad_probs, axis=-1, keepdims=True)
        grad_scores = (probs * (grad_probs - row_inner)).astype(jnp.bfloat16)
        grad_query_blocks.append(
            jnp.einsum("hrs,shd->rhd", grad_scores, keys_all, preferred_element_type=jnp.float32)
            * score_scale
        )
        grad_keys = (
            jnp.einsum("hrs,rhd->shd", grad_scores, query_rows, preferred_element_type=jnp.float32)
            * score_scale
        )
        grad_values = jnp.einsum(
            "hrs,rhd->shd", probs_low, grad_attended, preferred_element_type=jnp.float32
        )
        distance_sums = diagonal_sums(grad_scores.astype(jnp.float32), row_start)
    grad_table = jnp.dot(distance_sums, onehot_bucket, precision=lax.Precision.HIGHEST).reshape(-1)
    grad_queries = grad_query_blocks[0]
    grad_packed = jnp.concatenate(
        [
            grad_queries.reshape(slot_len, model_width),
            grad_keys.reshape(slot_len, model_width),
            grad_values.reshape(slot_len, model_width),
        ],
        axis=1,
    ).astype(jnp.bfloat16)
    grad_qkv = jnp.dot(normed_one.T, grad_packed, preferred_element_type=jnp.float32)
    grad_normone = jnp.dot(grad_packed, attn_back[2].T, preferred_element_type=jnp.float32)
    first_value, first_pull = jax.vjp(
        layer_norm, inputs, attn_back[0].astype(jnp.float32), attn_back[1].astype(jnp.float32)
    )
    grad_from_first, grad_gain_one, grad_shift_one = first_pull(grad_normone)
    grad_tokens = grad_middle + grad_from_first
    attn_shares = (
        lax.psum_scatter(grad_gain_one, "wide", scatter_dimension=0, tiled=True),
        lax.psum_scatter(grad_shift_one, "wide", scatter_dimension=0, tiled=True),
        lax.psum_scatter(grad_qkv, "wide", scatter_dimension=0, tiled=True),
        lax.psum_scatter(grad_table, "wide", scatter_dimension=0, tiled=True),
        lax.psum_scatter(grad_out, "wide", scatter_dimension=0, tiled=True),
    )
    summed = (
        lax.psum(attn_shares[0].astype(jnp.bfloat16), "narrow").astype(jnp.float32),
        lax.psum(attn_shares[1].astype(jnp.bfloat16), "narrow").astype(jnp.float32),
        lax.psum(attn_shares[2].astype(jnp.bfloat16), "narrow").astype(jnp.float32),
        lax.psum(attn_shares[3].astype(jnp.bfloat16), "narrow").astype(jnp.float32),
        lax.psum(attn_shares[4].astype(jnp.bfloat16), "narrow").astype(jnp.float32),
        lax.psum(ffn_shares[0].astype(jnp.bfloat16), "narrow").astype(jnp.float32),
        lax.psum(ffn_shares[1].astype(jnp.bfloat16), "narrow").astype(jnp.float32),
        lax.psum(ffn_shares[2].astype(jnp.bfloat16), "narrow").astype(jnp.float32),
        lax.psum(ffn_shares[3].astype(jnp.bfloat16), "narrow").astype(jnp.float32),
    )
    return (
        output,
        grad_tokens,
        summed[0],
        summed[1],
        summed[2],
        summed[3],
        summed[4],
        summed[5],
        summed[6],
        summed[7],
        summed[8],
    )


def solution(mesh):
    return jax.shard_map(
        local,
        mesh=mesh,
        in_specs=(
            P(("narrow", "wide"), None),
            P(("narrow", "wide")),
            P(),
            P("wide"),
            P("wide"),
            P("wide", None),
            P("wide"),
            P("wide", None),
            P("wide"),
            P("wide"),
            P("wide", None),
            P("wide", None),
            P(("narrow", "wide"), None),
        ),
        out_specs=(
            P(("narrow", "wide"), None),
            P(("narrow", "wide"), None),
            P("wide"),
            P("wide"),
            P("wide", None),
            P("wide"),
            P("wide", None),
            P("wide"),
            P("wide"),
            P("wide", None),
            P("wide", None),
        ),
        check_vma=False,
    )
```

profile of v0, /device:TPU:0, one launch (start us, length us, event | category | flops | bytes accessed | tf_op | source)
XLA Modules:
  0.0 2078.8 jit_solution(3635647872567231681)
XLA Ops:
  10.2 22.3 %all-gather = bf16[8,1,128]{2,1,0:T(2,128)(2,1)S(1)} all-gather(bf16[1,1,128]{2,1,0:T(2,128)(2,1)S(1)} %bitcast.98), channel_id=1, replica_groups=mesh['narrow'=4,'wide'=8] {'wide'}, dimensions={0}, use_global_device_ids=true | all-gather | bytes 2304 | tf_op jit(solution)/shard_map/all_gather | solution.py:52
  32.5 16.6 all-gather.1
  50.6 19.6 all-reduce.1
  70.9 861.5 %gather_fusion = f32[262144,16]{1,0:T(8,128)} fusion(f32[16,512]{0,1:T(8,128)S(1)} %fusion.42, s32[262144]{0:T(1024)S(1)} %broadcast_clamp_fusion), kind=kCustom, calls=%fused_computation.clone | custom fusion | bytes 34603008 | tf_op jit(solution)/shard_map/jit(_take)/gather | solution.py:86
  932.4 72.7 %copy.56 = f32[512,512,16]{0,1,2:T(8,128)} copy(f32[512,512,16]{2,1,0:T(8,128)} %bitcast.9) | data formatting | bytes 33554432 | tf_op jit(solution)/shard_map/jit(_take)/gather | solution.py:86
  1006.4 16.2 all-gather.2
  1022.6 18.4 all-gather.3
  1042.6 6.7 convolution_convert_fusion
  1056.0 11.5 fusion.60
  1067.5 8.4 fusion.1
  1075.9 8.5 fusion.26
  1088.1 10.8 fusion.55
  1098.9 12.9 fusion.9
  1131.5 17.0 multiply_reduce_fusion
  1148.5 8.2 multiply_convert_fusion
  1162.4 7.2 multiply_convert_fusion.2
  1174.6 10.2 fusion.30
  1186.4 11.0 fusion.54
  1198.6 15.3 fusion.35
  1215.3 120.9 %rev.3 = f32[16,512,512]{1,2,0:T(8,128)} reverse(bf16[16,512,512]{1,2,0:T(8,128)(2,1)} %copy-done), dimensions={2} | reverse | bytes 25165824 | tf_op jit(solution)/shard_map/rev | solution.py:23
  1336.2 17.8 copy.70
  1353.9 9.7 pad.6.clone
  1363.7 39.7 %copy.72 = f32[2,8,512,1024]{3,1,2,0:T(8,128)} copy(f32[2,8,512,1024]{3,2,1,0:T(8,128)S(1)} %bitcast.66) | data formatting | bytes 67108864
  1403.4 22.6 %slice.26 = f32[16,523776]{1,0:T(8,128)} slice(f32[16,524288]{1,0:T(8,128)} %bitcast.67), slice={[0:16], [0:523776]} | slice | bytes 67043328 | tf_op jit(solution)/shard_map/slice | solution.py:26
  1426.0 52.0 %reshape.187 = f32[16,512,1023]{2,1,0:T(8,128)} reshape(f32[16,523776]{1,0:T(8,128)} %slice.26) | data formatting | bytes 67043328 | tf_op jit(solution)/shard_map/reshape | solution.py:26
  1478.1 12.5 reduce_sum.153
  1491.0 7.0 fusion.56
  1500.4 35.5 %all-reduce.7 = (bf16[1024]{0:T(1024)(128)(2,1)S(1)}, bf16[1024]{0:T(1024)(128)(2,1)S(1)}, bf16[512]{0:T(512)(128)(2,1)S(1)}, bf16[1024]{0:T(1024)(128)(2,1)S(1)}, bf16[1024]{0:T(1024)(128)(2,1)S(1)}) all-reduce(f32[1024]{0:T(1024)S(1)} %get-tuple-element.14, ...), channel_id=2, replica_groups=mesh['narrow'=4,'wide'=8] {'wide'}, use_global_device_ids=true, to_apply=%region_12.14.clone | all-reduce | flops 4608 | bytes 27648
  1553.6 153.1 %reduce-scatter.9.cloned.1.call-done = f32[128,4096]{1,0:T(8,128)} async-done(((f32[1024,4096]{1,0:T(8,128)}), f32[128,4096]{1,0:T(8,128)}) %reduce-scatter.9.cloned.1.call-update) | async-done | bytes 2097168 | tf_op jit(solution)/shard_map/reduce_scatter | solution.py:146
  1709.4 282.9 %reduce-scatter.11.cloned.1.call-done = f32[512,1024]{1,0:T(8,128)} async-done(((f32[4096,1024]{1,0:T(8,128)}), f32[512,1024]{1,0:T(8,128)}) %reduce-scatter.11.cloned.1.call-update) | async-done | bytes 2097168 | tf_op jit(solution)/shard_map/reduce_scatter | solution.py:147
  1995.0 12.0 add_convert_fusion
  2007.1 57.2 %all-reduce.12.cloned.1.call-done = (bf16[128,3072]{1,0:T(8,128)(2,1)}, bf16[128,1024]{1,0:T(8,128)(2,1)}, bf16[128,4096]{1,0:T(8,128)(2,1)}, bf16[512,1024]{1,0:T(8,128)(2,1)}) async-done(((bf16[128,3072]{1,0:T(8,128)(2,1)}, bf16[128,1024]{1,0:T(8,128)(2,1)}, bf16[128,4096]{1,0:T(8,128)(2,1)}, bf16[512,1024]{1,0:T(8,128)(2,1)}), (bf16[128,3072]{1,0:T(8,128)(2,1)}, bf16[128,1024]{1,0:T(8,128)(2,1)}, ...) | async-done | bytes 3145744 | tf_op jit(solution)/shard_map/psum | solution.py:208
  (196 shorter events, 83.6 us)
Async XLA Ops:
  7.2 41.9 %copy-start.41 = (u32[32]{0:T(128)S(1)}, u32[32]{0:T(128)}, u32[]{:S(2)}) copy-start(u32[32]{0:T(128)} %constant.54) | copy-start | bytes 388
  7.2 25.3 %copy-start.43 = (bf16[128]{0:T(256)(128)(2,1)S(1)}, bf16[128]{0:T(256)(128)(2,1)}, u32[]{:S(2)}) copy-start(bf16[128]{0:T(256)(128)(2,1)} %param.19) | copy-start | bytes 772
  7.2 43.1 %copy-start.47 = (bf16[64]{0:T(256)(128)(2,1)S(1)}, bf16[64]{0:T(256)(128)(2,1)}, u32[]{:S(2)}) copy-start(bf16[64]{0:T(256)(128)(2,1)} %param.21) | copy-start | bytes 388
  7.2 63.3 %copy-start.39 = (s32[512]{0:T(512)S(1)}, s32[512]{0:T(512)}, u32[]{:S(2)}) copy-start(s32[512]{0:T(512)} %param.17) | copy-start | bytes 6148
  7.2 1035.3 %all-gather.9.cloned.1.call-start = ((), (), s32[]{:S(2)}) async-start(), calls=%async_computation.4 | async-start | bytes 7077888 | tf_op jit(solution)/shard_map/all_gather | solution.py:54
  8.0 1076.4 %all-gather.11.cloned.1.call-start = ((), (), s32[]{:S(2)}) async-start(), calls=%async_computation.5 | async-start | bytes 2359296 | tf_op jit(solution)/shard_map/all_gather | solution.py:56
  8.7 1079.3 %all-gather.13.cloned.1.call-start = ((), (), s32[]{:S(2)}) async-start(), calls=%async_computation.6 | async-start | bytes 9437184 | tf_op jit(solution)/shard_map/all_gather | solution.py:61
  9.5 1089.5 %all-gather.15.cloned.1.call-start = ((), (), s32[]{:S(2)}) async-start(), calls=%async_computation.7 | async-start | bytes 9437184 | tf_op jit(solution)/shard_map/all_gather | solution.py:62
  10.0 1539.3 %reduce-scatter.7.cloned.1.call-start = ((), (), s32[]{:S(2)}) async-start(), calls=%async_computation.9 | async-start | bytes 4718592 | tf_op jit(solution)/shard_map/reduce_scatter | solution.py:203
  49.1 993.5 %copy-start.34 = (f32[8,1,128]{2,1,0:T(1,128)}, f32[8,1,128]{2,1,0:T(1,128)S(1)}, u32[]{:S(2)}) copy-start(f32[8,1,128]{2,1,0:T(1,128)S(1)} %convert_element_type.178) | copy-start | bytes 12292
  932.4 73.9 %copy-start.44 = (bf16[128]{0:T(256)(128)(2,1)S(1)}, bf16[128]{0:T(256)(128)(2,1)}, u32[]{:S(2)}) copy-start(bf16[128]{0:T(256)(128)(2,1)} %param.23) | copy-start | bytes 772
  932.4 90.1 %copy-start.45 = (bf16[128]{0:T(256)(128)(2,1)S(1)}, bf16[128]{0:T(256)(128)(2,1)}, u32[]{:S(2)}) copy-start(bf16[128]{0:T(256)(128)(2,1)} %param.24) | copy-start | bytes 772
  932.4 108.6 %copy-start.1 = (bf16[512,1024]{1,0:T(8,128)(2,1)S(1)}, bf16[512,1024]{1,0:T(8,128)(2,1)}, u32[]{:S(2)}) copy-start(bf16[512,1024]{1,0:T(8,128)(2,1)} %param.15) | copy-start | bytes 3145732
  1022.6 94.8 %copy-start.30 = (f32[8,1,128]{2,1,0:T(1,128)}, f32[8,1,128]{2,1,0:T(1,128)S(1)}, u32[]{:S(2)}) copy-start(f32[8,1,128]{2,1,0:T(1,128)S(1)} %convert_element_type.179) | copy-start | bytes 12292
  1041.0 47.1 %copy-start.35 = (f32[8,1,128]{2,1,0:T(1,128)}, f32[8,1,128]{2,1,0:T(1,128)S(1)}, u32[]{:S(2)}) copy-start(f32[8,1,128]{2,1,0:T(1,128)S(1)} %convert_element_type.180) | copy-start | bytes 12292
  1051.5 16.1 copy-start.9
  1053.4 14.2 copy-start.7
  1087.6 29.7 %copy-start.4 = (f32[512,1024]{1,0:T(8,128)}, f32[512,1024]{1,0:T(8,128)S(1)}, u32[]{:S(2)}) copy-start(f32[512,1024]{1,0:T(8,128)S(1)} %get-tuple-element.43) | copy-start | bytes 6291460
  1087.7 29.7 %copy-start.28 = (f32[512]{0:T(512)}, f32[512]{0:T(512)S(1)}, u32[]{:S(2)}) copy-start(f32[512]{0:T(512)S(1)} %broadcast_multiply_fusion) | copy-start | bytes 6148
  1088.0 29.3 %copy-start.32 = (f32[512]{0:T(512)}, f32[512]{0:T(512)S(1)}, u32[]{:S(2)}) copy-start(f32[512]{0:T(512)S(1)} %fusion.47) | copy-start | bytes 6148
  1124.0 427.1 %reduce-scatter.5.cloned.1.call-start = ((), (), s32[]{:S(2)}) async-start(), calls=%async_computation.8 | async-start | bytes 14155776 | tf_op jit(solution)/shard_map/reduce_scatter | solution.py:201
  1131.5 17.0 slice-start
  1131.5 17.0 slice-start.1
  1131.5 17.0 slice-start.2
  1131.5 17.0 slice-start.3
  1184.8 521.8 %reduce-scatter.9.cloned.1.call-start = ((), (), s32[]{:S(2)}) async-start(), calls=%async_computation.10 | async-start | bytes 18874368 | tf_op jit(solution)/shard_map/reduce_scatter | solution.py:146
  1197.4 794.8 %reduce-scatter.11.cloned.1.call-start = ((), (), s32[]{:S(2)}) async-start(), calls=%async_computation.11 | async-start | bytes 18874368 | tf_op jit(solution)/shard_map/reduce_scatter | solution.py:147
  1214.0 850.3 %all-reduce.12.cloned.1.call-start = ((), (), s32[]{:S(2)}) async-start(), calls=%async_computation.12 | async-start | bytes 6291456 | tf_op jit(solution)/shard_map/psum | solution.py:208
  1478.1 12.9 copy-start.15
  1491.0 54.1 %copy-start.23 = (f32[512]{0:T(512)S(1)}, f32[512]{0:T(512)}, u32[]{:S(2)}) copy-start(f32[512]{0:T(512)} %copy-done.22) | copy-start | bytes 6148
  1498.0 47.2 %copy-start.3 = (f32[512,1024]{1,0:T(8,128)S(1)}, f32[512,1024]{1,0:T(8,128)}, u32[]{:S(2)}) copy-start(f32[512,1024]{1,0:T(8,128)} %copy-done.2) | copy-start | bytes 6291460
  1553.6 441.5 %copy-start.6 = (f32[512,1024]{1,0:T(8,128)S(1)}, f32[512,1024]{1,0:T(8,128)}, u32[]{:S(2)}) copy-start(f32[512,1024]{1,0:T(8,128)} %copy-done.4) | copy-start | bytes 6291460
  (30 other events, 160.0 us)
Sparse Core Ops, SparseCore 0:
  10.2 102.0 all-gather.8
  114.4 47.5 all-gather.10
  164.1 123.4 all-gather.12
  289.6 123.1 all-gather.14
  1124.1 84.8 reduce-scatter.6
  1212.9 207.0 reduce-scatter.4
  1424.2 282.3 reduce-scatter.8
  1710.4 281.7 reduce-scatter.10
  1996.2 68.0 all-reduce.11
where the time goes:
time: 2100 us; the launch traced here: 2080 us
  local copies, waits for them, and re-layouts  1220 us (58%)
  waiting for transfers between devices  496 us (24%)
  matrix products  153 us (7%)
  blocking collectives  135 us (6%)
  other arithmetic  58.3 us (3%)
    gather x2, local copies, waits for them, and re-layouts, block_scores(): scores = raw_scores * score_scale + jnp.take(by_distance, distance, axis=1)  934 us
    reduce_scatter x1, waiting for transfers between devices, local(): lax.psum_scatter(grad_down, 'wide', scatter_dimension=0, tiled=True)  283 us
    reduce_scatter x1, waiting for transfers between devices, local(): lax.psum_scatter(grad_up, 'wide', scatter_dimension=0, tiled=True)  153 us
    rev x1, local copies, waits for them, and re-layouts, diagonal_sums(): flipped = grad_scores[:, :, ::-1]  121 us
    unnamed x117, local copies, waits for them, and re-layouts  69.5 us
    psum x1, waiting for transfers between devices, local(): lax.psum(attn_shares[2].astype(jnp.bfloat16), 'narrow').astype(jnp.float32)  57.2 us
    unnamed x2, blocking collectives  55.1 us
    reshape x1, local copies, waits for them, and re-layouts, diagonal_sums(): flat_rows[:, :row_count * (col_count + row_count - 1)]  52 us
  transfers between devices with their start and end apart: 9, of which 3 were waited for; matrix products, arithmetic and copies ran while one was open for 67% of the time, Pallas kernels for 0%

commit v1 on v0

v1 whole, which is shorter than its diff:
```python
import functools

import jax
import jax.numpy as jnp
from jax import lax
from jax.experimental import pallas as pl
from jax.experimental.layout import Layout, with_layout_constraint
from jax.experimental.pallas import tpu as pltpu
from jax.sharding import PartitionSpec as P

HEADS = 16
HEAD_DIM = 64
BUCKETS = 32
TILE = 128
PAIR = 2 * HEAD_DIM

norm_eps = 1e-05
neg_large = -1e30
f32 = jnp.float32
bf16 = jnp.bfloat16
VMEM_LIMIT = 56 * 1024 * 1024


PEAK = 1.15e15


def cost(us, share=1.0):
    return pl.CostEstimate(flops=int(us * share * 1e-6 * PEAK), bytes_accessed=0, transcendentals=0)


def dot(a, b, dims=((1,), (0,))):
    return lax.dot_general(a, b, (dims, ((), ())), preferred_element_type=f32)


NT = ((1,), (1,))
TN = ((0,), (0,))


def block_of(x):
    zeros = (0,) * x.ndim
    return pl.BlockSpec(x.shape, lambda i: zeros)


def cut_attn_kernel(n_ref, qkv_ref, out_ref, small_ref, o_ref):
    n = n_ref[0]
    model = out_ref.shape[1]
    mine = model // 4
    at = 0
    for p in range(mine // PAIR):
        for part in range(3):
            start = pl.multiple_of(part * model + n * mine + p * PAIR, PAIR)
            o_ref[:, at : at + PAIR] = qkv_ref[:, pl.ds(start, PAIR)]
            at += PAIR
    o_ref[:, at : at + mine] = out_ref[:, pl.ds(pl.multiple_of(n * mine, mine), mine)]
    at += mine
    o_ref[:, at:] = jnp.zeros((o_ref.shape[0], TILE), bf16)
    o_ref[:16, at:] = small_ref[...]


def cut_attn(n, w_qkv, w_out, small):
    rows, model = w_out.shape
    return pl.pallas_call(
        cut_attn_kernel,
        grid=(1,),
        in_specs=[pl.BlockSpec(memory_space=pltpu.SMEM)]
        + [block_of(x) for x in (w_qkv, w_out, small)],
        out_specs=pl.BlockSpec((rows, model + TILE), lambda i: (0, 0)),
        out_shape=jax.ShapeDtypeStruct((rows, model + TILE), bf16),
        cost_estimate=cost(2),
        name="cut_attn",
    )(n, w_qkv, w_out, small)


def cut_ffn_kernel(n_ref, up_ref, down_ref, o_ref):
    n = n_ref[0]
    size = down_ref.shape[0]
    model = down_ref.shape[1]
    for d in range(model // size):
        start = pl.multiple_of(d * 4 * size + n * size, size)
        o_ref[0, :, d * size : (d + 1) * size] = up_ref[:, pl.ds(start, size)]
    o_ref[1] = down_ref[...]


def cut_ffn(n, w_up, w_down):
    rows = w_up.shape[0]
    quarter, model = w_down.shape[0] // 4, w_down.shape[1]
    return pl.pallas_call(
        cut_ffn_kernel,
        grid_spec=pltpu.PrefetchScalarGridSpec(
            num_scalar_prefetch=1,
            grid=(1,),
            in_specs=[
                pl.BlockSpec(w_up.shape, lambda i, n: (0, 0)),
                pl.BlockSpec((quarter, model), lambda i, n: (n[0], 0)),
            ],
            out_specs=pl.BlockSpec((2, rows, model), lambda i, n: (0, 0, 0)),
        ),
        out_shape=jax.ShapeDtypeStruct((2, rows, model), bf16),
        cost_estimate=cost(2, 0.05),
        name="cut_ffn",
    )(n, w_up, w_down)


def small_kernel(where_ref, *refs):
    out_ref = refs[-1]
    out_ref[...] = jnp.zeros_like(out_ref)
    lane = lax.broadcasted_iota(jnp.int32, (1, TILE), 1)
    for i, ref in enumerate(refs[:-1]):
        d = where_ref[i]
        got = ref[...].astype(f32)
        start = pl.multiple_of(d * TILE, TILE)
        for v in range(4):
            out_ref[v : v + 1, pl.ds(start, TILE)] = got[v : v + 1]
        rel = got[4:5]
        odd = lax.rem(d, 2) == 1
        rel = jnp.where(odd, pltpu.roll(rel, TILE // 2, 1), rel)
        rel = jnp.where((lane >= TILE // 2) == odd, rel, 0.0)
        start = pl.multiple_of((d // 2) * TILE, TILE)
        out_ref[4:5, pl.ds(start, TILE)] += rel


def small_rows(where, pieces, at):
    model = len(pieces) * TILE
    return pl.pallas_call(
        small_kernel,
        grid=(1,),
        in_specs=[pl.BlockSpec(memory_space=pltpu.SMEM)]
        + [pl.BlockSpec((16, TILE), lambda i: (0, at // TILE))] * len(pieces),
        out_specs=pl.BlockSpec((8, model), lambda i: (0, 0)),
        out_shape=jax.ShapeDtypeStruct((8, model), f32),
        cost_estimate=cost(2),
        name="small_rows",
    )(where, *pieces)


def tiles_kernel(n_ref, small_ref, buckets_ref, out_ref):
    heads, count = out_ref.shape[:2]
    lanes = heads * BUCKETS
    slot = buckets_ref.shape[1]
    rel = small_ref[4:5, pl.ds(pl.multiple_of(n_ref[0] * lanes, lanes), lanes)]
    head = lax.broadcasted_iota(jnp.int32, (8, lanes), 0)
    lane = lax.broadcasted_iota(jnp.int32, (8, lanes), 1)
    table = jnp.where(lane // BUCKETS == head, rel, 0.0).astype(bf16)
    bucket = lax.broadcasted_iota(jnp.int32, (lanes, slot), 0) % BUCKETS
    onehot = (buckets_ref[...] == bucket).astype(f32).astype(bf16)
    by_distance = dot(table, onehot)
    row = lax.broadcasted_iota(jnp.int32, (TILE, TILE), 0)
    col = lax.broadcasted_iota(jnp.int32, (TILE, TILE), 1)
    for h in range(heads):
        for delta in range(count):
            here = by_distance[h : h + 1, delta * TILE : (delta + 1) * TILE]
            below = by_distance[h : h + 1, max(delta - 1, 0) * TILE : max(delta, 1) * TILE]
            wide = jnp.broadcast_to(jnp.concatenate([here, below], axis=1), (TILE, 2 * TILE))
            tile = pltpu.roll(wide, 0, 1, stride=1, stride_axis=0)[:, :TILE].T
            if delta == 0:
                tile = jnp.where(col <= row, tile, neg_large)
            out_ref[h, delta] = tile


def bias_tiles(n, small, buckets, heads):
    slot = buckets.shape[0]
    buckets = buckets.reshape(1, slot)
    shape = (heads, slot // TILE, TILE, TILE)
    return pl.pallas_call(
        tiles_kernel,
        grid=(1,),
        in_specs=[pl.BlockSpec(memory_space=pltpu.SMEM), block_of(small), block_of(buckets)],
        out_specs=pl.BlockSpec(shape, lambda i: (0, 0, 0, 0)),
        out_shape=jax.ShapeDtypeStruct(shape, f32),
        cost_estimate=cost(4),
        name="bias_tiles",
    )(n, small, buckets)


def normalized(v):
    center = v - jnp.mean(v, axis=-1, keepdims=True)
    factor = lax.rsqrt(jnp.mean(center * center, axis=-1, keepdims=True) + norm_eps)
    return center * factor, factor


def xhat_kernel(*refs):
    out_ref = refs[-1]
    at = 0
    for ref in refs[:-1]:
        rows = ref.shape[0]
        out_ref[at : at + rows] = normalized(ref[...].astype(f32))[0]
        at += rows


def xhat_of(pieces):
    slot, model = sum(p.shape[0] for p in pieces), pieces[0].shape[1]
    return pl.pallas_call(
        xhat_kernel,
        grid=(1,),
        in_specs=[block_of(p) for p in pieces],
        out_specs=pl.BlockSpec((slot, model), lambda i: (0, 0)),
        out_shape=jax.ShapeDtypeStruct((slot, model), f32),
        compiler_params=pltpu.CompilerParams(vmem_limit_bytes=VMEM_LIMIT),
        cost_estimate=cost(2.5, 0.05),
        name="xhat",
    )(*pieces)


def qkv_kernel(count, where_ref, small_ref, *refs):
    xhats, pieces = refs[:4], refs[4 : 4 + count]
    norm_ref, packed_ref, wq_ref, wo_ref, w_ref, x_ref, sems, x_sems = refs[4 + count :]
    step = pl.program_id(0)
    width = wq_ref.shape[1]

    def fetch(r):
        return pltpu.make_async_copy(xhats[r], x_ref.at[r % 2], x_sems.at[r % 2])

    @pl.when(step == 0)
    def _():
        fetch(0).start()
        copies = []
        for i, piece in enumerate(pieces):
            size = piece.shape[0]
            start = pl.multiple_of(where_ref[i] * size, size)
            copies.append(pltpu.make_async_copy(piece, w_ref.at[pl.ds(start, size)], sems.at[i]))
            copies[-1].start()
        for copy in copies:
            copy.wait()
        wq_ref[...] = w_ref[:, :width]
        wo_ref[...] = w_ref[:, width : width + wo_ref.shape[1]]

    for r in range(4):

        @pl.when(step == r)
        def _(r=r):
            if r < 3:
                fetch(r + 1).start()
            fetch(r).wait()

    norm = (x_ref[lax.rem(step, 2)] * small_ref[0:1] + small_ref[1:2]).astype(bf16)
    norm_ref[...] = norm
    packed_ref[...] = dot(norm, wq_ref[...]).astype(bf16)


def qkv_of(where, small, xhats, pieces, width):
    slot, model = xhats[0].shape
    total = pieces[0].shape[1]
    out = model // 4
    whole = lambda shape: pl.BlockSpec(shape, lambda i: (0, 0))
    rows = lambda cols: pl.BlockSpec((slot, cols), lambda i: (i, 0))
    return pl.pallas_call(
        functools.partial(qkv_kernel, len(pieces)),
        grid=(4,),
        in_specs=[pl.BlockSpec(memory_space=pltpu.SMEM), whole(small.shape)]
        + [pl.BlockSpec(memory_space=pl.ANY)] * (4 + len(pieces)),
        out_specs=[rows(model), rows(width), whole((model, width)), whole((model, out))],
        out_shape=[
            jax.ShapeDtypeStruct((4 * slot, model), bf16),
            jax.ShapeDtypeStruct((4 * slot, width), bf16),
            jax.ShapeDtypeStruct((model, width), bf16),
            jax.ShapeDtypeStruct((model, out), bf16),
        ],
        scratch_shapes=[
            pltpu.VMEM((model, total), bf16),
            pltpu.VMEM((2, slot, model), f32),
            pltpu.SemaphoreType.DMA((len(pieces),)),
            pltpu.SemaphoreType.DMA((2,)),
        ],
        compiler_params=pltpu.CompilerParams(vmem_limit_bytes=VMEM_LIMIT),
        cost_estimate=cost(7),
        name="qkv",
    )(where, small, *xhats, *pieces)


def ln1_back_kernel(gp_ref, wq_ref, x0_ref, x1_ref, p0_ref, p1_ref, vec_ref):
    step = pl.program_id(0)
    grad = dot(gp_ref[...], wq_ref[...], NT)

    @pl.when(step == 0)
    def _():
        vec_ref[0:1] = jnp.sum(grad * x0_ref[...], axis=0, keepdims=True)
        vec_ref[1:2] = jnp.sum(grad, axis=0, keepdims=True)
        p0_ref[...] = grad.astype(p0_ref.dtype)

    @pl.when(step == 1)
    def _():
        vec_ref[0:1] += jnp.sum(grad * x1_ref[...], axis=0, keepdims=True)
        vec_ref[1:2] += jnp.sum(grad, axis=0, keepdims=True)
        p1_ref[...] = grad.astype(p1_ref.dtype)


def ln1_back(grad_packed, wqkv, xhats, first):
    slot, model = xhats[0].shape
    width = wqkv.shape[1]
    whole = lambda shape: pl.BlockSpec(shape, lambda i: (0, 0))
    return pl.pallas_call(
        ln1_back_kernel,
        grid=(2,),
        in_specs=[
            pl.BlockSpec((slot, width), lambda i: (first + i, 0)),
            whole((model, width)),
            whole((slot, model)),
            whole((slot, model)),
        ],
        out_specs=[whole((slot, model)), whole((slot, model)), whole((2, model))],
        out_shape=[
            jax.ShapeDtypeStruct((slot, model), bf16 if first else f32),
            jax.ShapeDtypeStruct((slot, model), bf16),
            jax.ShapeDtypeStruct((2, model), f32),
        ],
        compiler_params=pltpu.CompilerParams(vmem_limit_bytes=VMEM_LIMIT),
        cost_estimate=cost(5, 0.1 if first else 1.0),
        name="ln1_back",
    )(grad_packed, wqkv, *xhats)


def attn_fwd_kernel(len_ref, qkv_ref, tiles_ref, att_ref, p_ref):
    slot = qkv_ref.shape[0]
    blocks = range(slot // TILE)
    heads = range(2)
    length = len_ref[0]
    lane = lax.broadcasted_iota(jnp.int32, (1, PAIR), 1)
    col = lax.broadcasted_iota(jnp.int32, (1, slot), 1)
    hidden = jnp.where(col < length, 0.0, neg_large)
    q = qkv_ref[:, :PAIR] * HEAD_DIM ** (-0.5)
    k = qkv_ref[:, PAIR : 2 * PAIR]
    v = qkv_ref[:, 2 * PAIR :]
    own = [(lane // HEAD_DIM) == hh for hh in heads]
    qm = [jnp.where(own[hh], q, jnp.zeros_like(q)) for hh in heads]
    span = [(i + 1) * TILE for i in blocks]
    items = [(hh, i) for hh in heads for i in blocks]
    s = [dot(qm[hh][i * TILE : span[i]], k[: span[i]], NT) for hh, i in items]
    s = [
        x + jnp.concatenate([tiles_ref[hh, i - j] for j in range(i + 1)], axis=1) + hidden[:, : span[i]]
        for x, (hh, i) in zip(s, items)
    ]
    top = [jnp.max(x, axis=1, keepdims=True) for x in s]
    e = [jnp.exp(x - m) for x, m in zip(s, top)]
    scale = [1.0 / jnp.sum(x, axis=1, keepdims=True) for x in e]
    probs = [(x * r).astype(bf16) for x, r in zip(e, scale)]
    for x, (hh, i) in zip(probs, items):
        p_ref[hh, i * TILE : span[i], : span[i]] = x
    o = {item: dot(x, v[: span[item[1]]]) for x, item in zip(probs, items)}
    for i in blocks:
        att_ref[i * TILE : span[i], :] = jnp.where(own[0], o[0, i], o[1, i]).astype(bf16)


def attn_fwd(lengths, packed, tiles, seq):
    heads, count = tiles.shape[:2]
    slot = count * TILE
    return pl.pallas_call(
        attn_fwd_kernel,
        grid=(heads // 2,),
        in_specs=[
            pl.BlockSpec(memory_space=pltpu.SMEM),
            pl.BlockSpec((slot, 3 * PAIR), lambda p: (seq, p)),
            pl.BlockSpec((2, count, TILE, TILE), lambda p: (p, 0, 0, 0)),
        ],
        out_specs=[
            pl.BlockSpec((slot, PAIR), lambda p: (0, p)),
            pl.BlockSpec((2, slot, slot), lambda p: (p, 0, 0)),
        ],
        out_shape=[
            jax.ShapeDtypeStruct((slot, heads * HEAD_DIM), bf16),
            jax.ShapeDtypeStruct((heads, slot, slot), bf16),
        ],
        compiler_params=pltpu.CompilerParams(vmem_limit_bytes=VMEM_LIMIT),
        cost_estimate=cost(7.5),
        name="attn_fwd",
    )(lengths, packed, tiles)


def attn_bwd_kernel(qkv_ref, ga_ref, att_ref, p_ref, *refs):
    g_ref, sum_ref, ds_ref = refs[-3:]
    slot = qkv_ref.shape[0]
    blocks = range(slot // TILE)
    heads = range(2)
    lane = lax.broadcasted_iota(jnp.int32, (1, PAIR), 1)
    scale = HEAD_DIM ** (-0.5)
    q = qkv_ref[:, :PAIR] * scale
    k = qkv_ref[:, PAIR : 2 * PAIR]
    v = qkv_ref[:, 2 * PAIR :]
    ga = ga_ref[...]
    prod = ga.astype(f32) * att_ref[...].astype(f32)
    own = [(lane // HEAD_DIM) == hh for hh in heads]
    gam = [jnp.where(own[hh], ga, jnp.zeros_like(ga)) for hh in heads]
    inner = [jnp.sum(jnp.where(own[hh], prod, 0.0), axis=1, keepdims=True) for hh in heads]
    span = [(i + 1) * TILE for i in blocks]
    rows = [slice(i * TILE, span[i]) for i in blocks]
    items = [(hh, i) for hh in heads for i in blocks]
    dp = [dot(gam[hh][rows[i]], v[: span[i]], NT) for hh, i in items]
    ds = {
        (hh, i): (p_ref[hh, rows[i], : span[i]].astype(f32) * (x - inner[hh][rows[i]])).astype(bf16)
        for x, (hh, i) in zip(dp, items)
    }
    for hh, i in items:
        ds_ref[hh, rows[i], : span[i]] = ds[hh, i]
    dq = {(hh, i): dot(ds[hh, i], k[: span[i]]) for hh, i in items}
    dv = {(hh, j): dot(p_ref[hh, j * TILE :, rows[j]], ga[j * TILE :], TN) for hh, j in items}
    dk = {(hh, j): dot(ds_ref[hh, j * TILE :, rows[j]], q[j * TILE :], TN) for hh, j in items}
    for i in blocks:
        for at, got, factor in ((0, dq, scale), (PAIR, dk, 1.0), (2 * PAIR, dv, 1.0)):
            both = jnp.where(own[0], got[0, i], got[1, i]) * factor
            g_ref[rows[i], at : at + PAIR] = both.astype(bf16)
    row = lax.broadcasted_iota(jnp.int32, (TILE, TILE), 0)
    col = lax.broadcasted_iota(jnp.int32, (TILE, TILE), 1)
    flip = jnp.where(row + col == TILE - 1, 1.0, 0.0).astype(bf16)
    diag = {}
    for hh in heads:
        for delta in blocks:
            parts = [
                ds[hh, i][:, (i - delta) * TILE : (i - delta + 1) * TILE].astype(f32)
                for i in blocks
                if i >= delta
            ]
            diag[hh, delta] = functools.reduce(jnp.add, parts)
    high = {key: x.astype(bf16) for key, x in diag.items()}
    low = {key: (x - high[key].astype(f32)).astype(bf16) for key, x in diag.items()}
    turned = {key: dot(flip, high[key]) + dot(flip, low[key]) for key in diag}
    sums = {}
    for key, x in turned.items():
        wide = jnp.concatenate([x, jnp.zeros_like(x)], axis=1)
        wide = pltpu.roll(wide, 0, 1, stride=1, stride_axis=0)
        sums[key] = jnp.sum(wide, axis=0, keepdims=True)
    for hh in heads:
        for delta in blocks:
            here = sums[hh, delta][:, :TILE]
            if delta + 1 in blocks:
                here = here + sums[hh, delta + 1][:, TILE:]
            sum_ref[0, hh : hh + 1, rows[delta]] = here


def attn_bwd(packed, ga, att, probs, seq, into):
    heads, slot = probs.shape[:2]
    steps = heads // 2
    return pl.pallas_call(
        attn_bwd_kernel,
        grid=(steps,),
        in_specs=[
            pl.BlockSpec((slot, 3 * PAIR), lambda p: (seq, p)),
            pl.BlockSpec((slot, PAIR), lambda p: (0, p)),
            pl.BlockSpec((slot, PAIR), lambda p: (0, p)),
            pl.BlockSpec((2, slot, slot), lambda p: (p, 0, 0)),
        ]
        + ([] if into is None else [pl.BlockSpec(memory_space=pl.ANY)]),
        out_specs=[
            pl.BlockSpec((slot, 3 * PAIR), lambda p: (seq, p)),
            pl.BlockSpec((1, 2, slot), lambda p: (p, 0, 0)),
        ],
        out_shape=[
            jax.ShapeDtypeStruct(packed.shape, bf16),
            jax.ShapeDtypeStruct((steps, 2, slot), f32),
        ],
        scratch_shapes=[pltpu.VMEM((2, slot, slot), bf16)],
        input_output_aliases={} if into is None else {4: 0},
        compiler_params=pltpu.CompilerParams(vmem_limit_bytes=VMEM_LIMIT),
        cost_estimate=cost(5, 0.2),
        name="attn_bwd",
    )(packed, ga, att, probs, *(() if into is None else (into,)))


def ln1_last_kernel(tok_ref, xhat_ref, gmid_ref, small_ref, p0_ref, p1_ref, p2_ref, p3_ref, out_ref):
    _, factor = normalized(tok_ref[...].astype(f32))
    xhat = xhat_ref[...]
    low = pl.program_id(0) == 0
    e = p0_ref[...] + p1_ref[...].astype(f32) + jnp.where(low, p2_ref[...], p3_ref[...]).astype(f32)
    e = e * small_ref[0:1]
    out_ref[...] = gmid_ref[...] + factor * (
        e - jnp.mean(e, axis=-1, keepdims=True) - xhat * jnp.mean(e * xhat, axis=-1, keepdims=True)
    )


def ln1_last(tokens, xhat, grad_middle, small, p0, p1, p2, p3):
    slot, model = tokens.shape
    row = pl.BlockSpec((slot // 2, model), lambda i: (i, 0))
    part = pl.BlockSpec((slot // 2, model), lambda i: (0, 0))
    return pl.pallas_call(
        ln1_last_kernel,
        grid=(2,),
        in_specs=[row] * 3 + [block_of(small), row, row, part, part],
        out_specs=row,
        out_shape=jax.ShapeDtypeStruct((slot, model), f32),
        compiler_params=pltpu.CompilerParams(vmem_limit_bytes=VMEM_LIMIT),
        cost_estimate=cost(5, 0.05),
        name="ln1_last",
    )(tokens, xhat, grad_middle, small, p0, p1, p2, p3)


def quarters(n, r, size):
    return pl.ds(pl.multiple_of(lax.bitwise_xor(n, r) * size, size), size)


def out_ln2_kernel(part, n_ref, len_ref, tok_ref, small_ref, *refs):
    atts, wouts = refs[:4], refs[4:8]
    mid_ref, all_ref, norm_ref = refs[-3:]
    n = n_ref[0]
    rows, model = tok_ref.shape
    size = model // 4
    for r in range(4):
        all_ref[:, quarters(n, r, size)] = atts[r][...]
    valid = part * rows + lax.broadcasted_iota(jnp.int32, (rows, 1), 0) < len_ref[0]
    for r in range(4):
        cols = quarters(n, r, size)
        out = dot(all_ref[...], wouts[r][...])
        mid_ref[:, cols] = tok_ref[:, cols].astype(f32) + jnp.where(valid, out, 0.0)
    xhat, _ = normalized(mid_ref[...])
    norm_ref[...] = (xhat * small_ref[2:3] + small_ref[3:4]).astype(bf16)


def out_ln2(n, length, tokens, small, atts, wouts, part, into):
    slot, model = tokens.shape
    smem = pl.BlockSpec(memory_space=pltpu.SMEM)
    whole = lambda x: pl.BlockSpec(x.shape, lambda i: (0, 0))
    rows = lambda cols: pl.BlockSpec((slot // 2, cols), lambda i: (part, 0))
    return pl.pallas_call(
        functools.partial(out_ln2_kernel, part),
        grid=(1,),
        in_specs=[smem, smem, rows(model), whole(small)]
        + [rows(model // 4)] * 4
        + [whole(w) for w in wouts]
        + [pl.BlockSpec(memory_space=pl.ANY)] * len(into),
        out_specs=[rows(model), rows(model), pl.BlockSpec((slot // 2, model), lambda i: (0, 0))],
        out_shape=[
            jax.ShapeDtypeStruct((slot, model), f32),
            jax.ShapeDtypeStruct((slot, model), bf16),
            jax.ShapeDtypeStruct((slot // 2, model), bf16),
        ],
        input_output_aliases={12 + i: i for i in range(len(into))},
        compiler_params=pltpu.CompilerParams(vmem_limit_bytes=VMEM_LIMIT),
        cost_estimate=cost(4, 1 / 64),
        name="out_ln2",
    )(n, length, tokens, small, *atts, *wouts, *into)


def ln2_back_kernel(part, n_ref, len_ref, mid_ref, cot_ref, small_ref, p0_ref, p2_ref, *refs):
    near, wouts = refs[:2], refs[2:6]
    gmid_ref, keep_ref, send_ref = refs[-9:-6]
    gatts = refs[-6:-2]
    vec_ref, branch_ref = refs[-2:]
    n = n_ref[0]
    rows, model = mid_ref.shape
    size = model // 4
    xhat, factor = normalized(mid_ref[...])
    grad = p0_ref[...] + p2_ref[...].astype(f32)
    grad = grad + jnp.concatenate([x[...] for x in near], axis=0).astype(f32)
    vec_ref[0:1] = jnp.sum(grad * xhat, axis=0, keepdims=True)
    vec_ref[1:2] = jnp.sum(grad, axis=0, keepdims=True)
    e = grad * small_ref[2:3]
    back = factor * (
        e - jnp.mean(e, axis=-1, keepdims=True) - xhat * jnp.mean(e * xhat, axis=-1, keepdims=True)
    )
    gmid = cot_ref[...].astype(f32) + back
    gmid_ref[...] = gmid
    valid = part * rows + lax.broadcasted_iota(jnp.int32, (rows, 1), 0) < len_ref[0]
    branch_ref[...] = jnp.where(valid, gmid, 0.0).astype(bf16)
    cuts = [branch_ref[:, quarters(n, r, size)] for r in range(4)]
    keep_ref[:, :size] = cuts[0]
    keep_ref[:, size:] = cuts[2]
    send_ref[:, :size] = cuts[1]
    send_ref[:, size:] = cuts[3]
    for r in range(4):
        feats = quarters(n, r, size)
        total = dot(cuts[0], wouts[0][feats, :], NT)
        for k in range(1, 4):
            total = total + dot(cuts[k], wouts[k][feats, :], NT)
        gatts[r][...] = total.astype(bf16)


def ln2_back(n, length, middle, cot, small, p0, near, p2, wouts, part, into):
    slot, model = middle.shape
    smem = pl.BlockSpec(memory_space=pltpu.SMEM)
    whole = lambda x: pl.BlockSpec(x.shape, lambda i: (0, 0))
    rows = lambda cols: pl.BlockSpec((slot // 2, cols), lambda i: (part, 0))
    return pl.pallas_call(
        functools.partial(ln2_back_kernel, part),
        grid=(1,),
        in_specs=[smem, smem, rows(model), rows(model), whole(small), rows(model), whole(p2)]
        + [whole(w) for w in (*near, *wouts)]
        + [pl.BlockSpec(memory_space=pl.ANY)] * len(into),
        out_specs=[rows(model), rows(model // 2), rows(model // 2)]
        + [rows(model // 4)] * 4
        + [pl.BlockSpec((2, model), lambda i: (0, 0))],
        out_shape=[
            jax.ShapeDtypeStruct((slot, model), f32),
            jax.ShapeDtypeStruct((slot, model // 2), bf16),
            jax.ShapeDtypeStruct((slot, model // 2), bf16),
        ]
        + [jax.ShapeDtypeStruct((slot, model // 4), bf16)] * 4
        + [jax.ShapeDtypeStruct((2, model), f32)],
        scratch_shapes=[pltpu.VMEM((slot // 2, model), bf16)],
        input_output_aliases={13 + i: i for i in range(len(into))},
        compiler_params=pltpu.CompilerParams(vmem_limit_bytes=VMEM_LIMIT),
        cost_estimate=cost(5),
        name="ln2_back",
    )(n, length, middle, cot, small, p0, p2, *near, *wouts, *into)


def gelu_both(u):
    c0 = 0.7978845608028654
    c1 = 0.044715
    sq = u * u
    t = jnp.tanh(u * (c0 + (c0 * c1) * sq))
    half = 0.5 + 0.5 * t
    slope = half + (1.0 - t * t) * (u * (0.5 * c0 + (1.5 * c0 * c1) * sq))
    return u * half, slope


def ffn_kernel(count, places, start, cuts, w_any, *refs):
    norms, grads = refs[:count], refs[count : count + len(places)]
    n4_any, g4_any, hid4_any, gua4_any = refs[-13:-9]
    sums = refs[-16 - cuts : -13]
    o0_ref, gn0_ref = sums[:2]
    n_ref, g_ref, wu_ref, wd_ref, hid_ref, gua_ref, sems, w_sems, out_sems = refs[-9:]
    step = pl.program_id(0)
    steps = pl.num_programs(0) // 2
    rows = n_ref.shape[0]
    block = o0_ref.shape[1]
    mine = pl.ds(start, rows)
    outs = [
        pltpu.make_async_copy(src, dst.at[mine], out_sems.at[i])
        for i, (src, dst) in enumerate(
            ((n_ref, n4_any), (g_ref, g4_any), (hid_ref, hid4_any), (gua_ref, gua4_any))
        )
    ]
    shards, _, size, _ = w_any.shape
    weights = [
        [
            pltpu.make_async_copy(
                w_any.at[d, i], whole.at[pl.ds(d * size, size)], w_sems.at[d, i]
            )
            for d in range(shards)
        ]
        for i, whole in enumerate((wu_ref, wd_ref))
    ]
    acts = []
    grads = [g.at[pl.ds(first, size)] for g, (first, size) in zip(grads, places)]
    for j, (pieces, whole) in enumerate(((norms, n_ref), (grads, g_ref))):
        acts.append([])
        at = 0
        for i, piece in enumerate(pieces):
            here = piece.shape[0]
            acts[j].append(
                pltpu.make_async_copy(piece, whole.at[pl.ds(at, here)], sems.at[j, i])
            )
            at += here

    @pl.when(step == 0)
    def _():
        for copy in acts[0] + weights[0] + acts[1] + weights[1]:
            copy.start()
        for copy in acts[0] + weights[0]:
            copy.wait()

    @pl.when(step < steps)
    def _():
        cols = pl.ds(pl.multiple_of(step * block, block), block)
        u = dot(n_ref[...], wu_ref[:, cols])
        hid, slope = gelu_both(u)

        @pl.when(step == 0)
        def _():
            for copy in acts[1] + weights[1]:
                copy.wait()

        gh = dot(g_ref[...], wd_ref[cols, :], NT)
        hid_ref[:, cols] = hid.astype(bf16)
        gua_ref[:, cols] = (slope * gh).astype(bf16)

    @pl.when(step == steps)
    def _():
        for copy in outs:
            copy.start()

    @pl.when(step >= steps)
    def _():
        cols = pl.ds(pl.multiple_of((step - steps) * block, block), block)
        half = rows // 2
        gn = dot(gua_ref[...], wu_ref[cols, :], NT)
        o = dot(hid_ref[...], wd_ref[:, cols])
        for first, pieces, total in ((o0_ref, sums[2:3], o), (gn0_ref, sums[3:], gn)):
            first[...] = total[:half]
            size = half // len(pieces)
            for i, piece in enumerate(pieces):
                piece[...] = total[half + i * size : half + (i + 1) * size].astype(bf16)

    @pl.when(step == 2 * steps - 1)
    def _():
        for copy in outs:
            copy.wait()


def ffn(norms, grads, places, weights, start, into, cuts):
    width = norms[0].shape[1]
    rows = sum(x.shape[0] for x in norms)
    total = into[0].shape[0] if into else 2 * rows
    units = weights.shape[0] * weights.shape[2]
    block = min(512, units)
    steps = units // block
    half = rows // 2
    anywhere = pl.BlockSpec(memory_space=pl.ANY)
    late = lambda size: pl.BlockSpec((size, block), lambda i: (0, jnp.maximum(i - steps, 0)))
    acts = pltpu.VMEM((rows, width), bf16)
    hidden = pltpu.VMEM((rows, units), bf16)
    ins = 1 + len(norms) + len(grads)
    outs = 3 + cuts
    got = pl.pallas_call(
        functools.partial(ffn_kernel, len(norms), places, start, cuts),
        grid=(2 * steps,),
        in_specs=[anywhere] * (ins + len(into)),
        out_specs=[late(half)] * 2 + [late(half)] + [late(half // cuts)] * cuts + [anywhere] * 4,
        out_shape=[jax.ShapeDtypeStruct((half, width), f32)] * 2
        + [jax.ShapeDtypeStruct((half, width), bf16)]
        + [jax.ShapeDtypeStruct((half // cuts, width), bf16)] * cuts
        + [jax.ShapeDtypeStruct((total, width), bf16)] * 2
        + [jax.ShapeDtypeStruct((total, units), bf16)] * 2,
        scratch_shapes=[
            acts,
            acts,
            pltpu.VMEM((width, units), bf16),
            pltpu.VMEM((units, width), bf16),
            hidden,
            hidden,
            pltpu.SemaphoreType.DMA((2, max(len(norms), len(grads)))),
            pltpu.SemaphoreType.DMA((weights.shape[0], 2)),
            pltpu.SemaphoreType.DMA((4,)),
        ],
        input_output_aliases={ins + i: outs + i for i in range(len(into))},
        compiler_params=pltpu.CompilerParams(vmem_limit_bytes=VMEM_LIMIT),
        cost_estimate=cost(8 if into else 12, 1 / 64),
        name="ffn",
    )(weights, *norms, *grads, *into)
    return got[0], got[2], got[1], got[3:outs], got[outs:]


def pack_small_kernel(heads, n_ref, y_ref, one_ref, also_ref, two_ref, more_ref, buckets_ref, *refs):
    dists, (keep_ref, send_ref) = refs[:-2], refs[-2:]
    n = n_ref[0]
    odd = y_ref[0] == 1
    slot = buckets_ref.shape[1]
    total = dists[0][...]
    for ref in dists[1:]:
        total = total + ref[...]
    lanes = heads * BUCKETS
    bucket = lax.broadcasted_iota(jnp.int32, (lanes, slot), 0) % BUCKETS
    onehot = (buckets_ref[...] == bucket).astype(f32).astype(bf16)
    lane = lax.broadcasted_iota(jnp.int32, (1, lanes), 1)
    table = jnp.zeros((1, lanes), f32)
    for h in range(heads):
        row = jnp.broadcast_to(total[h // 2, h % 2 : h % 2 + 1], (8, slot))
        parts = []
        for _ in range(3):
            low = row.astype(bf16)
            parts.append(dot(low, onehot, NT))
            row = row - low.astype(f32)
        got = (parts[0] + parts[1] + parts[2])[0:1]
        table = jnp.where(lane // BUCKETS == h, got, table)
    zeros = jnp.zeros((1, TILE), f32)
    half = lanes // 2
    low = jnp.where(lane < half, table, 0.0)
    high = jnp.where(lane < half, pltpu.roll(table, half, 1), 0.0)
    for z in range(keep_ref.shape[0]):
        both = []
        for b, share in ((0, low), (1, high)):
            d = 2 * z + b
            cols = slice(d * TILE, (d + 1) * TILE)
            rel = jnp.where(d == 2 * n + b, share, zeros)
            both.append(
                jnp.concatenate(
                    [
                        one_ref[:, cols] + also_ref[:, cols],
                        two_ref[:, cols] + more_ref[:, cols],
                        rel,
                        zeros,
                        zeros,
                        zeros,
                    ],
                    axis=0,
                )
            )
        keep_ref[z] = jnp.where(odd, both[1], both[0])
        send_ref[z] = jnp.where(odd, both[0], both[1])


def pack_small(n, y, grad_one, grad_two, buckets, dists, heads):
    slot = buckets.shape[0]
    model = grad_one[0].shape[1]
    smem = pl.BlockSpec(memory_space=pltpu.SMEM)
    operands = [*grad_one, *grad_two, buckets.reshape(1, slot), *dists]
    shape = jax.ShapeDtypeStruct((model // TILE // 2, 8, TILE), f32)
    return pl.pallas_call(
        functools.partial(pack_small_kernel, heads),
        grid=(1,),
        in_specs=[smem, smem] + [block_of(x) for x in operands],
        out_specs=[pl.BlockSpec(shape.shape, lambda i: (0, 0, 0))] * 2,
        out_shape=[shape, shape],
        cost_estimate=cost(3),
        name="pack_small",
    )(n, y, *operands)


def join_ffn_kernel(quarter, n_ref, *refs):
    ins, (up_ref, down_ref) = refs[:4], refs[4:]
    model = down_ref.shape[1]
    rows = up_ref.shape[0]
    for r in range(4):
        j = lax.bitwise_xor(n_ref[0], r)
        for d in range(model // quarter):
            start = pl.multiple_of((d * 4 + j) * quarter, quarter)
            up_ref[:, pl.ds(start, quarter)] = ins[r][:, d * quarter : (d + 1) * quarter].astype(f32)
        down_ref[pl.ds(pl.multiple_of(j * quarter, quarter), quarter), :] = ins[r][:, model:].astype(f32)


def join_ffn(n, parts, quarter):
    rows, both = parts[0].shape
    model = both // 2
    shapes = [(rows, 4 * model), (4 * quarter, model)]
    if quarter % TILE:
        wide = model // quarter
        rel = jnp.stack(parts)
        rel = jnp.stack(
            [lax.dynamic_index_in_dim(rel, n[0] ^ j, 0, keepdims=False) for j in range(4)]
        ).astype(f32)
        up = rel[:, :, :model].reshape(4, rows, wide, quarter).transpose(1, 2, 0, 3)
        return up.reshape(shapes[0]), rel[:, :, model:].reshape(shapes[1])
    return pl.pallas_call(
        functools.partial(join_ffn_kernel, quarter),
        grid=(1,),
        in_specs=[pl.BlockSpec(memory_space=pltpu.SMEM)] + [block_of(x) for x in parts],
        out_specs=[pl.BlockSpec(x, lambda i: (0, 0)) for x in shapes],
        out_shape=[jax.ShapeDtypeStruct(x, f32) for x in shapes],
        compiler_params=pltpu.CompilerParams(vmem_limit_bytes=VMEM_LIMIT),
        cost_estimate=cost(4, 0.05),
        name="join_ffn",
    )(n, *parts)


def join_attn_kernel(n_ref, *refs):
    ins, (qkv_ref, out_ref) = refs[:4], refs[4:]
    model = out_ref.shape[1]
    mine = model // 4
    for r in range(4):
        j = lax.bitwise_xor(n_ref[0], r)
        at = 0
        for p in range(mine // PAIR):
            for part in range(3):
                start = pl.multiple_of(part * model + j * mine + p * PAIR, PAIR)
                qkv_ref[:, pl.ds(start, PAIR)] = ins[r][:, at : at + PAIR].astype(f32)
                at += PAIR
        out_ref[:, pl.ds(pl.multiple_of(j * mine, mine), mine)] = ins[r][
            :, at : at + mine
        ].astype(f32) + ins[r ^ 2][:, at + mine :].astype(f32)


def join_attn(n, parts, model):
    rows = parts[0].shape[0]
    shapes = [(rows, 3 * model), (rows, model)]
    return pl.pallas_call(
        join_attn_kernel,
        grid=(1,),
        in_specs=[pl.BlockSpec(memory_space=pltpu.SMEM)] + [block_of(x) for x in parts],
        out_specs=[pl.BlockSpec(x, lambda i: (0, 0)) for x in shapes],
        out_shape=[jax.ShapeDtypeStruct(x, f32) for x in shapes],
        cost_estimate=cost(3),
        name="join_attn",
    )(n, *parts)


def ring_order(size):
    return list(range(0, size, 2)) + list(range(size - 1, 0, -2))


def ring_member(pos, size):
    pos = lax.rem(pos + 2 * size, size)
    return jnp.where(pos < size // 2, 2 * pos, 2 * (size - 1 - pos) + 1)


def ring_pairs(narrow, size):
    order = ring_order(size)
    pairs = []
    for n in range(narrow):
        turn = 1 if n % 2 == 0 else -1
        for p in range(size):
            pairs.append((n * size + order[p], n * size + order[(p + turn) % size]))
    return pairs


class Places:
    def __init__(self):
        self.narrow = lax.axis_size("narrow")
        self.wide = lax.axis_size("wide")
        self.n = lax.axis_index("narrow")
        self.w = lax.axis_index("wide")
        self.core = lax.rem(self.n, 2)
        self.turn = 1 - 2 * self.core
        self.y = lax.rem(self.w, 2)
        self.z = self.w // 2
        self.pos = jnp.where(self.y == 0, self.z, self.wide - 1 - self.z)
        self.pairs = ring_pairs(self.narrow, self.wide)
        self.rings = self.wide <= 16

    def ring(self, x, way):
        pairs = self.pairs if way == 0 else [(b, a) for a, b in self.pairs]
        return lax.ppermute(x, ("narrow", "wide"), pairs)

    def member(self, steps):
        return ring_member(self.pos + self.turn * steps, self.wide)

    def swap(self, x, bit):
        return lax.ppermute(x, "narrow", [(i, i ^ bit) for i in range(self.narrow)])

    def all_narrow(self, x):
        far = self.swap(x, 2)
        return [x, self.swap(x, 1), far, self.swap(far, 1)]

    def swap_y(self, x):
        return lax.ppermute(x, "wide", [(i, i ^ 1) for i in range(self.wide)])

    def along_z(self, x, steps):
        return lax.ppermute(
            x, "wide", [(i, (i + 2 * steps) % self.wide) for i in range(self.wide)]
        )


def row_major(x):
    return with_layout_constraint(x, Layout(major_to_minor=tuple(range(x.ndim))))


def after(x, *deps):
    return lax.optimization_barrier((x, *deps))[0]


def add_low(*terms):
    return sum(t.astype(f32) for t in terms).astype(bf16)


def gather_ring(at, piece, holds):
    pieces, steps = [piece], [0]
    ahead = behind = piece
    far = at.wide // 2
    for k in range(1, far + 1):
        ahead = at.ring(ahead, 0)
        came = [ahead]
        if k < far:
            behind = at.ring(behind, 1)
            came.append(behind)
        held = holds[k](*came) if k in holds else ()
        came = lax.optimization_barrier((*came, *held))
        ahead = came[0]
        if k < far:
            behind = came[1]
            pieces.append(behind)
            steps.append(k)
        pieces.append(ahead)
        steps.append(-k)
    return pieces, steps


def reduce_ring(at, parts):
    size = at.wide

    def chunk(k):
        member = at.member(k)
        cut = [lax.dynamic_index_in_dim(p, member, 0, keepdims=False) for p in parts]
        return row_major(jnp.concatenate(cut, axis=1) if len(cut) > 1 else cut[0])

    far = size // 2
    ahead, behind = chunk(far), chunk(1 - far)
    yield ahead, behind
    for k in range(far - 1, 0, -1):
        ahead, behind = at.ring(ahead, 0), at.ring(behind, 1)
        held = yield ahead, behind
        ahead, behind, *_ = lax.optimization_barrier((ahead, behind, *(held or ())))
        ahead = row_major(add_low(ahead, chunk(k)))
        if k > 1:
            behind = row_major(add_low(behind, chunk(1 - k)))
        yield ahead, behind
    ahead = at.ring(ahead, 0)
    held = yield (ahead,)
    ahead, *_ = lax.optimization_barrier((ahead, *(held or ())))
    yield row_major(add_low(chunk(0), ahead, behind))


def scatter(at, parts):
    return jnp.concatenate(
        [lax.psum_scatter(p, "wide", scatter_dimension=0, tiled=True)[0] for p in parts], axis=1
    )


def local(
    tokens,
    lengths,
    buckets,
    ln1_gain,
    ln1_bias,
    w_qkv,
    rel_table,
    w_out,
    ln2_gain,
    ln2_bias,
    w_up,
    w_down,
    cotangent,
):
    at = Places()
    wide = at.wide
    slot, model = tokens.shape
    backwards = buckets.reshape(-1, TILE)[:, ::-1].reshape(slot)
    rows = w_qkv.shape[0]
    ff = w_up.shape[1]
    ff_rows = w_down.shape[0]
    quarter = ff_rows // 4
    heads = HEADS // 4
    width = 3 * model // 4
    rel_rows = rel_table.shape[0]
    n = at.n.reshape(1)
    far = wide // 2

    cut = slot // 16 * 7
    tokens_far = [at.swap(tokens[:cut], 2), at.swap(tokens[cut:], 2)]
    tokens_all = [[tokens], [at.swap(tokens, 1)], tokens_far, [at.swap(t, 1) for t in tokens_far]]

    lengths_far = at.swap(after(lengths, tokens_far[0]), 2)
    lengths_all = [lengths, at.swap(lengths, 1), lengths_far, at.swap(lengths_far, 1)]

    vectors = [ln1_gain, ln1_bias, ln2_gain, ln2_bias, rel_table]
    vectors = jnp.stack([jnp.pad(s, (0, TILE - s.shape[0])) for s in vectors])
    vectors = jnp.pad(vectors, ((0, 16 - vectors.shape[0]), (0, 0)))
    if at.rings:
        attn_piece = cut_attn(n, w_qkv, w_out, vectors)
        ffn_piece = cut_ffn(n, after(w_up, attn_piece), w_down)
        came, xhats = [], []

        def hold(x, *deps):
            xhats.append(xhat_of([after(t, *deps) for t in x]))
            return xhats[-1]

        pieces, steps = gather_ring(
            at,
            attn_piece,
            {
                1: lambda *x: [ffn_piece, tokens_far[0]],
                2: lambda *x: [
                    lengths_far,
                    tokens_far[1],
                    hold(tokens_all[0], *x),
                    hold(tokens_all[1], *x),
                ],
                3: lambda *x: came.extend(x) or lengths_all[1::2],
            },
        )
        hold(tokens_all[2], *came)
        hold(tokens_all[3], *came)
        ffn_piece = after(ffn_piece, *came)
        where = jnp.stack([at.member(k) for k in steps])
        small = small_rows(where, pieces, model)
    else:
        pick = lambda x, axis: lax.dynamic_index_in_dim(x, at.n, axis, keepdims=False)
        cut = pick(w_qkv.reshape(rows, 3, 4, heads // 2, PAIR), 2)
        cut = cut.transpose(0, 2, 1, 3).reshape(rows, width)
        cut = [cut, pick(w_out.reshape(rows, 4, model // 4), 1), jnp.zeros((rows, TILE), bf16)]
        attn_piece = jnp.concatenate(cut, axis=1)
        ffn_piece = jnp.stack(
            [
                pick(w_up.reshape(rows, wide, 4, quarter), 2).reshape(rows, wide * quarter),
                pick(w_down.reshape(4, quarter, model), 0),
            ]
        )
        pieces = [lax.all_gather(attn_piece, "wide", axis=0, tiled=True)]
        where = jnp.zeros((1,), jnp.int32)
        small = lax.all_gather(vectors, "wide", axis=0).astype(f32)
        small = [small[:, i, :rows].reshape(1, model) for i in range(4)] + [
            jnp.pad(small[:, 4, :rel_rows].reshape(1, -1), ((0, 0), (0, model - HEADS * BUCKETS)))
        ]
        small = jnp.pad(jnp.concatenate(small, axis=0), ((0, 3), (0, 0)))
    w_ffn = lax.all_gather(ffn_piece, "wide", axis=0)

    if not at.rings:
        xhats = [xhat_of(t) for t in tokens_all]
    valid = (jnp.arange(slot, dtype=jnp.int32) < lengths[0]).astype(f32)[:, None]
    cotan = cotangent.astype(f32)
    grad_ffn = at.all_narrow(after((valid * cotan).astype(bf16), xhats[2]))
    half = slot // 2
    norm_one, packed, wqkv, wout = qkv_of(where, small, xhats, pieces, width)
    wouts = at.all_narrow(wout)
    tiles = bias_tiles(n, small, buckets, heads)
    atts, probs = [None] * 4, [None] * 4
    for r in (3, 2, 1, 0):
        length = after(lengths_all[r], *grad_ffn[1:]) if r == 0 else lengths_all[r]
        atts[r], probs[r] = attn_fwd(length, packed, tiles, r)
    attended = [atts[0]] + [at.swap(atts[r], r) for r in (1, 2, 3)]
    whole, norm_two, norm_far = [], [], []
    for i in range(2):
        *whole, norm = out_ln2(n, lengths, tokens, small, attended, wouts, i, whole)
        norm_two.append(norm)
        norm_far.append(at.swap(norm, 2))
    middle, attended = whole

    norm_near = norm_two + [at.swap(x, 1) for x in norm_two]
    o0, o1, gn0, gn1, rows_all = ffn(
        norm_near, grad_ffn[:2], [(0, slot)] * 2, w_ffn, 0, [], 4
    )
    gn_near = [at.swap(x, 1) for x in gn1]

    def chip_sum(p2, p3):
        return add_low(p2, jnp.concatenate([at.swap(x, 1) for x in p3], axis=0))

    cuts = 4
    gn_far, o_far, gn_back = [], [], []
    for i in range(2):
        norms = after(norm_far[i], gn2 if i else gn0)
        cut = half // cuts
        norms = [norms] + [at.swap(norms[j : j + cut], 1) for j in range(0, half, cut)]
        norms[0] = after(norms[0], *gn_far)
        o2, o3, gn2, gn3, rows_all = ffn(
            norms, grad_ffn[2:], [(i * half, half)] * 2, w_ffn, 2 * slot + i * slot, rows_all, cuts
        )
        gn_far.append(chip_sum(gn2, gn3))
        o_far.append((o2, o3))
        gn_back.append(at.swap(gn_far[i], 2))
    norms, grads, hid, gua = rows_all
    gu = dot(norms, after(gua, gn_back[0], *gn_far), TN).astype(bf16)
    gd = dot(hid, after(grads, gn_back[0], *gn_far), TN).astype(bf16)
    shape = (wide, rows, model)
    if at.rings:
        turns = reduce_ring(at, [gu.reshape(shape), gd.reshape(shape)])
        next(turns)

    whole, grad_two = [], []
    for i in range(2):
        near = gn_near[2 * i : 2 * i + 2]
        *whole, vec = ln2_back(
            n, lengths, middle, cotangent, small, gn0, near, gn_back[i], wouts, i, whole
        )
        grad_two.append(vec)
    grad_middle, branch_keep, branch_send, *grad_att = whole
    if at.rings:
        next(turns)
        grad_att[0] = after(grad_att[0], *next(turns))
    grad_att = [grad_att[0]] + [at.swap(grad_att[r], r) for r in (1, 2, 3)]
    grad_packed, dists = None, []

    def backward(r, *deps):
        ga = after(grad_att[r], *deps) if deps else grad_att[r]
        return attn_bwd(packed, ga, atts[r], probs[r], r, grad_packed)

    def turned():
        return list(next(turns)) if at.rings else []

    def turn_after(*deps):
        if at.rings:
            turns.send(list(deps))

    grad_packed, dist = backward(0)
    dists.append(dist)
    attended = after(attended, dist, *grad_att[2:])
    out_send = dot(attended, branch_send, TN).astype(bf16)
    out_keep = dot(attended, branch_keep, TN).astype(bf16)
    o_far = [chip_sum(after(x, dist), [after(y, dist)]) for x, y in o_far]
    out_back = [at.swap(o_far[0], 2)]
    grad_packed, dist = backward(2, out_send, out_keep, *turned())
    turn_after(grad_att[2])
    dists.append(dist)
    out_sum = add_low(out_keep, at.swap(out_send, 1))
    grad_packed, dist = backward(3, out_sum)
    dists.append(dist)
    p2, p3, more_one = ln1_back(after(grad_packed, out_back[0], *turned()), wqkv, xhats[2:], 2)
    turn_after(p3)
    p_far = chip_sum(p2, [p3])
    p_back = [at.swap(p_far[:half], 2)]
    grad_packed, dist = backward(1, p_far)
    dists.append(dist)
    grad_qkv = dot(norm_one, after(grad_packed, p_back[0]), TN).astype(bf16)
    parts = [grad_qkv.reshape(wide, rows, width), out_sum.reshape(wide, rows, model // 2)]
    if at.rings:
        next(turns)
        ffn_own = turns.send([dist])
        turns = reduce_ring(at, parts)
        grad_packed = after(grad_packed, *next(turns))
    else:
        ffn_own = scatter(at, [gu.reshape(shape), gd.reshape(shape)])
        attn_own = scatter(at, parts)
    ffn_all = at.all_narrow(after(ffn_own, p_back[0]))
    p_back.append(at.swap(after(p_far[half:], ffn_all[2]), 2))
    out_back.append(at.swap(after(o_far[1], p_back[1]), 2))

    p0, p1, grad_one = ln1_back(grad_packed, wqkv, xhats[:2], 0)
    grad_one = [grad_one, more_one]
    p_near = at.swap(p1, 1)
    up_full, down_full = join_ffn(n, ffn_all, quarter)
    if at.rings:
        keep, send = pack_small(n, at.y.reshape(1), grad_one, grad_two, backwards, dists, heads)
        next(turns)
        sent = turns.send([p1, keep, ffn_all[2]])
        smalls = keep + at.swap_y(after(send, *sent))
        next(turns)
        sent = turns.send([p_back[1], up_full])
        p0 = after(p0, *sent)
    grad_tokens = ln1_last(tokens, xhats[0], grad_middle, small, p0, p_near, *p_back)

    outs = [o0, at.swap(o1, 1), jnp.concatenate(out_back, axis=0)]
    if at.rings:
        next(turns)
        sent = turns.send([grad_tokens, out_back[1], smalls])
        smalls, outs[0] = after(smalls, *sent), after(o0, *sent)
        pick = lambda i: lax.dynamic_index_in_dim(smalls, i, 0, keepdims=False)
        z_parts = [pick(at.z)] + [
            at.along_z(pick(lax.rem(at.z + k, far)), k) for k in range(1, far)
        ]
    output = (middle + valid * sum(p.astype(f32) for p in outs)).astype(bf16)
    if at.rings:
        next(turns)
        attn_own = turns.send([output])
        smalls = after(z_parts[0], attn_own) + sum(z_parts[1:])

    if not at.rings:
        onehot = (backwards[:, None] == jnp.arange(BUCKETS, dtype=jnp.int32)[None, :]).astype(f32)
        table = jnp.dot(sum(dists).reshape(heads, slot), onehot, precision=lax.Precision.HIGHEST)
        table = lax.dynamic_update_slice(
            jnp.zeros((4, heads * BUCKETS), f32), table.reshape(1, -1), (at.n, 0)
        )
        two = grad_two[0] + grad_two[1]
        one = grad_one[0] + grad_one[1]
        smalls = [one[0], one[1], two[0], two[1], table]
        smalls = [g.reshape(wide, 1, -1) for g in smalls]
        smalls = [jnp.pad(g, ((0, 0), (0, 0), (0, TILE - g.shape[2]))) for g in smalls]
        smalls = jnp.concatenate(smalls + [jnp.zeros((wide, 3, TILE), f32)], axis=1)
        smalls = lax.psum_scatter(smalls, "wide", scatter_dimension=0, tiled=True)[0]
    smalls = smalls + at.swap(smalls, 2)
    smalls = smalls + at.swap(smalls, 1)

    qkv_full, out_full = join_attn(n, at.all_narrow(attn_own), model)

    return (
        output,
        grad_tokens,
        smalls[0, :rows],
        smalls[1, :rows],
        qkv_full,
        smalls[4, :rel_rows],
        out_full,
        smalls[2, :rows],
        smalls[3, :rows],
        up_full,
        down_full,
    )


def solution(mesh):
    return jax.shard_map(
        local,
        mesh=mesh,
        in_specs=(
            P(("narrow", "wide"), None),
            P(("narrow", "wide")),
            P(),
            P("wide"),
            P("wide"),
            P("wide", None),
            P("wide"),
            P("wide", None),
            P("wide"),
            P("wide"),
            P("wide", None),
            P("wide", None),
            P(("narrow", "wide"), None),
        ),
        out_specs=(
            P(("narrow", "wide"), None),
            P(("narrow", "wide"), None),
            P("wide"),
            P("wide"),
            P("wide", None),
            P("wide"),
            P("wide", None),
            P("wide"),
            P("wide"),
            P("wide", None),
            P("wide", None),
        ),
        check_vma=False,
    )
```

time: 2100 us -> 362 us (0.17)
  local copies, waits for them, and re-layouts: 1220 us -> 18.8 us
  waiting for transfers between devices: 496 us -> 69.9 us
  Pallas kernels: 0 us -> 154 us
  blocking collectives: 135 us -> 0 us
  matrix products: 153 us -> 22.5 us
  starting transfers between devices: 0.36 us -> 60 us
  other arithmetic: 58.3 us -> 15.5 us
    gather x2 -> x0, local copies, waits for them, and re-layouts: 934 us -> none  [block_scores(): scores = raw_scores * score_scale + jnp.take(by_distance, distance, axis=1)]
    reduce_scatter x4 -> x0, waiting for transfers between devices: 436 us -> none  [the longest x1 283 us: local(): lax.psum_scatter(grad_down, 'wide', scatter_dimension=0, tiled=True)]
    pallas_call x0 -> x30, Pallas kernels: none -> 154 us  [the longest x3 37.7 us: ffn(): pl.pallas_call(functools.partial(ffn_kernel, len(norms), places, start, c...]
    dot_general x20 -> x5, matrix products: 153 us -> 22.5 us  [dot(): return lax.dot_general(a, b, (dims, ((), ())), preferred_element_type=f32)]
    rev x1, local copies, waits for them, and re-layouts: 121 us -> 0.67 us  [local(): backwards = buckets.reshape(-1, TILE)[:, ::-1].reshape(slot)]
    all_gather x4 -> x0, blocking collectives: 73.5 us -> none  [the longest x1 22.3 us: local(): lax.all_gather(ln1_gain, 'wide', axis=0, tiled=True)]
    ppermute x0 -> x89, waiting for transfers between devices: none -> 69.9 us  [the longest x64 40.4 us: swap(): return lax.ppermute(x, 'narrow', [(i, i ^ bit) for i in range(self.narrow)])]
    ppermute x0 -> x89, starting transfers between devices: none -> 60 us  [the longest x64 31.7 us: swap(): return lax.ppermute(x, 'narrow', [(i, i ^ bit) for i in range(self.narrow)])]
  transfers between devices with their start and end apart: 9 -> 90, of which waited for: 3 -> 34; matrix products, arithmetic and copies ran while one was open for 67% -> 13% of each run, Pallas kernels for 0% -> 40%
where the time goes in v1:
time: 362 us; the launch traced here: 356 us
  Pallas kernels  154 us (43%)
  waiting for transfers between devices  69.9 us (19%)
  starting transfers between devices  60 us (17%)
  matrix products  22.5 us (6%)
  local copies, waits for them, and re-layouts  18.8 us (5%)
  between operations  15.8 us (4%)
  other arithmetic  15.5 us (4%)
    ppermute x64, waiting for transfers between devices, swap(): return lax.ppermute(x, 'narrow', [(i, i ^ bit) for i in range(self.narrow)])  40.4 us
    pallas_call x3, Pallas kernels, ffn(): pl.pallas_call(functools.partial(ffn_kernel, len(norms), places, start, c...  37.7 us
    ppermute x64, starting transfers between devices, swap(): return lax.ppermute(x, 'narrow', [(i, i ^ bit) for i in range(self.narrow)])  31.7 us
    ppermute x21, waiting for transfers between devices, ring(): return lax.ppermute(x, ('narrow', 'wide'), pairs)  27.9 us
    ppermute x21, starting transfers between devices, ring(): return lax.ppermute(x, ('narrow', 'wide'), pairs)  22.5 us
    dot_general x5, matrix products, dot(): return lax.dot_general(a, b, (dims, ((), ())), preferred_element_type=f32)  22.5 us
    pallas_call x4, Pallas kernels, attn_bwd(): pl.pallas_call(attn_bwd_kernel, grid=(steps,), in_specs=[pl.BlockSpec((sl...  18.9 us
    pallas_call x4, Pallas kernels, attn_fwd(): pl.pallas_call(attn_fwd_kernel, grid=(heads // 2,), in_specs=[pl.BlockSpe...  16.9 us
  transfers between devices with their start and end apart: 90, of which 34 were waited for; matrix products, arithmetic and copies ran while one was open for 13% of the time, Pallas kernels for 40%

profile of v1, /device:TPU:0, one launch (start us, length us, event | category | flops | bytes accessed | tf_op | source)
XLA Modules:
  0.0 356.3 jit_solution(1793655282171707886)
XLA Ops:
  19.8 5.3 %collective-permute-done.refs_2_.refs_6_ = bf16[128,1152]{1,0:T(8,128)(2,1)S(1)} collective-permute-done((bf16[128,1152]{1,0:T(8,128)(2,1)}, bf16[128,1152]{1,0:T(8,128)(2,1)S(1)}, u32[]{:S(2)}, u32[]{:S(2)}) %collective-permute-start) | collective-permute-done | bytes 294944 | tf_op jit(solution)/shard_map/ppermute | solution.py:898
  27.3 6.7 %collective-permute-done.3.refs_4_.refs_8_ = bf16[128,1152]{1,0:T(8,128)(2,1)S(1)} collective-permute-done((bf16[128,1152]{1,0:T(8,128)(2,1)S(1)}, bf16[128,1152]{1,0:T(8,128)(2,1)S(1)}, u32[]{:S(2)}, u32[]{:S(2)}) %collective-permute-start.3) | collective-permute-done | bytes 294944 | tf_op jit(solution)/shard_map/ppermute | solution.py:898
  34.7 3.3 xhat.4.refs_0_.x0_ref.xhat_ref
  44.2 7.1 %collective-permute-done.8.refs_6_.refs_10_ = bf16[128,1152]{1,0:T(8,128)(2,1)S(1)} collective-permute-done((bf16[128,1152]{1,0:T(8,128)(2,1)S(1)}, bf16[128,1152]{1,0:T(8,128)(2,1)S(1)}, u32[]{:S(2)}, u32[]{:S(2)}) %collective-permute-start.8) | collective-permute-done | bytes 294944 | tf_op jit(solution)/shard_map/ppermute | solution.py:898
  58.0 3.6 %xhat.6.refs_2_.x0_ref = f32[512,1024]{1,0:T(8,128)} custom-call(bf16[224,1024]{1,0:T(8,128)(2,1)} %collective-permute-done.2.refs_0_, bf16[288,1024]{1,0:T(8,128)(2,1)} %collective-permute-done.6.refs_1_), custom_call_target="tpu_custom_call" | custom-call | flops 143750000 | tf_op jit(solution)/shard_map/xhat/pallas_call | solution.py:192
  70.5 11.1 %qkv.1 = (bf16[2048,1024]{1,0:T(8,128)(2,1)}, bf16[2048,768]{1,0:T(8,128)(2,1)}, bf16[1024,768]{1,0:T(8,128)(2,1)}, bf16[1024,256]{1,0:T(8,128)(2,1)}) custom-call(s32[8]{0:T(128)} %stack.53.where_ref, f32[8,1024]{1,0:T(8,128)} %small_rows.1.small_ref, f32[512,1024]{1,0:T(8,128)} %xhat.4.refs_0_.x0_ref.xhat_ref, f32[512,1024]{1,0:T(8,128)} %xhat.5.refs_1_.x1_ref, ...), custom_call_target="tpu_custom_call" | custom-call | flops 8049999872 | tf_op jit(solution)/shard_map/qkv/pallas_call | solution.py:246
  81.6 4.3 %attn_fwd.7 = (bf16[512,256]{1,0:T(8,128)(2,1)}, bf16[4,512,512]{2,1,0:T(8,128)(2,1)}) custom-call(s32[1]{0:T(128)} %collective-permute-done.11.len_ref, bf16[2048,768]{1,0:T(8,128)(2,1)} %get-tuple-element.170.qkv_ref, f32[4,4,128,128]{3,2,1,0:T(8,128)} %bias_tiles.1.tiles_ref), custom_call_target="tpu_custom_call" | custom-call | flops 8625000448 | tf_op jit(solution)/shard_map/attn_fwd/pallas_call | solution.py:346
  87.9 4.3 %attn_fwd.6 = (bf16[512,256]{1,0:T(8,128)(2,1)}, bf16[4,512,512]{2,1,0:T(8,128)(2,1)}) custom-call(s32[1]{0:T(128)} %collective-permute-done.5.len_ref, bf16[2048,768]{1,0:T(8,128)(2,1)} %get-tuple-element.170.qkv_ref, f32[4,4,128,128]{3,2,1,0:T(8,128)} %bias_tiles.1.tiles_ref), custom_call_target="tpu_custom_call" | custom-call | flops 8625000448 | tf_op jit(solution)/shard_map/attn_fwd/pallas_call | solution.py:346
  94.3 4.4 %attn_fwd.5 = (bf16[512,256]{1,0:T(8,128)(2,1)}, bf16[4,512,512]{2,1,0:T(8,128)(2,1)}) custom-call(s32[1]{0:T(128)} %collective-permute-done.10.len_ref, bf16[2048,768]{1,0:T(8,128)(2,1)} %get-tuple-element.170.qkv_ref, f32[4,4,128,128]{3,2,1,0:T(8,128)} %bias_tiles.1.tiles_ref), custom_call_target="tpu_custom_call" | custom-call | flops 8625000448 | tf_op jit(solution)/shard_map/attn_fwd/pallas_call | solution.py:346
  101.6 10.3 %collective-permute-done.22.refs_6_.refs_4_ = bf16[1024,256]{1,0:T(8,128)(2,1)S(1)} collective-permute-done((bf16[1024,256]{1,0:T(8,128)(2,1)S(1)}, bf16[1024,256]{1,0:T(8,128)(2,1)S(1)}, u32[]{:S(2)}, u32[]{:S(2)}) %collective-permute-start.22) | collective-permute-done | bytes 524320 | tf_op jit(solution)/shard_map/ppermute | solution.py:904
  112.5 3.8 %attn_fwd.4 = (bf16[512,256]{1,0:T(8,128)(2,1)}, bf16[4,512,512]{2,1,0:T(8,128)(2,1)}) custom-call(s32[1]{0:T(128)} %copy.64.len_ref, bf16[2048,768]{1,0:T(8,128)(2,1)} %get-tuple-element.170.qkv_ref, f32[4,4,128,128]{3,2,1,0:T(8,128)} %bias_tiles.1.tiles_ref), custom_call_target="tpu_custom_call" | custom-call | flops 8625000448 | tf_op jit(solution)/shard_map/attn_fwd/pallas_call | solution.py:346
  117.4 3.9 %out_ln2.2 = (f32[512,1024]{1,0:T(8,128)}, bf16[512,1024]{1,0:T(8,128)(2,1)}, bf16[256,1024]{1,0:T(8,128)(2,1)}) custom-call(s32[1]{0:T(128)} %bitcast.n_ref, s32[1]{0:T(128)} %copy.64.len_ref, bf16[512,1024]{1,0:T(8,128)(2,1)} %tok_ref.5, f32[8,1024]{1,0:T(8,128)} %small_rows.1.small_ref, bf16[512,256]{1,0:T(8,128)(2,1)} %get-tuple-element.171.refs_0_.att_ref, ...), custom_call_target="tpu_custom_call" | custom-call | flops 71875000 | tf_op jit(solution)/shard_map/out_ln2/pallas_call | solution.py:510
  121.3 3.9 %out_ln2.3 = (f32[512,1024]{1,0:T(8,128)}, bf16[512,1024]{1,0:T(8,128)(2,1)}, bf16[256,1024]{1,0:T(8,128)(2,1)}) custom-call(s32[1]{0:T(128)} %bitcast.n_ref, s32[1]{0:T(128)} %copy.64.len_ref, bf16[512,1024]{1,0:T(8,128)(2,1)} %tok_ref.5, f32[8,1024]{1,0:T(8,128)} %small_rows.1.small_ref, ...), custom_call_target="tpu_custom_call", output_to_operand_aliasing={{0}: (12, {}), {1}: (13, {})} | custom-call | flops 71875000 | tf_op jit(solution)/shard_map/out_ln2/pallas_call | solution.py:510
  128.2 16.5 %ffn.3 = (f32[512,1024]{1,0:T(8,128)}, f32[512,1024]{1,0:T(8,128)}, bf16[512,1024]{1,0:T(8,128)(2,1)}, bf16[128,1024]{1,0:T(8,128)(2,1)}, bf16[128,1024]{1,0:T(8...) custom-call(bf16[8,2,128,1024]{3,2,1,0:T(8,128)(2,1)} %bitcast.118, ...), custom_call_target="tpu_custom_call" | custom-call | flops 215624992 | tf_op jit(solution)/shard_map/ffn/pallas_call | solution.py:701
  148.7 10.7 %ffn.4 = (f32[256,1024]{1,0:T(8,128)}, f32[256,1024]{1,0:T(8,128)}, bf16[256,1024]{1,0:T(8,128)(2,1)}, bf16[64,1024]{1,0:T(8,128)(2,1)}, bf16[64,1024]{1,0:T(8,1...) custom-call(bf16[8,2,128,1024]{3,2,1,0:T(8,128)(2,1)} %bitcast.119, ...), custom_call_target="tpu_custom_call", output_to_operand_aliasing={{7}: (8, {}), {8}: (9, {}), {9}: (10, {}), {10}: (11, {})} | custom-call | flops 143750000 | tf_op jit(solution)/shard_map/ffn/pallas_call | solution.py:701
  165.6 10.6 %ffn.5 = (f32[256,1024]{1,0:T(8,128)}, f32[256,1024]{1,0:T(8,128)}, bf16[256,1024]{1,0:T(8,128)(2,1)}, bf16[64,1024]{1,0:T(8,128)(2,1)}, bf16[64,1024]{1,0:T(8,1...) custom-call(bf16[8,2,128,1024]{3,2,1,0:T(8,128)(2,1)} %bitcast.120, ...), custom_call_target="tpu_custom_call", output_to_operand_aliasing={{7}: (8, {}), {8}: (9, {}), {9}: (10, {}), {10}: (11, {})} | custom-call | flops 143750000 | tf_op jit(solution)/shard_map/ffn/pallas_call | solution.py:701
  180.8 8.2 %convolution_convert_fusion.1 = bf16[1024,1024]{1,0:T(8,128)(2,1)S(1)} fusion(bf16[2048,1024]{1,0:T(8,128)(2,1)} %get-tuple-element.221, bf16[2048,1024]{1,0:T(8,128)(2,1)} %get-tuple-element.223), kind=kOutput, calls=%fused_computation.5 | convolution fusion | flops 4296015872 | bytes 10485760 | tf_op jit(solution)/shard_map/dot_general | solution.py:32
  189.0 5.0 %convolution_convert_fusion = bf16[1024,1024]{1,0:T(8,128)(2,1)S(1)} fusion(bf16[2048,1024]{1,0:T(8,128)(2,1)S(1)} %copy-done.2, bf16[2048,1024]{1,0:T(8,128)(2,1)S(1)} %copy-done.1), kind=kOutput, calls=%fused_computation.4 | convolution fusion | flops 4296015872 | bytes 10485760 | tf_op jit(solution)/shard_map/dot_general | solution.py:32
  197.8 5.0 %ln2_back.2 = (f32[512,1024]{1,0:T(8,128)}, bf16[512,512]{1,0:T(8,128)(2,1)}, bf16[512,512]{1,0:T(8,128)(2,1)}, bf16[512,256]{1,0:T(8,128)(2,1)}, bf16[512,256]{...) custom-call(s32[1]{0:T(128)} %bitcast.n_ref, s32[1]{0:T(128)} %copy.64.len_ref, ...), custom_call_target="tpu_custom_call" | custom-call | flops 5750000128 | tf_op jit(solution)/shard_map/ln2_back/pallas_call | solution.py:569
  203.8 5.2 %ln2_back.3 = (f32[512,1024]{1,0:T(8,128)}, bf16[512,512]{1,0:T(8,128)(2,1)}, bf16[512,512]{1,0:T(8,128)(2,1)}, bf16[512,256]{1,0:T(8,128)(2,1)}, bf16[512,256]{...) custom-call(s32[1]{0:T(128)} %bitcast.n_ref, ...), custom_call_target="tpu_custom_call", output_to_operand_aliasing={{0}: (13, {}), {1}: (14, {}), {2}: (15, {}), {3}: (16, {}),... | custom-call | flops 5750000128 | tf_op jit(solution)/shard_map/ln2_back/pallas_call | solution.py:569
  213.0 4.7 %attn_bwd.4 = (bf16[2048,768]{1,0:T(8,128)(2,1)}, f32[2,2,512]{2,1,0:T(2,128)}) custom-call(bf16[2048,768]{1,0:T(8,128)(2,1)} %get-tuple-element.170.qkv_ref, bf16[512,256]{1,0:T(8,128)(2,1)} %get-tuple-element.229.ga_ref, bf16[512,256]{1,0:T(8,128)(2,1)} %get-tuple-element.171.refs_0_.att_ref, bf16[4,512,512]{2,1,0:T(8,128)(2,1)} %get-tuple-element.230.p_ref), custom_call_target="tpu_custom_call" | custom-call | flops 1150000000 | tf_op jit(solution)/shard_map/attn_bwd/pallas_call | solution.py:431
  230.1 5.0 %attn_bwd.5 = (bf16[2048,768]{1,0:T(8,128)(2,1)}, f32[2,2,512]{2,1,0:T(2,128)}) custom-call(bf16[2048,768]{1,0:T(8,128)(2,1)} %get-tuple-element.170.qkv_ref, bf16[512,256]{1,0:T(8,128)(2,1)} %copy-done.45, bf16[512,256]{1,0:T(8,128)(2,1)} %get-tuple-element.173.att_ref, ...), custom_call_target="tpu_custom_call", output_to_operand_aliasing={{0}: (4, {})} | custom-call | flops 1150000000 | tf_op jit(solution)/shard_map/attn_bwd/pallas_call | solution.py:431
  235.4 4.6 %attn_bwd.6 = (bf16[2048,768]{1,0:T(8,128)(2,1)}, f32[2,2,512]{2,1,0:T(2,128)}) custom-call(bf16[2048,768]{1,0:T(8,128)(2,1)} %get-tuple-element.170.qkv_ref, bf16[512,256]{1,0:T(8,128)(2,1)} %copy-done.44, bf16[512,256]{1,0:T(8,128)(2,1)} %get-tuple-element.174.att_ref, ...), custom_call_target="tpu_custom_call", output_to_operand_aliasing={{0}: (4, {})} | custom-call | flops 1150000000 | tf_op jit(solution)/shard_map/attn_bwd/pallas_call | solution.py:431
  241.4 7.3 %ln1_back.2 = (bf16[512,1024]{1,0:T(8,128)(2,1)}, bf16[512,1024]{1,0:T(8,128)(2,1)}, f32[2,1024]{1,0:T(2,128)}) custom-call(bf16[2048,768]{1,0:T(8,128)(2,1)} %get-tuple-element.249.gp_ref.refs_0_, bf16[1024,768]{1,0:T(8,128)(2,1)} %get-tuple-element.250.wq_ref, f32[512,1024]{1,0:T(8,128)} %xhat.6.refs_2_.x0_ref, f32[512,1024]{1,0:T(8,128)} %xhat.7.refs_3_.x1_ref), custom_call_target="tpu_custom_call" | custom-call | flops 575000000 | tf_op jit(solution)/shard_map/ln1_back/pallas_call | solution.py:291
  253.7 4.7 %attn_bwd.7 = (bf16[2048,768]{1,0:T(8,128)(2,1)}, f32[2,2,512]{2,1,0:T(2,128)}) custom-call(bf16[2048,768]{1,0:T(8,128)(2,1)} %get-tuple-element.170.qkv_ref, bf16[512,256]{1,0:T(8,128)(2,1)} %copy-done.46, bf16[512,256]{1,0:T(8,128)(2,1)} %get-tuple-element.172.att_ref, ...), custom_call_target="tpu_custom_call", output_to_operand_aliasing={{0}: (4, {})} | custom-call | flops 1150000000 | tf_op jit(solution)/shard_map/attn_bwd/pallas_call | solution.py:431
  260.5 6.4 %collective-permute-done.63.p2_ref = bf16[256,1024]{1,0:T(8,128)(2,1)S(1)} collective-permute-done((bf16[256,1024]{1,0:T(8,128)(2,1)S(1)}, bf16[256,1024]{1,0:T(8,128)(2,1)S(1)}, u32[]{:S(2)}, u32[]{:S(2)}) %collective-permute-start.63) | collective-permute-done | bytes 524320 | tf_op jit(solution)/shard_map/ppermute | solution.py:904
  266.8 6.9 %convolution_convert_fusion.2 = bf16[1024,768]{1,0:T(8,128)(2,1)S(1)} fusion(bf16[2048,1024]{1,0:T(8,128)(2,1)} %get-tuple-element.183, bf16[2048,768]{1,0:T(8,128)(2,1)} %get-tuple-element.257.gp_ref), kind=kOutput, calls=%fused_computation.6 | convolution fusion | flops 3222011904 | bytes 8912896 | tf_op jit(solution)/shard_map/dot_general | solution.py:32
  278.0 7.8 %ln1_back.3 = (f32[512,1024]{1,0:T(8,128)}, bf16[512,1024]{1,0:T(8,128)(2,1)}, f32[2,1024]{1,0:T(2,128)}) custom-call(bf16[2048,768]{1,0:T(8,128)(2,1)} %get-tuple-element.257.gp_ref, bf16[1024,768]{1,0:T(8,128)(2,1)} %get-tuple-element.250.wq_ref, f32[512,1024]{1,0:T(8,128)} %xhat.4.refs_0_.x0_ref.xhat_ref, f32[512,1024]{1,0:T(8,128)} %xhat.5.refs_1_.x1_ref), custom_call_target="tpu_custom_call" | custom-call | flops 5750000128 | tf_op jit(solution)/shard_map/ln1_back/pallas_call | solution.py:291
  297.3 4.9 %collective-permute-done.70.p3_ref = bf16[256,1024]{1,0:T(8,128)(2,1)S(1)} collective-permute-done((bf16[256,1024]{1,0:T(8,128)(2,1)S(1)}, bf16[256,1024]{1,0:T(8,128)(2,1)S(1)}, u32[]{:S(2)}, u32[]{:S(2)}) %collective-permute-start.70) | collective-permute-done | bytes 524320 | tf_op jit(solution)/shard_map/ppermute | solution.py:904
  304.8 3.9 %join_ffn.1 = (f32[128,4096]{1,0:T(8,128)}, f32[512,1024]{1,0:T(8,128)}) custom-call(s32[1]{0:T(128)} %bitcast.n_ref, bf16[128,2048]{1,0:T(8,128)(2,1)} %copy-done.8, bf16[128,2048]{1,0:T(8,128)(2,1)} %collective-permute-done.71.refs_1_, bf16[128,2048]{1,0:T(8,128)(2,1)} %collective-permute-done.67.refs_2_, bf16[128,2048]{1,0:T(8,128)(2,1)} %copy-done.32), custom_call_target="tpu_custom_call" | custom-call | flops 230000000 | tf_op jit(solution)/shard_map/join_ffn/pallas_call | solution.py:820
  315.1 5.8 %ln1_last.1 = f32[512,1024]{1,0:T(8,128)} custom-call(bf16[512,1024]{1,0:T(8,128)(2,1)} %tok_ref.5, f32[512,1024]{1,0:T(8,128)} %xhat.4.refs_0_.x0_ref.xhat_ref, f32[512,1024]{1,0:T(8,128)} %get-tuple-element.277.gmid_ref, f32[8,1024]{1,0:T(8,128)} %small_rows.1.small_ref, f32[512,1024]{1,0:T(8,128)} %get-tuple-element.279.p0_ref, ...), custom_call_target="tpu_custom_call" | custom-call | flops 287500000 | tf_op jit(solution)/shard_map/ln1_last/pallas_call | solution.py:472
  326.2 4.5 %collective-permute-done.80 = bf16[128,1280]{1,0:T(8,128)(2,1)S(1)} collective-permute-done((bf16[128,1280]{1,0:T(8,128)(2,1)S(1)}, bf16[128,1280]{1,0:T(8,128)(2,1)S(1)}, u32[]{:S(2)}, u32[]{:S(2)}) %collective-permute-start.80) | collective-permute-done | bytes 327712 | tf_op jit(solution)/shard_map/ppermute | solution.py:898
  (385 shorter events, 141.1 us)
Async XLA Ops:
  7.2 121.0 %all-gather.3.cloned.1.call-start = ((), (), s32[]{:S(2)}) async-start(), calls=%async_computation | async-start | bytes 4718592 | tf_op jit(solution)/shard_map/all_gather | solution.py:1070
  7.2 30.7 %collective-permute-start.7 = (bf16[512,1024]{1,0:T(8,128)(2,1)}, bf16[512,1024]{1,0:T(8,128)(2,1)S(1)}, u32[]{:S(2)}, u32[]{:S(2)}) collective-permute-start(bf16[512,1024]{1,0:T(8,128)(2,1)} %tok_ref.5), channel_id=1, source_target_pairs={{0,8},{8,0},{16,24},{24,16},{1,9},{9,1},{17,25},{25,17},{2,10},{10... | collective-permute-start | bytes 3145736 | tf_op jit(solution)/shard_map/ppermute | solution.py:904
  8.8 16.3 %collective-permute-start.2 = (bf16[224,1024]{1,0:T(8,128)(2,1)S(1)}, bf16[224,1024]{1,0:T(8,128)(2,1)}, u32[]{:S(2)}, u32[]{:S(2)}) collective-permute-start(bf16[224,1024]{1,0:T(8,128)(2,1)S(1)} %slice.51), channel_id=1, source_target_pairs={{0,16},{8,24},{16,0},{24,8},{1,17},{9,25},{17,1},{25,9},{2,18},{10... | collective-permute-start | bytes 1376264 | tf_op jit(solution)/shard_map/ppermute | solution.py:904
  17.5 24.6 %collective-permute-start.6 = (bf16[288,1024]{1,0:T(8,128)(2,1)S(1)}, bf16[288,1024]{1,0:T(8,128)(2,1)}, u32[]{:S(2)}, u32[]{:S(2)}) collective-permute-start(bf16[288,1024]{1,0:T(8,128)(2,1)S(1)} %slice.52), channel_id=1, source_target_pairs={{0,16},{8,24},{16,0},{24,8},{1,17},{9,25},{17,1},{25,9},{2,18},{10... | collective-permute-start | bytes 1769480 | tf_op jit(solution)/shard_map/ppermute | solution.py:904
  27.2 14.9 %collective-permute-start.5 = (s32[1]{0:T(128)}, s32[1]{0:T(128)}, u32[]{:S(2)}, u32[]{:S(2)}) collective-permute-start(s32[1]{0:T(128)} %param.14), channel_id=1, source_target_pairs={{0,16},{8,24},{16,0},{24,8},{1,17},{9,25},{17,1},{25,9},{2,18},{10... | collective-permute-start | bytes 20 | tf_op jit(solution)/shard_map/ppermute | solution.py:904
  61.6 50.4 %collective-permute-start.14 = (bf16[512,1024]{1,0:T(8,128)(2,1)S(1)}, bf16[512,1024]{1,0:T(8,128)(2,1)S(1)}, u32[]{:S(2)}, u32[]{:S(2)}) collective-permute-start(bf16[512,1024]{1,0:T(8,128)(2,1)S(1)} %multiply_convert_fusion.refs_4_), channel_id=1, source_target_pairs={{0,16},{8,24},{16,0},{24,8},{1,17},{9,25},{17,1},{25,9},{2,18},{10... | collective-permute-start | bytes 3145736 | tf_op jit(solution)/shard_map/ppermute | solution.py:904
  61.8 65.5 %collective-permute-start.13 = (bf16[512,1024]{1,0:T(8,128)(2,1)S(1)}, bf16[512,1024]{1,0:T(8,128)(2,1)}, u32[]{:S(2)}, u32[]{:S(2)}) collective-permute-start(bf16[512,1024]{1,0:T(8,128)(2,1)S(1)} %multiply_convert_fusion.refs_4_), channel_id=1, source_target_pairs={{0,8},{8,0},{16,24},{24,16},{1,9},{9,1},{17,25},{25,17},{2,10},{10... | collective-permute-start | bytes 3145736 | tf_op jit(solution)/shard_map/ppermute | solution.py:904
  92.5 19.5 %collective-permute-start.22 = (bf16[1024,256]{1,0:T(8,128)(2,1)S(1)}, bf16[1024,256]{1,0:T(8,128)(2,1)S(1)}, u32[]{:S(2)}, u32[]{:S(2)}) collective-permute-start(bf16[1024,256]{1,0:T(8,128)(2,1)S(1)} %copy-done.10), channel_id=1, source_target_pairs={{0,16},{8,24},{16,0},{24,8},{1,17},{9,25},{17,1},{25,9},{2,18},{10... | collective-permute-start | bytes 1572872 | tf_op jit(solution)/shard_map/ppermute | solution.py:904
  98.7 17.6 %collective-permute-start.21 = (bf16[1024,256]{1,0:T(8,128)(2,1)S(1)}, bf16[1024,256]{1,0:T(8,128)(2,1)S(1)}, u32[]{:S(2)}, u32[]{:S(2)}) collective-permute-start(bf16[1024,256]{1,0:T(8,128)(2,1)S(1)} %copy-done.10), channel_id=1, source_target_pairs={{0,8},{8,0},{16,24},{24,16},{1,9},{9,1},{17,25},{25,17},{2,10},{10... | collective-permute-start | bytes 1572872 | tf_op jit(solution)/shard_map/ppermute | solution.py:904
  101.6 14.7 %collective-permute-start.18 = (bf16[512,256]{1,0:T(8,128)(2,1)}, bf16[512,256]{1,0:T(8,128)(2,1)S(1)}, u32[]{:S(2)}, u32[]{:S(2)}) collective-permute-start(bf16[512,256]{1,0:T(8,128)(2,1)} %get-tuple-element.172.att_ref), channel_id=1, source_target_pairs={{0,8},{8,0},{16,24},{24,16},{1,9},{9,1},{17,25},{25,17},{2,10},{10... | collective-permute-start | bytes 786440 | tf_op jit(solution)/shard_map/ppermute | solution.py:904
  112.0 34.8 %collective-permute-start.15 = (bf16[512,1024]{1,0:T(8,128)(2,1)S(1)}, bf16[512,1024]{1,0:T(8,128)(2,1)S(1)}, u32[]{:S(2)}, u32[]{:S(2)}) collective-permute-start(bf16[512,1024]{1,0:T(8,128)(2,1)S(1)} %collective-permute-done.14.refs_5_), channel_id=1, source_target_pairs={{0,8},{8,0},{16,24},{24,16},{1,9},{9,1},{17,25},{25,17},{2,10},{10... | collective-permute-start | bytes 3145736 | tf_op jit(solution)/shard_map/ppermute | solution.py:904
  125.7 19.0 %collective-permute-start.27 = (bf16[256,1024]{1,0:T(8,128)(2,1)}, bf16[256,1024]{1,0:T(8,128)(2,1)}, u32[]{:S(2)}, u32[]{:S(2)}) collective-permute-start(bf16[256,1024]{1,0:T(8,128)(2,1)} %get-tuple-element.180.refs_0_), channel_id=1, source_target_pairs={{0,16},{8,24},{16,0},{24,8},{1,17},{9,25},{17,1},{25,9},{2,18},{10... | collective-permute-start | bytes 1572872 | tf_op jit(solution)/shard_map/ppermute | solution.py:904
  127.3 33.2 %collective-permute-start.26 = (bf16[256,1024]{1,0:T(8,128)(2,1)}, bf16[256,1024]{1,0:T(8,128)(2,1)S(1)}, u32[]{:S(2)}, u32[]{:S(2)}) collective-permute-start(bf16[256,1024]{1,0:T(8,128)(2,1)} %get-tuple-element.181.refs_1_), channel_id=1, source_target_pairs={{0,16},{8,24},{16,0},{24,8},{1,17},{9,25},{17,1},{25,9},{2,18},{10... | collective-permute-start | bytes 1572872 | tf_op jit(solution)/shard_map/ppermute | solution.py:904
  163.1 17.1 %collective-permute-start.47 = (bf16[256,1024]{1,0:T(8,128)(2,1)S(1)}, bf16[256,1024]{1,0:T(8,128)(2,1)S(1)}, u32[]{:S(2)}, u32[]{:S(2)}) collective-permute-start(bf16[256,1024]{1,0:T(8,128)(2,1)S(1)} %add_convert_fusion.12), channel_id=1, source_target_pairs={{0,16},{8,24},{16,0},{24,8},{1,17},{9,25},{17,1},{25,9},{2,18},{10... | collective-permute-start | bytes 1572872 | tf_op jit(solution)/shard_map/ppermute | solution.py:904
  177.8 17.9 %collective-permute-start.48 = (bf16[128,1024]{1,0:T(8,128)(2,1)S(1)}, bf16[128,1024]{1,0:T(8,128)(2,1)S(1)}, u32[]{:S(2)}, u32[]{:S(2)}) collective-permute-start(bf16[128,1024]{1,0:T(8,128)(2,1)S(1)} %copy-done.70), channel_id=1, source_target_pairs={{0,8},{8,0},{16,24},{24,16},{1,9},{9,1},{17,25},{25,17},{2,10},{10... | collective-permute-start | bytes 786440 | tf_op jit(solution)/shard_map/ppermute | solution.py:904
  178.0 18.7 %collective-permute-start.49 = (bf16[128,1024]{1,0:T(8,128)(2,1)S(1)}, bf16[128,1024]{1,0:T(8,128)(2,1)S(1)}, u32[]{:S(2)}, u32[]{:S(2)}) collective-permute-start(bf16[128,1024]{1,0:T(8,128)(2,1)S(1)} %copy-done.69), channel_id=1, source_target_pairs={{0,8},{8,0},{16,24},{24,16},{1,9},{9,1},{17,25},{25,17},{2,10},{10... | collective-permute-start | bytes 786440 | tf_op jit(solution)/shard_map/ppermute | solution.py:904
  178.3 24.5 %collective-permute-start.45 = (bf16[128,1024]{1,0:T(8,128)(2,1)S(1)}, bf16[128,1024]{1,0:T(8,128)(2,1)S(1)}, u32[]{:S(2)}, u32[]{:S(2)}) collective-permute-start(bf16[128,1024]{1,0:T(8,128)(2,1)S(1)} %copy-done.68), channel_id=1, source_target_pairs={{0,8},{8,0},{16,24},{24,16},{1,9},{9,1},{17,25},{25,17},{2,10},{10... | collective-permute-start | bytes 786440 | tf_op jit(solution)/shard_map/ppermute | solution.py:904
  178.5 24.3 %collective-permute-start.46 = (bf16[128,1024]{1,0:T(8,128)(2,1)S(1)}, bf16[128,1024]{1,0:T(8,128)(2,1)S(1)}, u32[]{:S(2)}, u32[]{:S(2)}) collective-permute-start(bf16[128,1024]{1,0:T(8,128)(2,1)S(1)} %copy-done.67), channel_id=1, source_target_pairs={{0,8},{8,0},{16,24},{24,16},{1,9},{9,1},{17,25},{25,17},{2,10},{10... | collective-permute-start | bytes 786440 | tf_op jit(solution)/shard_map/ppermute | solution.py:904
  180.3 22.6 %collective-permute-start.44 = (bf16[256,1024]{1,0:T(8,128)(2,1)S(1)}, bf16[256,1024]{1,0:T(8,128)(2,1)S(1)}, u32[]{:S(2)}, u32[]{:S(2)}) collective-permute-start(bf16[256,1024]{1,0:T(8,128)(2,1)S(1)} %add_convert_fusion.11), channel_id=1, source_target_pairs={{0,16},{8,24},{16,0},{24,8},{1,17},{9,25},{17,1},{25,9},{2,18},{10... | collective-permute-start | bytes 1572872 | tf_op jit(solution)/shard_map/ppermute | solution.py:904
  195.7 14.9 %collective-permute-start.53 = (bf16[128,2048]{1,0:T(8,128)(2,1)S(1)}, bf16[128,2048]{1,0:T(8,128)(2,1)S(1)}, u32[]{:S(2)}, u32[]{:S(2)}) collective-permute-start(bf16[128,2048]{1,0:T(8,128)(2,1)S(1)} %pad_maximum_fusion.1), channel_id=1, source_target_pairs={{2,0},{4,2},{6,4},{7,6},{5,7},{3,5},{1,3},{0,1},{9,8},{8,10},{10,1... | collective-permute-start | bytes 1572872 | tf_op jit(solution)/shard_map/ppermute | solution.py:898
  196.7 13.9 %collective-permute-start.52 = (bf16[128,2048]{1,0:T(8,128)(2,1)S(1)}, bf16[128,2048]{1,0:T(8,128)(2,1)S(1)}, u32[]{:S(2)}, u32[]{:S(2)}) collective-permute-start(bf16[128,2048]{1,0:T(8,128)(2,1)S(1)} %pad_maximum_fusion), channel_id=1, source_target_pairs={{0,2},{2,4},{4,6},{6,7},{7,5},{5,3},{3,1},{1,0},{8,9},{10,8},{12,1... | collective-permute-start | bytes 1572872 | tf_op jit(solution)/shard_map/ppermute | solution.py:898
  210.7 14.6 %collective-permute-start.57 = (bf16[128,2048]{1,0:T(8,128)(2,1)S(1)}, bf16[128,2048]{1,0:T(8,128)(2,1)S(1)}, u32[]{:S(2)}, u32[]{:S(2)}) collective-permute-start(bf16[128,2048]{1,0:T(8,128)(2,1)S(1)} %add_convert_fusion.9), channel_id=1, source_target_pairs={{2,0},{4,2},{6,4},{7,6},{5,7},{3,5},{1,3},{0,1},{9,8},{8,10},{10,1... | collective-permute-start | bytes 1572872 | tf_op jit(solution)/shard_map/ppermute | solution.py:898
  225.5 14.6 %collective-permute-start.61 = (bf16[128,2048]{1,0:T(8,128)(2,1)S(1)}, bf16[128,2048]{1,0:T(8,128)(2,1)S(1)}, u32[]{:S(2)}, u32[]{:S(2)}) collective-permute-start(bf16[128,2048]{1,0:T(8,128)(2,1)S(1)} %add_convert_fusion.6), channel_id=1, source_target_pairs={{2,0},{4,2},{6,4},{7,6},{5,7},{3,5},{1,3},{0,1},{9,8},{8,10},{10,1... | collective-permute-start | bytes 1572872 | tf_op jit(solution)/shard_map/ppermute | solution.py:898
  227.9 13.4 %collective-permute-start.59 = (bf16[256,1024]{1,0:T(8,128)(2,1)S(1)}, bf16[256,1024]{1,0:T(8,128)(2,1)S(1)}, u32[]{:S(2)}, u32[]{:S(2)}) collective-permute-start(bf16[256,1024]{1,0:T(8,128)(2,1)S(1)} %add_convert_fusion.8), channel_id=1, source_target_pairs={{0,16},{8,24},{16,0},{24,8},{1,17},{9,25},{17,1},{25,9},{2,18},{10... | collective-permute-start | bytes 1572872 | tf_op jit(solution)/shard_map/ppermute | solution.py:904
  250.0 44.1 %collective-permute-start.76 = (bf16[256,1024]{1,0:T(8,128)(2,1)}, bf16[256,1024]{1,0:T(8,128)(2,1)}, u32[]{:S(2)}, u32[]{:S(2)}) collective-permute-start(bf16[256,1024]{1,0:T(8,128)(2,1)} %get-tuple-element.283), channel_id=1, source_target_pairs={{0,8},{8,0},{16,24},{24,16},{1,9},{9,1},{17,25},{25,17},{2,10},{10... | collective-permute-start | bytes 1572872 | tf_op jit(solution)/shard_map/ppermute | solution.py:904
  252.5 14.4 %collective-permute-start.63 = (bf16[256,1024]{1,0:T(8,128)(2,1)S(1)}, bf16[256,1024]{1,0:T(8,128)(2,1)S(1)}, u32[]{:S(2)}, u32[]{:S(2)}) collective-permute-start(bf16[256,1024]{1,0:T(8,128)(2,1)S(1)} %get-tuple-element.330), channel_id=1, source_target_pairs={{0,16},{8,24},{16,0},{24,8},{1,17},{9,25},{17,1},{25,9},{2,18},{10... | collective-permute-start | bytes 1572872 | tf_op jit(solution)/shard_map/ppermute | solution.py:904
  273.9 13.9 %collective-permute-start.65 = (bf16[128,1280]{1,0:T(8,128)(2,1)S(1)}, bf16[128,1280]{1,0:T(8,128)(2,1)}, u32[]{:S(2)}, u32[]{:S(2)}) collective-permute-start(bf16[128,1280]{1,0:T(8,128)(2,1)S(1)} %pad_maximum_fusion.3), channel_id=1, source_target_pairs={{2,0},{4,2},{6,4},{7,6},{5,7},{3,5},{1,3},{0,1},{9,8},{8,10},{10,1... | collective-permute-start | bytes 983048 | tf_op jit(solution)/shard_map/ppermute | solution.py:898
  277.9 25.1 %collective-permute-start.71 = (bf16[128,2048]{1,0:T(8,128)(2,1)S(1)}, bf16[128,2048]{1,0:T(8,128)(2,1)}, u32[]{:S(2)}, u32[]{:S(2)}) collective-permute-start(bf16[128,2048]{1,0:T(8,128)(2,1)S(1)} %add_convert_fusion.4.refs_0_), channel_id=1, source_target_pairs={{0,8},{8,0},{16,24},{24,16},{1,9},{9,1},{17,25},{25,17},{2,10},{10... | collective-permute-start | bytes 1572872 | tf_op jit(solution)/shard_map/ppermute | solution.py:904
  292.1 16.6 %collective-permute-start.69 = (bf16[128,1280]{1,0:T(8,128)(2,1)S(1)}, bf16[128,1280]{1,0:T(8,128)(2,1)S(1)}, u32[]{:S(2)}, u32[]{:S(2)}) collective-permute-start(bf16[128,1280]{1,0:T(8,128)(2,1)S(1)} %add_convert_fusion.17), channel_id=1, source_target_pairs={{2,0},{4,2},{6,4},{7,6},{5,7},{3,5},{1,3},{0,1},{9,8},{8,10},{10,1... | collective-permute-start | bytes 983048 | tf_op jit(solution)/shard_map/ppermute | solution.py:898
  294.1 15.6 %collective-permute-start.68 = (bf16[128,1280]{1,0:T(8,128)(2,1)S(1)}, bf16[128,1280]{1,0:T(8,128)(2,1)S(1)}, u32[]{:S(2)}, u32[]{:S(2)}) collective-permute-start(bf16[128,1280]{1,0:T(8,128)(2,1)S(1)} %add_convert_fusion.18), channel_id=1, source_target_pairs={{0,2},{2,4},{4,6},{6,7},{7,5},{5,3},{3,1},{1,0},{8,9},{10,8},{12,1... | collective-permute-start | bytes 983048 | tf_op jit(solution)/shard_map/ppermute | solution.py:898
  303.0 21.8 %collective-permute-start.79 = (bf16[512,1024]{1,0:T(8,128)(2,1)}, bf16[512,1024]{1,0:T(8,128)(2,1)S(1)}, u32[]{:S(2)}, u32[]{:S(2)}) collective-permute-start(bf16[512,1024]{1,0:T(8,128)(2,1)} %get-tuple-element.290), channel_id=1, source_target_pairs={{0,8},{8,0},{16,24},{24,16},{1,9},{9,1},{17,25},{25,17},{2,10},{10... | collective-permute-start | bytes 3145736 | tf_op jit(solution)/shard_map/ppermute | solution.py:904
  308.7 13.8 %collective-permute-start.77 = (bf16[256,1024]{1,0:T(8,128)(2,1)}, bf16[256,1024]{1,0:T(8,128)(2,1)S(1)}, u32[]{:S(2)}, u32[]{:S(2)}) collective-permute-start(bf16[256,1024]{1,0:T(8,128)(2,1)} %add_convert_fusion.3), channel_id=1, source_target_pairs={{0,16},{8,24},{16,0},{24,8},{1,17},{9,25},{17,1},{25,9},{2,18},{10... | collective-permute-start | bytes 1572872 | tf_op jit(solution)/shard_map/ppermute | solution.py:904
  (136 other events, 823.5 us)
Sparse Core Ops, SparseCore 0:
  52.5 72.7 all-gather.2

commit v2 on v1

--- a/solution.py
+++ b/solution.py
@@ -262,7 +262,7 @@
             pltpu.SemaphoreType.DMA((2,)),
         ],
         compiler_params=pltpu.CompilerParams(vmem_limit_bytes=VMEM_LIMIT),
-        cost_estimate=cost(7),
+        cost_estimate=cost(7, 0.05),
         name="qkv",
     )(where, small, *xhats, *pieces)
 
@@ -360,7 +360,7 @@
             jax.ShapeDtypeStruct((heads, slot, slot), bf16),
         ],
         compiler_params=pltpu.CompilerParams(vmem_limit_bytes=VMEM_LIMIT),
-        cost_estimate=cost(7.5),
+        cost_estimate=cost(4.5, 0.1),
         name="attn_fwd",
     )(lengths, packed, tiles)
 
@@ -1073,15 +1073,17 @@
         xhats = [xhat_of(t) for t in tokens_all]
     valid = (jnp.arange(slot, dtype=jnp.int32) < lengths[0]).astype(f32)[:, None]
     cotan = cotangent.astype(f32)
-    grad_ffn = at.all_narrow(after((valid * cotan).astype(bf16), xhats[2]))
+    grad_ffn = at.all_narrow(after((valid * cotan).astype(bf16), *tokens_far))
     half = slot // 2
     norm_one, packed, wqkv, wout = qkv_of(where, small, xhats, pieces, width)
-    wouts = at.all_narrow(wout)
+    wout_far = at.swap(wout, 2)
     tiles = bias_tiles(n, small, buckets, heads)
     atts, probs = [None] * 4, [None] * 4
     for r in (3, 2, 1, 0):
-        length = after(lengths_all[r], *grad_ffn[1:]) if r == 0 else lengths_all[r]
+        length = {2: [grad_ffn[2]], 0: grad_ffn[1:]}.get(r, [])
+        length = after(lengths_all[r], *length) if length else lengths_all[r]
         atts[r], probs[r] = attn_fwd(length, packed, tiles, r)
+    wouts = [wout, at.swap(wout, 1), wout_far, at.swap(after(wout_far, atts[1]), 1)]
     attended = [atts[0]] + [at.swap(atts[r], r) for r in (1, 2, 3)]
     whole, norm_two, norm_far = [], [], []
     for i in range(2):
@@ -1164,13 +1166,13 @@
     p_back = [at.swap(p_far[:half], 2)]
     grad_packed, dist = backward(1, p_far)
     dists.append(dist)
-    grad_qkv = dot(norm_one, after(grad_packed, p_back[0]), TN).astype(bf16)
+    grad_qkv = dot(norm_one, grad_packed, TN).astype(bf16)
     parts = [grad_qkv.reshape(wide, rows, width), out_sum.reshape(wide, rows, model // 2)]
     if at.rings:
         next(turns)
         ffn_own = turns.send([dist])
         turns = reduce_ring(at, parts)
-        grad_packed = after(grad_packed, *next(turns))
+        grad_packed = after(grad_packed, p_back[0], *next(turns))
     else:
         ffn_own = scatter(at, [gu.reshape(shape), gd.reshape(shape)])
         attn_own = scatter(at, parts)
@@ -1181,21 +1183,20 @@
     p0, p1, grad_one = ln1_back(grad_packed, wqkv, xhats[:2], 0)
     grad_one = [grad_one, more_one]
     p_near = at.swap(p1, 1)
-    up_full, down_full = join_ffn(n, ffn_all, quarter)
     if at.rings:
         keep, send = pack_small(n, at.y.reshape(1), grad_one, grad_two, backwards, dists, heads)
         next(turns)
         sent = turns.send([p1, keep, ffn_all[2]])
         smalls = keep + at.swap_y(after(send, *sent))
         next(turns)
-        sent = turns.send([p_back[1], up_full])
+        sent = turns.send([p_back[1]])
         p0 = after(p0, *sent)
     grad_tokens = ln1_last(tokens, xhats[0], grad_middle, small, p0, p_near, *p_back)
 
     outs = [o0, at.swap(o1, 1), jnp.concatenate(out_back, axis=0)]
     if at.rings:
         next(turns)
-        sent = turns.send([grad_tokens, out_back[1], smalls])
+        sent = turns.send([grad_tokens, smalls])
         smalls, outs[0] = after(smalls, *sent), after(o0, *sent)
         pick = lambda i: lax.dynamic_index_in_dim(smalls, i, 0, keepdims=False)
         z_parts = [pick(at.z)] + [
@@ -1223,6 +1224,8 @@
     smalls = smalls + at.swap(smalls, 2)
     smalls = smalls + at.swap(smalls, 1)
 
+    ffn_all[0] = after(ffn_all[0], attn_own)
+    up_full, down_full = join_ffn(n, ffn_all, quarter)
     qkv_full, out_full = join_attn(n, at.all_narrow(attn_own), model)
 
     return (

time: 362 us -> 363 us (level)
    ppermute x64, waiting for transfers between devices: 40.4 us -> 29.1 us  [swap(): return lax.ppermute(x, 'narrow', [(i, i ^ bit) for i in range(self.narrow)])]
    ppermute x1, waiting for transfers between devices: 0.01 us -> 5.85 us  [swap_y(): return lax.ppermute(x, 'wide', [(i, i ^ 1) for i in range(self.wide)])]
    unnamed x156 -> x150, local copies, waits for them, and re-layouts: 9.59 us -> 11 us
  transfers between devices with their start and end apart: 90 -> 90, of which waited for: 34 -> 33; matrix products, arithmetic and copies ran while one was open for 13% -> 14% of each run, Pallas kernels for 40% -> 40%
where the time goes in v2:
time: 363 us; the launch traced here: 357 us
  Pallas kernels  153 us (42%)
  waiting for transfers between devices  71.7 us (20%)
  starting transfers between devices  57.3 us (16%)
  matrix products  22.3 us (6%)
  local copies, waits for them, and re-layouts  21 us (6%)
  other arithmetic  16 us (4%)
  between operations  15.7 us (4%)
    pallas_call x3, Pallas kernels, ffn(): pl.pallas_call(functools.partial(ffn_kernel, len(norms), places, start, c...  37.6 us
    ppermute x64, starting transfers between devices, swap(): return lax.ppermute(x, 'narrow', [(i, i ^ bit) for i in range(self.narrow)])  31.2 us
    ppermute x64, waiting for transfers between devices, swap(): return lax.ppermute(x, 'narrow', [(i, i ^ bit) for i in range(self.narrow)])  29.1 us
    ppermute x21, waiting for transfers between devices, ring(): return lax.ppermute(x, ('narrow', 'wide'), pairs)  29.1 us
    dot_general x5, matrix products, dot(): return lax.dot_general(a, b, (dims, ((), ())), preferred_element_type=f32)  22.3 us
    ppermute x21, starting transfers between devices, ring(): return lax.ppermute(x, ('narrow', 'wide'), pairs)  21.5 us
    pallas_call x4, Pallas kernels, attn_bwd(): pl.pallas_call(attn_bwd_kernel, grid=(steps,), in_specs=[pl.BlockSpec((sl...  18.8 us
    pallas_call x4, Pallas kernels, attn_fwd(): pl.pallas_call(attn_fwd_kernel, grid=(heads // 2,), in_specs=[pl.BlockSpe...  17.1 us
  transfers between devices with their start and end apart: 90, of which 33 were waited for; matrix products, arithmetic and copies ran while one was open for 14% of the time, Pallas kernels for 40%

profile of v2, /device:TPU:0, one launch (start us, length us, event | category | flops | bytes accessed | tf_op | source)
XLA Modules:
  0.0 357.4 jit_solution(1061795852258435589)
XLA Ops:
  19.8 5.3 %collective-permute-done.refs_2_.refs_6_ = bf16[128,1152]{1,0:T(8,128)(2,1)S(1)} collective-permute-done((bf16[128,1152]{1,0:T(8,128)(2,1)}, bf16[128,1152]{1,0:T(8,128)(2,1)S(1)}, u32[]{:S(2)}, u32[]{:S(2)}) %collective-permute-start) | collective-permute-done | bytes 294944 | tf_op jit(solution)/shard_map/ppermute | solution.py:898
  27.3 6.7 %collective-permute-done.3.refs_4_.refs_8_ = bf16[128,1152]{1,0:T(8,128)(2,1)S(1)} collective-permute-done((bf16[128,1152]{1,0:T(8,128)(2,1)S(1)}, bf16[128,1152]{1,0:T(8,128)(2,1)S(1)}, u32[]{:S(2)}, u32[]{:S(2)}) %collective-permute-start.3) | collective-permute-done | bytes 294944 | tf_op jit(solution)/shard_map/ppermute | solution.py:898
  34.7 3.3 xhat.4.refs_0_.x0_ref.xhat_ref
  44.2 7.1 %collective-permute-done.8.refs_6_.refs_10_ = bf16[128,1152]{1,0:T(8,128)(2,1)S(1)} collective-permute-done((bf16[128,1152]{1,0:T(8,128)(2,1)S(1)}, bf16[128,1152]{1,0:T(8,128)(2,1)S(1)}, u32[]{:S(2)}, u32[]{:S(2)}) %collective-permute-start.8) | collective-permute-done | bytes 294944 | tf_op jit(solution)/shard_map/ppermute | solution.py:898
  59.9 3.2 xhat.7.refs_3_.x1_ref
  67.8 11.1 %qkv.1 = (bf16[2048,1024]{1,0:T(8,128)(2,1)}, bf16[2048,768]{1,0:T(8,128)(2,1)}, bf16[1024,768]{1,0:T(8,128)(2,1)}, bf16[1024,256]{1,0:T(8,128)(2,1)}) custom-call(s32[8]{0:T(128)} %stack.53.where_ref, f32[8,1024]{1,0:T(8,128)} %small_rows.1.small_ref, f32[512,1024]{1,0:T(8,128)} %xhat.4.refs_0_.x0_ref.xhat_ref, f32[512,1024]{1,0:T(8,128)} %xhat.5.refs_1_.x1_ref, ...), custom_call_target="tpu_custom_call" | custom-call | flops 402500000 | tf_op jit(solution)/shard_map/qkv/pallas_call | solution.py:246
  83.2 4.4 %attn_fwd.7 = (bf16[512,256]{1,0:T(8,128)(2,1)}, bf16[4,512,512]{2,1,0:T(8,128)(2,1)}) custom-call(s32[1]{0:T(128)} %collective-permute-done.11.len_ref, bf16[2048,768]{1,0:T(8,128)(2,1)} %get-tuple-element.172.qkv_ref, f32[4,4,128,128]{3,2,1,0:T(8,128)} %bias_tiles.1.tiles_ref), custom_call_target="tpu_custom_call" | custom-call | flops 517500000 | tf_op jit(solution)/shard_map/attn_fwd/pallas_call | solution.py:346
  88.0 4.4 %attn_fwd.5 = (bf16[512,256]{1,0:T(8,128)(2,1)}, bf16[4,512,512]{2,1,0:T(8,128)(2,1)}) custom-call(s32[1]{0:T(128)} %collective-permute-done.10.len_ref, bf16[2048,768]{1,0:T(8,128)(2,1)} %get-tuple-element.172.qkv_ref, f32[4,4,128,128]{3,2,1,0:T(8,128)} %bias_tiles.1.tiles_ref), custom_call_target="tpu_custom_call" | custom-call | flops 517500000 | tf_op jit(solution)/shard_map/attn_fwd/pallas_call | solution.py:346
  94.0 4.5 %attn_fwd.6 = (bf16[512,256]{1,0:T(8,128)(2,1)}, bf16[4,512,512]{2,1,0:T(8,128)(2,1)}) custom-call(s32[1]{0:T(128)} %collective-permute-done.5.len_ref, bf16[2048,768]{1,0:T(8,128)(2,1)} %get-tuple-element.172.qkv_ref, f32[4,4,128,128]{3,2,1,0:T(8,128)} %bias_tiles.1.tiles_ref), custom_call_target="tpu_custom_call" | custom-call | flops 517500000 | tf_op jit(solution)/shard_map/attn_fwd/pallas_call | solution.py:346
  100.3 7.1 %collective-permute-done.19.refs_2_ = bf16[512,256]{1,0:T(8,128)(2,1)S(1)} collective-permute-done((bf16[512,256]{1,0:T(8,128)(2,1)}, bf16[512,256]{1,0:T(8,128)(2,1)S(1)}, u32[]{:S(2)}, u32[]{:S(2)}) %collective-permute-start.19) | collective-permute-done | bytes 262176 | tf_op jit(solution)/shard_map/ppermute | solution.py:904
  107.4 3.9 %attn_fwd.4 = (bf16[512,256]{1,0:T(8,128)(2,1)}, bf16[4,512,512]{2,1,0:T(8,128)(2,1)}) custom-call(s32[1]{0:T(128)} %copy.64.len_ref, bf16[2048,768]{1,0:T(8,128)(2,1)} %get-tuple-element.172.qkv_ref, f32[4,4,128,128]{3,2,1,0:T(8,128)} %bias_tiles.1.tiles_ref), custom_call_target="tpu_custom_call" | custom-call | flops 517500000 | tf_op jit(solution)/shard_map/attn_fwd/pallas_call | solution.py:346
  112.2 3.9 %out_ln2.2 = (f32[512,1024]{1,0:T(8,128)}, bf16[512,1024]{1,0:T(8,128)(2,1)}, bf16[256,1024]{1,0:T(8,128)(2,1)}) custom-call(s32[1]{0:T(128)} %bitcast.n_ref, s32[1]{0:T(128)} %copy.64.len_ref, bf16[512,1024]{1,0:T(8,128)(2,1)} %tok_ref.5, f32[8,1024]{1,0:T(8,128)} %small_rows.1.small_ref, bf16[512,256]{1,0:T(8,128)(2,1)} %get-tuple-element.173.refs_0_.att_ref, ...), custom_call_target="tpu_custom_call" | custom-call | flops 71875000 | tf_op jit(solution)/shard_map/out_ln2/pallas_call | solution.py:510
  116.1 3.9 %out_ln2.3 = (f32[512,1024]{1,0:T(8,128)}, bf16[512,1024]{1,0:T(8,128)(2,1)}, bf16[256,1024]{1,0:T(8,128)(2,1)}) custom-call(s32[1]{0:T(128)} %bitcast.n_ref, s32[1]{0:T(128)} %copy.64.len_ref, bf16[512,1024]{1,0:T(8,128)(2,1)} %tok_ref.5, f32[8,1024]{1,0:T(8,128)} %small_rows.1.small_ref, ...), custom_call_target="tpu_custom_call", output_to_operand_aliasing={{0}: (12, {}), {1}: (13, {})} | custom-call | flops 71875000 | tf_op jit(solution)/shard_map/out_ln2/pallas_call | solution.py:510
  125.5 16.6 %ffn.3 = (f32[512,1024]{1,0:T(8,128)}, f32[512,1024]{1,0:T(8,128)}, bf16[512,1024]{1,0:T(8,128)(2,1)}, bf16[128,1024]{1,0:T(8,128)(2,1)}, bf16[128,1024]{1,0:T(8...) custom-call(bf16[8,2,128,1024]{3,2,1,0:T(8,128)(2,1)} %bitcast.118, ...), custom_call_target="tpu_custom_call" | custom-call | flops 215624992 | tf_op jit(solution)/shard_map/ffn/pallas_call | solution.py:701
  146.0 10.5 %ffn.4 = (f32[256,1024]{1,0:T(8,128)}, f32[256,1024]{1,0:T(8,128)}, bf16[256,1024]{1,0:T(8,128)(2,1)}, bf16[64,1024]{1,0:T(8,128)(2,1)}, bf16[64,1024]{1,0:T(8,1...) custom-call(bf16[8,2,128,1024]{3,2,1,0:T(8,128)(2,1)} %bitcast.119, ...), custom_call_target="tpu_custom_call", output_to_operand_aliasing={{7}: (8, {}), {8}: (9, {}), {9}: (10, {}), {10}: (11, {})} | custom-call | flops 143750000 | tf_op jit(solution)/shard_map/ffn/pallas_call | solution.py:701
  162.8 10.5 %ffn.5 = (f32[256,1024]{1,0:T(8,128)}, f32[256,1024]{1,0:T(8,128)}, bf16[256,1024]{1,0:T(8,128)(2,1)}, bf16[64,1024]{1,0:T(8,128)(2,1)}, bf16[64,1024]{1,0:T(8,1...) custom-call(bf16[8,2,128,1024]{3,2,1,0:T(8,128)(2,1)} %bitcast.120, ...), custom_call_target="tpu_custom_call", output_to_operand_aliasing={{7}: (8, {}), {8}: (9, {}), {9}: (10, {}), {10}: (11, {})} | custom-call | flops 143750000 | tf_op jit(solution)/shard_map/ffn/pallas_call | solution.py:701
  177.9 8.2 %convolution_convert_fusion.1 = bf16[1024,1024]{1,0:T(8,128)(2,1)S(1)} fusion(bf16[2048,1024]{1,0:T(8,128)(2,1)} %get-tuple-element.225, bf16[2048,1024]{1,0:T(8,128)(2,1)} %get-tuple-element.227), kind=kOutput, calls=%fused_computation.5 | convolution fusion | flops 4296015872 | bytes 10485760 | tf_op jit(solution)/shard_map/dot_general | solution.py:32
  186.2 5.0 %convolution_convert_fusion = bf16[1024,1024]{1,0:T(8,128)(2,1)S(1)} fusion(bf16[2048,1024]{1,0:T(8,128)(2,1)S(1)} %copy-done.2, bf16[2048,1024]{1,0:T(8,128)(2,1)S(1)} %copy-done.1), kind=kOutput, calls=%fused_computation.4 | convolution fusion | flops 4296015872 | bytes 10485760 | tf_op jit(solution)/shard_map/dot_general | solution.py:32
  194.9 5.0 %ln2_back.2 = (f32[512,1024]{1,0:T(8,128)}, bf16[512,512]{1,0:T(8,128)(2,1)}, bf16[512,512]{1,0:T(8,128)(2,1)}, bf16[512,256]{1,0:T(8,128)(2,1)}, bf16[512,256]{...) custom-call(s32[1]{0:T(128)} %bitcast.n_ref, s32[1]{0:T(128)} %copy.64.len_ref, ...), custom_call_target="tpu_custom_call" | custom-call | flops 5750000128 | tf_op jit(solution)/shard_map/ln2_back/pallas_call | solution.py:569
  201.0 5.2 %ln2_back.3 = (f32[512,1024]{1,0:T(8,128)}, bf16[512,512]{1,0:T(8,128)(2,1)}, bf16[512,512]{1,0:T(8,128)(2,1)}, bf16[512,256]{1,0:T(8,128)(2,1)}, bf16[512,256]{...) custom-call(s32[1]{0:T(128)} %bitcast.n_ref, ...), custom_call_target="tpu_custom_call", output_to_operand_aliasing={{0}: (13, {}), {1}: (14, {}), {2}: (15, {}), {3}: (16, {}),... | custom-call | flops 5750000128 | tf_op jit(solution)/shard_map/ln2_back/pallas_call | solution.py:569
  210.1 4.7 %attn_bwd.4 = (bf16[2048,768]{1,0:T(8,128)(2,1)}, f32[2,2,512]{2,1,0:T(2,128)}) custom-call(bf16[2048,768]{1,0:T(8,128)(2,1)} %get-tuple-element.172.qkv_ref, bf16[512,256]{1,0:T(8,128)(2,1)} %get-tuple-element.233.ga_ref, bf16[512,256]{1,0:T(8,128)(2,1)} %get-tuple-element.173.refs_0_.att_ref, bf16[4,512,512]{2,1,0:T(8,128)(2,1)} %get-tuple-element.234.p_ref), custom_call_target="tpu_custom_call" | custom-call | flops 1150000000 | tf_op jit(solution)/shard_map/attn_bwd/pallas_call | solution.py:431
  227.2 5.0 %attn_bwd.5 = (bf16[2048,768]{1,0:T(8,128)(2,1)}, f32[2,2,512]{2,1,0:T(2,128)}) custom-call(bf16[2048,768]{1,0:T(8,128)(2,1)} %get-tuple-element.172.qkv_ref, bf16[512,256]{1,0:T(8,128)(2,1)} %copy-done.47, bf16[512,256]{1,0:T(8,128)(2,1)} %get-tuple-element.176.att_ref, ...), custom_call_target="tpu_custom_call", output_to_operand_aliasing={{0}: (4, {})} | custom-call | flops 1150000000 | tf_op jit(solution)/shard_map/attn_bwd/pallas_call | solution.py:431
  232.5 4.6 %attn_bwd.6 = (bf16[2048,768]{1,0:T(8,128)(2,1)}, f32[2,2,512]{2,1,0:T(2,128)}) custom-call(bf16[2048,768]{1,0:T(8,128)(2,1)} %get-tuple-element.172.qkv_ref, bf16[512,256]{1,0:T(8,128)(2,1)} %copy-done.46, bf16[512,256]{1,0:T(8,128)(2,1)} %get-tuple-element.177.att_ref, ...), custom_call_target="tpu_custom_call", output_to_operand_aliasing={{0}: (4, {})} | custom-call | flops 1150000000 | tf_op jit(solution)/shard_map/attn_bwd/pallas_call | solution.py:431
  238.4 7.3 %ln1_back.2 = (bf16[512,1024]{1,0:T(8,128)(2,1)}, bf16[512,1024]{1,0:T(8,128)(2,1)}, f32[2,1024]{1,0:T(2,128)}) custom-call(bf16[2048,768]{1,0:T(8,128)(2,1)} %get-tuple-element.253.gp_ref.refs_0_, bf16[1024,768]{1,0:T(8,128)(2,1)} %get-tuple-element.254.wq_ref, f32[512,1024]{1,0:T(8,128)} %xhat.6.refs_2_.x0_ref, f32[512,1024]{1,0:T(8,128)} %xhat.7.refs_3_.x1_ref), custom_call_target="tpu_custom_call" | custom-call | flops 575000000 | tf_op jit(solution)/shard_map/ln1_back/pallas_call | solution.py:291
  250.0 4.6 %attn_bwd.7 = (bf16[2048,768]{1,0:T(8,128)(2,1)}, f32[2,2,512]{2,1,0:T(2,128)}) custom-call(bf16[2048,768]{1,0:T(8,128)(2,1)} %get-tuple-element.172.qkv_ref, bf16[512,256]{1,0:T(8,128)(2,1)} %copy-done.48, bf16[512,256]{1,0:T(8,128)(2,1)} %get-tuple-element.174.att_ref, ...), custom_call_target="tpu_custom_call", output_to_operand_aliasing={{0}: (4, {})} | custom-call | flops 1150000000 | tf_op jit(solution)/shard_map/attn_bwd/pallas_call | solution.py:431
  258.5 6.7 %convolution_convert_fusion.2 = bf16[1024,768]{1,0:T(8,128)(2,1)S(1)} fusion(bf16[2048,1024]{1,0:T(8,128)(2,1)} %get-tuple-element.187, bf16[2048,768]{1,0:T(8,128)(2,1)} %get-tuple-element.260.gp_ref), kind=kOutput, calls=%fused_computation.6 | convolution fusion | flops 3222011904 | bytes 8912896 | tf_op jit(solution)/shard_map/dot_general | solution.py:32
  272.0 7.8 %ln1_back.3 = (f32[512,1024]{1,0:T(8,128)}, bf16[512,1024]{1,0:T(8,128)(2,1)}, f32[2,1024]{1,0:T(2,128)}) custom-call(bf16[2048,768]{1,0:T(8,128)(2,1)} %get-tuple-element.260.gp_ref, bf16[1024,768]{1,0:T(8,128)(2,1)} %get-tuple-element.254.wq_ref, f32[512,1024]{1,0:T(8,128)} %xhat.4.refs_0_.x0_ref.xhat_ref, f32[512,1024]{1,0:T(8,128)} %xhat.5.refs_1_.x1_ref), custom_call_target="tpu_custom_call" | custom-call | flops 5750000128 | tf_op jit(solution)/shard_map/ln1_back/pallas_call | solution.py:291
  289.4 5.4 %collective-permute-done.69 = bf16[128,1280]{1,0:T(8,128)(2,1)S(1)} collective-permute-done((bf16[128,1280]{1,0:T(8,128)(2,1)S(1)}, bf16[128,1280]{1,0:T(8,128)(2,1)S(1)}, u32[]{:S(2)}, u32[]{:S(2)}) %collective-permute-start.69) | collective-permute-done | bytes 327712 | tf_op jit(solution)/shard_map/ppermute | solution.py:898
  301.5 5.9 %collective-permute-done.74 = f32[4,8,128]{2,1,0:T(8,128)S(1)} collective-permute-done((f32[4,8,128]{2,1,0:T(8,128)S(1)}, f32[4,8,128]{2,1,0:T(8,128)S(1)}, u32[]{:S(2)}, u32[]{:S(2)}) %collective-permute-start.74) | collective-permute-done | bytes 16416 | tf_op jit(solution)/shard_map/ppermute | solution.py:911
  309.6 5.8 %ln1_last.1 = f32[512,1024]{1,0:T(8,128)} custom-call(bf16[512,1024]{1,0:T(8,128)(2,1)} %tok_ref.5, f32[512,1024]{1,0:T(8,128)} %xhat.4.refs_0_.x0_ref.xhat_ref, f32[512,1024]{1,0:T(8,128)} %get-tuple-element.279.gmid_ref, f32[8,1024]{1,0:T(8,128)} %small_rows.1.small_ref, f32[512,1024]{1,0:T(8,128)} %get-tuple-element.281.p0_ref, ...), custom_call_target="tpu_custom_call" | custom-call | flops 287500000 | tf_op jit(solution)/shard_map/ln1_last/pallas_call | solution.py:472
  316.7 3.9 %collective-permute-done.77 = bf16[256,1024]{1,0:T(8,128)(2,1)} collective-permute-done((bf16[256,1024]{1,0:T(8,128)(2,1)}, bf16[256,1024]{1,0:T(8,128)(2,1)}, u32[]{:S(2)}, u32[]{:S(2)}) %collective-permute-start.77) | collective-permute-done | bytes 524320 | tf_op jit(solution)/shard_map/ppermute | solution.py:904
  340.6 3.9 %join_ffn.1 = (f32[128,4096]{1,0:T(8,128)}, f32[512,1024]{1,0:T(8,128)}) custom-call(s32[1]{0:T(128)} %bitcast.n_ref, bf16[128,2048]{1,0:T(8,128)(2,1)} %copy-done.8, bf16[128,2048]{1,0:T(8,128)(2,1)} %copy-done.28, bf16[128,2048]{1,0:T(8,128)(2,1)} %copy-done.25, bf16[128,2048]{1,0:T(8,128)(2,1)} %copy-done.29), custom_call_target="tpu_custom_call" | custom-call | flops 230000000 | tf_op jit(solution)/shard_map/join_ffn/pallas_call | solution.py:820
  (379 shorter events, 146.6 us)
Async XLA Ops:
  7.2 118.4 %all-gather.3.cloned.1.call-start = ((), (), s32[]{:S(2)}) async-start(), calls=%async_computation | async-start | bytes 4718592 | tf_op jit(solution)/shard_map/all_gather | solution.py:1070
  7.2 30.7 %collective-permute-start.7 = (bf16[512,1024]{1,0:T(8,128)(2,1)}, bf16[512,1024]{1,0:T(8,128)(2,1)S(1)}, u32[]{:S(2)}, u32[]{:S(2)}) collective-permute-start(bf16[512,1024]{1,0:T(8,128)(2,1)} %tok_ref.5), channel_id=1, source_target_pairs={{0,8},{8,0},{16,24},{24,16},{1,9},{9,1},{17,25},{25,17},{2,10},{10... | collective-permute-start | bytes 3145736 | tf_op jit(solution)/shard_map/ppermute | solution.py:904
  8.8 16.4 %collective-permute-start.2 = (bf16[224,1024]{1,0:T(8,128)(2,1)S(1)}, bf16[224,1024]{1,0:T(8,128)(2,1)}, u32[]{:S(2)}, u32[]{:S(2)}) collective-permute-start(bf16[224,1024]{1,0:T(8,128)(2,1)S(1)} %slice.51), channel_id=1, source_target_pairs={{0,16},{8,24},{16,0},{24,8},{1,17},{9,25},{17,1},{25,9},{2,18},{10... | collective-permute-start | bytes 1376264 | tf_op jit(solution)/shard_map/ppermute | solution.py:904
  17.5 24.6 %collective-permute-start.6 = (bf16[288,1024]{1,0:T(8,128)(2,1)S(1)}, bf16[288,1024]{1,0:T(8,128)(2,1)}, u32[]{:S(2)}, u32[]{:S(2)}) collective-permute-start(bf16[288,1024]{1,0:T(8,128)(2,1)S(1)} %slice.52), channel_id=1, source_target_pairs={{0,16},{8,24},{16,0},{24,8},{1,17},{9,25},{17,1},{25,9},{2,18},{10... | collective-permute-start | bytes 1769480 | tf_op jit(solution)/shard_map/ppermute | solution.py:904
  27.2 14.9 %collective-permute-start.5 = (s32[1]{0:T(128)}, s32[1]{0:T(128)}, u32[]{:S(2)}, u32[]{:S(2)}) collective-permute-start(s32[1]{0:T(128)} %param.14), channel_id=1, source_target_pairs={{0,16},{8,24},{16,0},{24,8},{1,17},{9,25},{17,1},{25,9},{2,18},{10... | collective-permute-start | bytes 20 | tf_op jit(solution)/shard_map/ppermute | solution.py:904
  53.9 34.0 %collective-permute-start.14 = (bf16[512,1024]{1,0:T(8,128)(2,1)S(1)}, bf16[512,1024]{1,0:T(8,128)(2,1)S(1)}, u32[]{:S(2)}, u32[]{:S(2)}) collective-permute-start(bf16[512,1024]{1,0:T(8,128)(2,1)S(1)} %multiply_convert_fusion.refs_4_), channel_id=1, source_target_pairs={{0,16},{8,24},{16,0},{24,8},{1,17},{9,25},{17,1},{25,9},{2,18},{10... | collective-permute-start | bytes 3145736 | tf_op jit(solution)/shard_map/ppermute | solution.py:904
  58.4 63.7 %collective-permute-start.13 = (bf16[512,1024]{1,0:T(8,128)(2,1)S(1)}, bf16[512,1024]{1,0:T(8,128)(2,1)}, u32[]{:S(2)}, u32[]{:S(2)}) collective-permute-start(bf16[512,1024]{1,0:T(8,128)(2,1)S(1)} %multiply_convert_fusion.refs_4_), channel_id=1, source_target_pairs={{0,8},{8,0},{16,24},{24,16},{1,9},{9,1},{17,25},{25,17},{2,10},{10... | collective-permute-start | bytes 3145736 | tf_op jit(solution)/shard_map/ppermute | solution.py:904
  78.9 15.1 %collective-permute-start.22 = (bf16[1024,256]{1,0:T(8,128)(2,1)}, bf16[1024,256]{1,0:T(8,128)(2,1)}, u32[]{:S(2)}, u32[]{:S(2)}) collective-permute-start(bf16[1024,256]{1,0:T(8,128)(2,1)} %get-tuple-element.178.refs_4_.refs_2_), channel_id=1, source_target_pairs={{0,16},{8,24},{16,0},{24,8},{1,17},{9,25},{17,1},{25,9},{2,18},{10... | collective-permute-start | bytes 1572872 | tf_op jit(solution)/shard_map/ppermute | solution.py:904
  80.5 30.8 %collective-permute-start.21 = (bf16[1024,256]{1,0:T(8,128)(2,1)}, bf16[1024,256]{1,0:T(8,128)(2,1)}, u32[]{:S(2)}, u32[]{:S(2)}) collective-permute-start(bf16[1024,256]{1,0:T(8,128)(2,1)} %get-tuple-element.178.refs_4_.refs_2_), channel_id=1, source_target_pairs={{0,8},{8,0},{16,24},{24,16},{1,9},{9,1},{17,25},{25,17},{2,10},{10... | collective-permute-start | bytes 1572872 | tf_op jit(solution)/shard_map/ppermute | solution.py:904
  94.0 17.3 %collective-permute-start.23 = (bf16[1024,256]{1,0:T(8,128)(2,1)}, bf16[1024,256]{1,0:T(8,128)(2,1)S(1)}, u32[]{:S(2)}, u32[]{:S(2)}) collective-permute-start(bf16[1024,256]{1,0:T(8,128)(2,1)} %collective-permute-done.22.refs_6_.refs_4_), channel_id=1, source_target_pairs={{0,8},{8,0},{16,24},{24,16},{1,9},{9,1},{17,25},{25,17},{2,10},{10... | collective-permute-start | bytes 1572872 | tf_op jit(solution)/shard_map/ppermute | solution.py:904
  107.4 36.6 %collective-permute-start.15 = (bf16[512,1024]{1,0:T(8,128)(2,1)S(1)}, bf16[512,1024]{1,0:T(8,128)(2,1)S(1)}, u32[]{:S(2)}, u32[]{:S(2)}) collective-permute-start(bf16[512,1024]{1,0:T(8,128)(2,1)S(1)} %collective-permute-done.14.refs_5_), channel_id=1, source_target_pairs={{0,8},{8,0},{16,24},{24,16},{1,9},{9,1},{17,25},{25,17},{2,10},{10... | collective-permute-start | bytes 3145736 | tf_op jit(solution)/shard_map/ppermute | solution.py:904
  120.5 21.6 %collective-permute-start.27 = (bf16[256,1024]{1,0:T(8,128)(2,1)}, bf16[256,1024]{1,0:T(8,128)(2,1)}, u32[]{:S(2)}, u32[]{:S(2)}) collective-permute-start(bf16[256,1024]{1,0:T(8,128)(2,1)} %get-tuple-element.184.refs_0_), channel_id=1, source_target_pairs={{0,16},{8,24},{16,0},{24,8},{1,17},{9,25},{17,1},{25,9},{2,18},{10... | collective-permute-start | bytes 1572872 | tf_op jit(solution)/shard_map/ppermute | solution.py:904
  122.1 35.6 %collective-permute-start.26 = (bf16[256,1024]{1,0:T(8,128)(2,1)}, bf16[256,1024]{1,0:T(8,128)(2,1)S(1)}, u32[]{:S(2)}, u32[]{:S(2)}) collective-permute-start(bf16[256,1024]{1,0:T(8,128)(2,1)} %get-tuple-element.185.refs_1_), channel_id=1, source_target_pairs={{0,16},{8,24},{16,0},{24,8},{1,17},{9,25},{17,1},{25,9},{2,18},{10... | collective-permute-start | bytes 1572872 | tf_op jit(solution)/shard_map/ppermute | solution.py:904
  160.4 16.9 %collective-permute-start.47 = (bf16[256,1024]{1,0:T(8,128)(2,1)S(1)}, bf16[256,1024]{1,0:T(8,128)(2,1)S(1)}, u32[]{:S(2)}, u32[]{:S(2)}) collective-permute-start(bf16[256,1024]{1,0:T(8,128)(2,1)S(1)} %add_convert_fusion.12), channel_id=1, source_target_pairs={{0,16},{8,24},{16,0},{24,8},{1,17},{9,25},{17,1},{25,9},{2,18},{10... | collective-permute-start | bytes 1572872 | tf_op jit(solution)/shard_map/ppermute | solution.py:904
  174.9 18.0 %collective-permute-start.48 = (bf16[128,1024]{1,0:T(8,128)(2,1)S(1)}, bf16[128,1024]{1,0:T(8,128)(2,1)S(1)}, u32[]{:S(2)}, u32[]{:S(2)}) collective-permute-start(bf16[128,1024]{1,0:T(8,128)(2,1)S(1)} %copy-done.67), channel_id=1, source_target_pairs={{0,8},{8,0},{16,24},{24,16},{1,9},{9,1},{17,25},{25,17},{2,10},{10... | collective-permute-start | bytes 786440 | tf_op jit(solution)/shard_map/ppermute | solution.py:904
  175.1 18.4 %collective-permute-start.49 = (bf16[128,1024]{1,0:T(8,128)(2,1)S(1)}, bf16[128,1024]{1,0:T(8,128)(2,1)S(1)}, u32[]{:S(2)}, u32[]{:S(2)}) collective-permute-start(bf16[128,1024]{1,0:T(8,128)(2,1)S(1)} %copy-done.66), channel_id=1, source_target_pairs={{0,8},{8,0},{16,24},{24,16},{1,9},{9,1},{17,25},{25,17},{2,10},{10... | collective-permute-start | bytes 786440 | tf_op jit(solution)/shard_map/ppermute | solution.py:904
  175.4 24.6 %collective-permute-start.45 = (bf16[128,1024]{1,0:T(8,128)(2,1)S(1)}, bf16[128,1024]{1,0:T(8,128)(2,1)S(1)}, u32[]{:S(2)}, u32[]{:S(2)}) collective-permute-start(bf16[128,1024]{1,0:T(8,128)(2,1)S(1)} %copy-done.65), channel_id=1, source_target_pairs={{0,8},{8,0},{16,24},{24,16},{1,9},{9,1},{17,25},{25,17},{2,10},{10... | collective-permute-start | bytes 786440 | tf_op jit(solution)/shard_map/ppermute | solution.py:904
  175.6 24.4 %collective-permute-start.46 = (bf16[128,1024]{1,0:T(8,128)(2,1)S(1)}, bf16[128,1024]{1,0:T(8,128)(2,1)S(1)}, u32[]{:S(2)}, u32[]{:S(2)}) collective-permute-start(bf16[128,1024]{1,0:T(8,128)(2,1)S(1)} %copy-done.64), channel_id=1, source_target_pairs={{0,8},{8,0},{16,24},{24,16},{1,9},{9,1},{17,25},{25,17},{2,10},{10... | collective-permute-start | bytes 786440 | tf_op jit(solution)/shard_map/ppermute | solution.py:904
  177.3 22.7 %collective-permute-start.44 = (bf16[256,1024]{1,0:T(8,128)(2,1)S(1)}, bf16[256,1024]{1,0:T(8,128)(2,1)S(1)}, u32[]{:S(2)}, u32[]{:S(2)}) collective-permute-start(bf16[256,1024]{1,0:T(8,128)(2,1)S(1)} %add_convert_fusion.11), channel_id=1, source_target_pairs={{0,16},{8,24},{16,0},{24,8},{1,17},{9,25},{17,1},{25,9},{2,18},{10... | collective-permute-start | bytes 1572872 | tf_op jit(solution)/shard_map/ppermute | solution.py:904
  192.8 14.8 %collective-permute-start.53 = (bf16[128,2048]{1,0:T(8,128)(2,1)S(1)}, bf16[128,2048]{1,0:T(8,128)(2,1)S(1)}, u32[]{:S(2)}, u32[]{:S(2)}) collective-permute-start(bf16[128,2048]{1,0:T(8,128)(2,1)S(1)} %pad_maximum_fusion.1), channel_id=1, source_target_pairs={{2,0},{4,2},{6,4},{7,6},{5,7},{3,5},{1,3},{0,1},{9,8},{8,10},{10,1... | collective-permute-start | bytes 1572872 | tf_op jit(solution)/shard_map/ppermute | solution.py:898
  193.4 14.2 %collective-permute-start.52 = (bf16[128,2048]{1,0:T(8,128)(2,1)S(1)}, bf16[128,2048]{1,0:T(8,128)(2,1)S(1)}, u32[]{:S(2)}, u32[]{:S(2)}) collective-permute-start(bf16[128,2048]{1,0:T(8,128)(2,1)S(1)} %pad_maximum_fusion), channel_id=1, source_target_pairs={{0,2},{2,4},{4,6},{6,7},{7,5},{5,3},{3,1},{1,0},{8,9},{10,8},{12,1... | collective-permute-start | bytes 1572872 | tf_op jit(solution)/shard_map/ppermute | solution.py:898
  207.8 14.5 %collective-permute-start.57 = (bf16[128,2048]{1,0:T(8,128)(2,1)S(1)}, bf16[128,2048]{1,0:T(8,128)(2,1)S(1)}, u32[]{:S(2)}, u32[]{:S(2)}) collective-permute-start(bf16[128,2048]{1,0:T(8,128)(2,1)S(1)} %add_convert_fusion.9), channel_id=1, source_target_pairs={{2,0},{4,2},{6,4},{7,6},{5,7},{3,5},{1,3},{0,1},{9,8},{8,10},{10,1... | collective-permute-start | bytes 1572872 | tf_op jit(solution)/shard_map/ppermute | solution.py:898
  222.5 14.8 %collective-permute-start.61 = (bf16[128,2048]{1,0:T(8,128)(2,1)S(1)}, bf16[128,2048]{1,0:T(8,128)(2,1)S(1)}, u32[]{:S(2)}, u32[]{:S(2)}) collective-permute-start(bf16[128,2048]{1,0:T(8,128)(2,1)S(1)} %add_convert_fusion.6), channel_id=1, source_target_pairs={{2,0},{4,2},{6,4},{7,6},{5,7},{3,5},{1,3},{0,1},{9,8},{8,10},{10,1... | collective-permute-start | bytes 1572872 | tf_op jit(solution)/shard_map/ppermute | solution.py:898
  223.2 14.0 %collective-permute-start.60 = (bf16[128,2048]{1,0:T(8,128)(2,1)S(1)}, bf16[128,2048]{1,0:T(8,128)(2,1)S(1)}, u32[]{:S(2)}, u32[]{:S(2)}) collective-permute-start(bf16[128,2048]{1,0:T(8,128)(2,1)S(1)} %add_convert_fusion.7), channel_id=1, source_target_pairs={{0,2},{2,4},{4,6},{6,7},{7,5},{5,3},{3,1},{1,0},{8,9},{10,8},{12,1... | collective-permute-start | bytes 1572872 | tf_op jit(solution)/shard_map/ppermute | solution.py:898
  265.3 19.3 %collective-permute-start.64 = (bf16[128,1280]{1,0:T(8,128)(2,1)S(1)}, bf16[128,1280]{1,0:T(8,128)(2,1)}, u32[]{:S(2)}, u32[]{:S(2)}) collective-permute-start(bf16[128,1280]{1,0:T(8,128)(2,1)S(1)} %pad_maximum_fusion.3), channel_id=1, source_target_pairs={{2,0},{4,2},{6,4},{7,6},{5,7},{3,5},{1,3},{0,1},{9,8},{8,10},{10,1... | collective-permute-start | bytes 983048 | tf_op jit(solution)/shard_map/ppermute | solution.py:898
  266.2 18.5 %collective-permute-start.63 = (bf16[128,1280]{1,0:T(8,128)(2,1)S(1)}, bf16[128,1280]{1,0:T(8,128)(2,1)}, u32[]{:S(2)}, u32[]{:S(2)}) collective-permute-start(bf16[128,1280]{1,0:T(8,128)(2,1)S(1)} %pad_maximum_fusion.2), channel_id=1, source_target_pairs={{0,2},{2,4},{4,6},{6,7},{7,5},{5,3},{3,1},{1,0},{8,9},{10,8},{12,1... | collective-permute-start | bytes 983048 | tf_op jit(solution)/shard_map/ppermute | solution.py:898
  288.9 27.8 %collective-permute-start.75 = (bf16[512,1024]{1,0:T(8,128)(2,1)}, bf16[512,1024]{1,0:T(8,128)(2,1)S(1)}, u32[]{:S(2)}, u32[]{:S(2)}) collective-permute-start(bf16[512,1024]{1,0:T(8,128)(2,1)} %get-tuple-element.287), channel_id=1, source_target_pairs={{0,8},{8,0},{16,24},{24,16},{1,9},{9,1},{17,25},{25,17},{2,10},{10... | collective-permute-start | bytes 3145736 | tf_op jit(solution)/shard_map/ppermute | solution.py:904
  297.1 18.3 %collective-permute-start.72 = (bf16[128,1280]{1,0:T(8,128)(2,1)}, bf16[128,1280]{1,0:T(8,128)(2,1)}, u32[]{:S(2)}, u32[]{:S(2)}) collective-permute-start(bf16[128,1280]{1,0:T(8,128)(2,1)} %add_convert_fusion.15), channel_id=1, source_target_pairs={{2,0},{4,2},{6,4},{7,6},{5,7},{3,5},{1,3},{0,1},{9,8},{8,10},{10,1... | collective-permute-start | bytes 983048 | tf_op jit(solution)/shard_map/ppermute | solution.py:898
  298.5 17.0 %collective-permute-start.71 = (bf16[128,1280]{1,0:T(8,128)(2,1)}, bf16[128,1280]{1,0:T(8,128)(2,1)}, u32[]{:S(2)}, u32[]{:S(2)}) collective-permute-start(bf16[128,1280]{1,0:T(8,128)(2,1)} %add_convert_fusion.16), channel_id=1, source_target_pairs={{0,2},{2,4},{4,6},{6,7},{7,5},{5,3},{3,1},{1,0},{8,9},{10,8},{12,1... | collective-permute-start | bytes 983048 | tf_op jit(solution)/shard_map/ppermute | solution.py:898
  308.6 30.4 %collective-permute-start.87 = (bf16[128,2048]{1,0:T(8,128)(2,1)S(1)}, bf16[128,2048]{1,0:T(8,128)(2,1)S(1)}, u32[]{:S(2)}, u32[]{:S(2)}) collective-permute-start(bf16[128,2048]{1,0:T(8,128)(2,1)S(1)} %add_convert_fusion.4.refs_0_), channel_id=1, source_target_pairs={{0,8},{8,0},{16,24},{24,16},{1,9},{9,1},{17,25},{25,17},{2,10},{10... | collective-permute-start | bytes 1572872 | tf_op jit(solution)/shard_map/ppermute | solution.py:904
  315.4 23.6 %collective-permute-start.88 = (bf16[128,2048]{1,0:T(8,128)(2,1)S(1)}, bf16[128,2048]{1,0:T(8,128)(2,1)S(1)}, u32[]{:S(2)}, u32[]{:S(2)}) collective-permute-start(bf16[128,2048]{1,0:T(8,128)(2,1)S(1)} %copy-done.26), channel_id=1, source_target_pairs={{0,8},{8,0},{16,24},{24,16},{1,9},{9,1},{17,25},{25,17},{2,10},{10... | collective-permute-start | bytes 1572872 | tf_op jit(solution)/shard_map/ppermute | solution.py:904
  324.9 19.6 %collective-permute-start.85 = (bf16[128,1280]{1,0:T(8,128)(2,1)S(1)}, bf16[128,1280]{1,0:T(8,128)(2,1)S(1)}, u32[]{:S(2)}, u32[]{:S(2)}) collective-permute-start(bf16[128,1280]{1,0:T(8,128)(2,1)S(1)} %add_convert_fusion.13.refs_0_), channel_id=1, source_target_pairs={{0,16},{8,24},{16,0},{24,8},{1,17},{9,25},{17,1},{25,9},{2,18},{10... | collective-permute-start | bytes 983048 | tf_op jit(solution)/shard_map/ppermute | solution.py:904
  (133 other events, 830.2 us)
Sparse Core Ops, SparseCore 0:
  51.9 73.6 all-gather.2

commit v3 on v2

--- a/solution.py
+++ b/solution.py
@@ -1189,14 +1189,15 @@
         sent = turns.send([p1, keep, ffn_all[2]])
         smalls = keep + at.swap_y(after(send, *sent))
         next(turns)
-        sent = turns.send([p_back[1]])
+        sent = turns.send([p_back[1], smalls])
         p0 = after(p0, *sent)
+        up_full, down_full = join_ffn(n, ffn_all, quarter)
     grad_tokens = ln1_last(tokens, xhats[0], grad_middle, small, p0, p_near, *p_back)
 
     outs = [o0, at.swap(o1, 1), jnp.concatenate(out_back, axis=0)]
     if at.rings:
         next(turns)
-        sent = turns.send([grad_tokens, smalls])
+        sent = turns.send([grad_tokens, up_full])
         smalls, outs[0] = after(smalls, *sent), after(o0, *sent)
         pick = lambda i: lax.dynamic_index_in_dim(smalls, i, 0, keepdims=False)
         z_parts = [pick(at.z)] + [
@@ -1205,7 +1206,7 @@
     output = (middle + valid * sum(p.astype(f32) for p in outs)).astype(bf16)
     if at.rings:
         next(turns)
-        attn_own = turns.send([output])
+        attn_own = turns.send([output, *z_parts[1:]])
         smalls = after(z_parts[0], attn_own) + sum(z_parts[1:])
 
     if not at.rings:
@@ -1224,8 +1225,8 @@
     smalls = smalls + at.swap(smalls, 2)
     smalls = smalls + at.swap(smalls, 1)
 
-    ffn_all[0] = after(ffn_all[0], attn_own)
-    up_full, down_full = join_ffn(n, ffn_all, quarter)
+    if not at.rings:
+        up_full, down_full = join_ffn(n, ffn_all, quarter)
     qkv_full, out_full = join_attn(n, at.all_narrow(attn_own), model)
 
     return (

time: 363 us -> 354 us (0.975)
  waiting for transfers between devices: 71.7 us -> 59.1 us
    ppermute x21, waiting for transfers between devices: 29.1 us -> 23.1 us  [ring(): return lax.ppermute(x, ('narrow', 'wide'), pairs)]
    ppermute x3, waiting for transfers between devices: 5.18 us -> 0.94 us  [along_z(): lax.ppermute(x, 'wide', [(i, (i + 2 * steps) % self.wide) for i in range(...]
    unnamed x150 -> x148, local copies, waits for them, and re-layouts: 11 us -> 9.76 us
  transfers between devices with their start and end apart: 90 -> 90, of which waited for: 33 -> 30; matrix products, arithmetic and copies ran while one was open for 14% -> 14% of each run, Pallas kernels for 40% -> 41%
where the time goes in v3:
time: 354 us; the launch traced here: 348 us
  Pallas kernels  153 us (43%)
  starting transfers between devices  59.1 us (17%)
  waiting for transfers between devices  59.1 us (17%)
  matrix products  22.3 us (6%)
  local copies, waits for them, and re-layouts  19.8 us (6%)
  other arithmetic  18.9 us (5%)
  between operations  15.7 us (4%)
    pallas_call x3, Pallas kernels, ffn(): pl.pallas_call(functools.partial(ffn_kernel, len(norms), places, start, c...  37.7 us
    ppermute x64, starting transfers between devices, swap(): return lax.ppermute(x, 'narrow', [(i, i ^ bit) for i in range(self.narrow)])  31.8 us
    ppermute x64, waiting for transfers between devices, swap(): return lax.ppermute(x, 'narrow', [(i, i ^ bit) for i in range(self.narrow)])  27.3 us
    ppermute x21, waiting for transfers between devices, ring(): return lax.ppermute(x, ('narrow', 'wide'), pairs)  23.1 us
    dot_general x5, matrix products, dot(): return lax.dot_general(a, b, (dims, ((), ())), preferred_element_type=f32)  22.3 us
    ppermute x21, starting transfers between devices, ring(): return lax.ppermute(x, ('narrow', 'wide'), pairs)  21.4 us
    pallas_call x4, Pallas kernels, attn_bwd(): pl.pallas_call(attn_bwd_kernel, grid=(steps,), in_specs=[pl.BlockSpec((sl...  18.9 us
    pallas_call x4, Pallas kernels, attn_fwd(): pl.pallas_call(attn_fwd_kernel, grid=(heads // 2,), in_specs=[pl.BlockSpe...  17 us
  transfers between devices with their start and end apart: 90, of which 30 were waited for; matrix products, arithmetic and copies ran while one was open for 14% of the time, Pallas kernels for 41%

profile of v3, /device:TPU:0, one launch (start us, length us, event | category | flops | bytes accessed | tf_op | source)
XLA Modules:
  0.0 348.4 jit_solution(9822023451250533865)
XLA Ops:
  19.8 5.3 %collective-permute-done.refs_2_.refs_6_ = bf16[128,1152]{1,0:T(8,128)(2,1)S(1)} collective-permute-done((bf16[128,1152]{1,0:T(8,128)(2,1)}, bf16[128,1152]{1,0:T(8,128)(2,1)S(1)}, u32[]{:S(2)}, u32[]{:S(2)}) %collective-permute-start) | collective-permute-done | bytes 294944 | tf_op jit(solution)/shard_map/ppermute | solution.py:898
  27.3 6.7 %collective-permute-done.3.refs_4_.refs_8_ = bf16[128,1152]{1,0:T(8,128)(2,1)S(1)} collective-permute-done((bf16[128,1152]{1,0:T(8,128)(2,1)S(1)}, bf16[128,1152]{1,0:T(8,128)(2,1)S(1)}, u32[]{:S(2)}, u32[]{:S(2)}) %collective-permute-start.3) | collective-permute-done | bytes 294944 | tf_op jit(solution)/shard_map/ppermute | solution.py:898
  34.7 3.3 xhat.4.refs_0_.x0_ref.xhat_ref
  44.2 7.1 %collective-permute-done.8.refs_6_.refs_10_ = bf16[128,1152]{1,0:T(8,128)(2,1)S(1)} collective-permute-done((bf16[128,1152]{1,0:T(8,128)(2,1)S(1)}, bf16[128,1152]{1,0:T(8,128)(2,1)S(1)}, u32[]{:S(2)}, u32[]{:S(2)}) %collective-permute-start.8) | collective-permute-done | bytes 294944 | tf_op jit(solution)/shard_map/ppermute | solution.py:898
  60.0 3.2 xhat.7.refs_3_.x1_ref
  67.9 11.1 %qkv.1 = (bf16[2048,1024]{1,0:T(8,128)(2,1)}, bf16[2048,768]{1,0:T(8,128)(2,1)}, bf16[1024,768]{1,0:T(8,128)(2,1)}, bf16[1024,256]{1,0:T(8,128)(2,1)}) custom-call(s32[8]{0:T(128)} %stack.53.where_ref, f32[8,1024]{1,0:T(8,128)} %small_rows.1.small_ref, f32[512,1024]{1,0:T(8,128)} %xhat.4.refs_0_.x0_ref.xhat_ref, f32[512,1024]{1,0:T(8,128)} %xhat.5.refs_1_.x1_ref, ...), custom_call_target="tpu_custom_call" | custom-call | flops 402500000 | tf_op jit(solution)/shard_map/qkv/pallas_call | solution.py:246
  83.2 4.4 %attn_fwd.7 = (bf16[512,256]{1,0:T(8,128)(2,1)}, bf16[4,512,512]{2,1,0:T(8,128)(2,1)}) custom-call(s32[1]{0:T(128)} %collective-permute-done.11.len_ref, bf16[2048,768]{1,0:T(8,128)(2,1)} %get-tuple-element.171.qkv_ref, f32[4,4,128,128]{3,2,1,0:T(8,128)} %bias_tiles.1.tiles_ref), custom_call_target="tpu_custom_call" | custom-call | flops 517500000 | tf_op jit(solution)/shard_map/attn_fwd/pallas_call | solution.py:346
  88.0 4.3 %attn_fwd.5 = (bf16[512,256]{1,0:T(8,128)(2,1)}, bf16[4,512,512]{2,1,0:T(8,128)(2,1)}) custom-call(s32[1]{0:T(128)} %collective-permute-done.10.len_ref, bf16[2048,768]{1,0:T(8,128)(2,1)} %get-tuple-element.171.qkv_ref, f32[4,4,128,128]{3,2,1,0:T(8,128)} %bias_tiles.1.tiles_ref), custom_call_target="tpu_custom_call" | custom-call | flops 517500000 | tf_op jit(solution)/shard_map/attn_fwd/pallas_call | solution.py:346
  94.0 4.4 %attn_fwd.6 = (bf16[512,256]{1,0:T(8,128)(2,1)}, bf16[4,512,512]{2,1,0:T(8,128)(2,1)}) custom-call(s32[1]{0:T(128)} %collective-permute-done.5.len_ref, bf16[2048,768]{1,0:T(8,128)(2,1)} %get-tuple-element.171.qkv_ref, f32[4,4,128,128]{3,2,1,0:T(8,128)} %bias_tiles.1.tiles_ref), custom_call_target="tpu_custom_call" | custom-call | flops 517500000 | tf_op jit(solution)/shard_map/attn_fwd/pallas_call | solution.py:346
  100.2 7.2 %collective-permute-done.19.refs_2_ = bf16[512,256]{1,0:T(8,128)(2,1)S(1)} collective-permute-done((bf16[512,256]{1,0:T(8,128)(2,1)}, bf16[512,256]{1,0:T(8,128)(2,1)S(1)}, u32[]{:S(2)}, u32[]{:S(2)}) %collective-permute-start.19) | collective-permute-done | bytes 262176 | tf_op jit(solution)/shard_map/ppermute | solution.py:904
  107.4 3.9 %attn_fwd.4 = (bf16[512,256]{1,0:T(8,128)(2,1)}, bf16[4,512,512]{2,1,0:T(8,128)(2,1)}) custom-call(s32[1]{0:T(128)} %copy.64.len_ref, bf16[2048,768]{1,0:T(8,128)(2,1)} %get-tuple-element.171.qkv_ref, f32[4,4,128,128]{3,2,1,0:T(8,128)} %bias_tiles.1.tiles_ref), custom_call_target="tpu_custom_call" | custom-call | flops 517500000 | tf_op jit(solution)/shard_map/attn_fwd/pallas_call | solution.py:346
  112.1 3.9 %out_ln2.2 = (f32[512,1024]{1,0:T(8,128)}, bf16[512,1024]{1,0:T(8,128)(2,1)}, bf16[256,1024]{1,0:T(8,128)(2,1)}) custom-call(s32[1]{0:T(128)} %bitcast.n_ref, s32[1]{0:T(128)} %copy.64.len_ref, bf16[512,1024]{1,0:T(8,128)(2,1)} %tok_ref.5, f32[8,1024]{1,0:T(8,128)} %small_rows.1.small_ref, bf16[512,256]{1,0:T(8,128)(2,1)} %get-tuple-element.172.refs_0_.att_ref, ...), custom_call_target="tpu_custom_call" | custom-call | flops 71875000 | tf_op jit(solution)/shard_map/out_ln2/pallas_call | solution.py:510
  116.1 3.9 %out_ln2.3 = (f32[512,1024]{1,0:T(8,128)}, bf16[512,1024]{1,0:T(8,128)(2,1)}, bf16[256,1024]{1,0:T(8,128)(2,1)}) custom-call(s32[1]{0:T(128)} %bitcast.n_ref, s32[1]{0:T(128)} %copy.64.len_ref, bf16[512,1024]{1,0:T(8,128)(2,1)} %tok_ref.5, f32[8,1024]{1,0:T(8,128)} %small_rows.1.small_ref, ...), custom_call_target="tpu_custom_call", output_to_operand_aliasing={{0}: (12, {}), {1}: (13, {})} | custom-call | flops 71875000 | tf_op jit(solution)/shard_map/out_ln2/pallas_call | solution.py:510
  125.4 16.6 %ffn.3 = (f32[512,1024]{1,0:T(8,128)}, f32[512,1024]{1,0:T(8,128)}, bf16[512,1024]{1,0:T(8,128)(2,1)}, bf16[128,1024]{1,0:T(8,128)(2,1)}, bf16[128,1024]{1,0:T(8...) custom-call(bf16[8,2,128,1024]{3,2,1,0:T(8,128)(2,1)} %bitcast.118, ...), custom_call_target="tpu_custom_call" | custom-call | flops 215624992 | tf_op jit(solution)/shard_map/ffn/pallas_call | solution.py:701
  145.9 10.6 %ffn.4 = (f32[256,1024]{1,0:T(8,128)}, f32[256,1024]{1,0:T(8,128)}, bf16[256,1024]{1,0:T(8,128)(2,1)}, bf16[64,1024]{1,0:T(8,128)(2,1)}, bf16[64,1024]{1,0:T(8,1...) custom-call(bf16[8,2,128,1024]{3,2,1,0:T(8,128)(2,1)} %bitcast.119, ...), custom_call_target="tpu_custom_call", output_to_operand_aliasing={{7}: (8, {}), {8}: (9, {}), {9}: (10, {}), {10}: (11, {})} | custom-call | flops 143750000 | tf_op jit(solution)/shard_map/ffn/pallas_call | solution.py:701
  162.7 10.6 %ffn.5 = (f32[256,1024]{1,0:T(8,128)}, f32[256,1024]{1,0:T(8,128)}, bf16[256,1024]{1,0:T(8,128)(2,1)}, bf16[64,1024]{1,0:T(8,128)(2,1)}, bf16[64,1024]{1,0:T(8,1...) custom-call(bf16[8,2,128,1024]{3,2,1,0:T(8,128)(2,1)} %bitcast.120, ...), custom_call_target="tpu_custom_call", output_to_operand_aliasing={{7}: (8, {}), {8}: (9, {}), {9}: (10, {}), {10}: (11, {})} | custom-call | flops 143750000 | tf_op jit(solution)/shard_map/ffn/pallas_call | solution.py:701
  178.0 8.2 %convolution_convert_fusion.1 = bf16[1024,1024]{1,0:T(8,128)(2,1)S(1)} fusion(bf16[2048,1024]{1,0:T(8,128)(2,1)} %get-tuple-element.224, bf16[2048,1024]{1,0:T(8,128)(2,1)} %get-tuple-element.226), kind=kOutput, calls=%fused_computation.5 | convolution fusion | flops 4296015872 | bytes 10485760 | tf_op jit(solution)/shard_map/dot_general | solution.py:32
  186.2 5.0 %convolution_convert_fusion = bf16[1024,1024]{1,0:T(8,128)(2,1)S(1)} fusion(bf16[2048,1024]{1,0:T(8,128)(2,1)S(1)} %copy-done.2, bf16[2048,1024]{1,0:T(8,128)(2,1)S(1)} %copy-done.1), kind=kOutput, calls=%fused_computation.4 | convolution fusion | flops 4296015872 | bytes 10485760 | tf_op jit(solution)/shard_map/dot_general | solution.py:32
  195.0 5.1 %ln2_back.2 = (f32[512,1024]{1,0:T(8,128)}, bf16[512,512]{1,0:T(8,128)(2,1)}, bf16[512,512]{1,0:T(8,128)(2,1)}, bf16[512,256]{1,0:T(8,128)(2,1)}, bf16[512,256]{...) custom-call(s32[1]{0:T(128)} %bitcast.n_ref, s32[1]{0:T(128)} %copy.64.len_ref, ...), custom_call_target="tpu_custom_call" | custom-call | flops 5750000128 | tf_op jit(solution)/shard_map/ln2_back/pallas_call | solution.py:569
  201.1 5.2 %ln2_back.3 = (f32[512,1024]{1,0:T(8,128)}, bf16[512,512]{1,0:T(8,128)(2,1)}, bf16[512,512]{1,0:T(8,128)(2,1)}, bf16[512,256]{1,0:T(8,128)(2,1)}, bf16[512,256]{...) custom-call(s32[1]{0:T(128)} %bitcast.n_ref, ...), custom_call_target="tpu_custom_call", output_to_operand_aliasing={{0}: (13, {}), {1}: (14, {}), {2}: (15, {}), {3}: (16, {}),... | custom-call | flops 5750000128 | tf_op jit(solution)/shard_map/ln2_back/pallas_call | solution.py:569
  210.1 4.7 %attn_bwd.4 = (bf16[2048,768]{1,0:T(8,128)(2,1)}, f32[2,2,512]{2,1,0:T(2,128)}) custom-call(bf16[2048,768]{1,0:T(8,128)(2,1)} %get-tuple-element.171.qkv_ref, bf16[512,256]{1,0:T(8,128)(2,1)} %get-tuple-element.232.ga_ref, bf16[512,256]{1,0:T(8,128)(2,1)} %get-tuple-element.172.refs_0_.att_ref, bf16[4,512,512]{2,1,0:T(8,128)(2,1)} %get-tuple-element.233.p_ref), custom_call_target="tpu_custom_call" | custom-call | flops 1150000000 | tf_op jit(solution)/shard_map/attn_bwd/pallas_call | solution.py:431
  227.2 5.0 %attn_bwd.5 = (bf16[2048,768]{1,0:T(8,128)(2,1)}, f32[2,2,512]{2,1,0:T(2,128)}) custom-call(bf16[2048,768]{1,0:T(8,128)(2,1)} %get-tuple-element.171.qkv_ref, bf16[512,256]{1,0:T(8,128)(2,1)} %copy-done.44, bf16[512,256]{1,0:T(8,128)(2,1)} %get-tuple-element.175.att_ref, ...), custom_call_target="tpu_custom_call", output_to_operand_aliasing={{0}: (4, {})} | custom-call | flops 1150000000 | tf_op jit(solution)/shard_map/attn_bwd/pallas_call | solution.py:431
  232.6 4.6 %attn_bwd.6 = (bf16[2048,768]{1,0:T(8,128)(2,1)}, f32[2,2,512]{2,1,0:T(2,128)}) custom-call(bf16[2048,768]{1,0:T(8,128)(2,1)} %get-tuple-element.171.qkv_ref, bf16[512,256]{1,0:T(8,128)(2,1)} %copy-done.43, bf16[512,256]{1,0:T(8,128)(2,1)} %get-tuple-element.176.att_ref, ...), custom_call_target="tpu_custom_call", output_to_operand_aliasing={{0}: (4, {})} | custom-call | flops 1150000000 | tf_op jit(solution)/shard_map/attn_bwd/pallas_call | solution.py:431
  238.4 7.3 %ln1_back.2 = (bf16[512,1024]{1,0:T(8,128)(2,1)}, bf16[512,1024]{1,0:T(8,128)(2,1)}, f32[2,1024]{1,0:T(2,128)}) custom-call(bf16[2048,768]{1,0:T(8,128)(2,1)} %get-tuple-element.252.gp_ref.refs_0_, bf16[1024,768]{1,0:T(8,128)(2,1)} %get-tuple-element.253.wq_ref, f32[512,1024]{1,0:T(8,128)} %xhat.6.refs_2_.x0_ref, f32[512,1024]{1,0:T(8,128)} %xhat.7.refs_3_.x1_ref), custom_call_target="tpu_custom_call" | custom-call | flops 575000000 | tf_op jit(solution)/shard_map/ln1_back/pallas_call | solution.py:291
  250.1 4.6 %attn_bwd.7 = (bf16[2048,768]{1,0:T(8,128)(2,1)}, f32[2,2,512]{2,1,0:T(2,128)}) custom-call(bf16[2048,768]{1,0:T(8,128)(2,1)} %get-tuple-element.171.qkv_ref, bf16[512,256]{1,0:T(8,128)(2,1)} %copy-done.45, bf16[512,256]{1,0:T(8,128)(2,1)} %get-tuple-element.173.att_ref, ...), custom_call_target="tpu_custom_call", output_to_operand_aliasing={{0}: (4, {})} | custom-call | flops 1150000000 | tf_op jit(solution)/shard_map/attn_bwd/pallas_call | solution.py:431
  258.6 6.7 %convolution_convert_fusion.2 = bf16[1024,768]{1,0:T(8,128)(2,1)S(1)} fusion(bf16[2048,1024]{1,0:T(8,128)(2,1)} %get-tuple-element.186, bf16[2048,768]{1,0:T(8,128)(2,1)} %get-tuple-element.259.gp_ref), kind=kOutput, calls=%fused_computation.6 | convolution fusion | flops 3222011904 | bytes 8912896 | tf_op jit(solution)/shard_map/dot_general | solution.py:32
  272.1 7.8 %ln1_back.3 = (f32[512,1024]{1,0:T(8,128)}, bf16[512,1024]{1,0:T(8,128)(2,1)}, f32[2,1024]{1,0:T(2,128)}) custom-call(bf16[2048,768]{1,0:T(8,128)(2,1)} %get-tuple-element.259.gp_ref, bf16[1024,768]{1,0:T(8,128)(2,1)} %get-tuple-element.253.wq_ref, f32[512,1024]{1,0:T(8,128)} %xhat.4.refs_0_.x0_ref.xhat_ref, f32[512,1024]{1,0:T(8,128)} %xhat.5.refs_1_.x1_ref), custom_call_target="tpu_custom_call" | custom-call | flops 5750000128 | tf_op jit(solution)/shard_map/ln1_back/pallas_call | solution.py:291
  291.1 5.4 %collective-permute-done.71 = f32[4,8,128]{2,1,0:T(8,128)S(1)} collective-permute-done((f32[4,8,128]{2,1,0:T(8,128)}, f32[4,8,128]{2,1,0:T(8,128)S(1)}, u32[]{:S(2)}, u32[]{:S(2)}) %collective-permute-start.71) | collective-permute-done | bytes 16416 | tf_op jit(solution)/shard_map/ppermute | solution.py:911
  307.2 3.9 %join_ffn.1 = (f32[128,4096]{1,0:T(8,128)}, f32[512,1024]{1,0:T(8,128)}) custom-call(s32[1]{0:T(128)} %bitcast.n_ref, bf16[128,2048]{1,0:T(8,128)(2,1)} %copy-done.8, bf16[128,2048]{1,0:T(8,128)(2,1)} %copy-done.25, bf16[128,2048]{1,0:T(8,128)(2,1)} %collective-permute-done.67.refs_2_, bf16[128,2048]{1,0:T(8,128)(2,1)} %collective-permute-done.76.refs_3_), custom_call_target="tpu_custom_call" | custom-call | flops 230000000 | tf_op jit(solution)/shard_map/join_ffn/pallas_call | solution.py:820
  311.1 5.8 %ln1_last.1 = f32[512,1024]{1,0:T(8,128)} custom-call(bf16[512,1024]{1,0:T(8,128)(2,1)} %tok_ref.5, f32[512,1024]{1,0:T(8,128)} %xhat.4.refs_0_.x0_ref.xhat_ref, f32[512,1024]{1,0:T(8,128)} %get-tuple-element.280.gmid_ref, f32[8,1024]{1,0:T(8,128)} %small_rows.1.small_ref, f32[512,1024]{1,0:T(8,128)} %get-tuple-element.282.p0_ref, ...), custom_call_target="tpu_custom_call" | custom-call | flops 287500000 | tf_op jit(solution)/shard_map/ln1_last/pallas_call | solution.py:472
  318.8 3.2 collective-permute-start.82
  328.8 5.8 %collective-permute-done.84 = f32[8,128]{1,0:T(8,128)S(1)} collective-permute-done((f32[8,128]{1,0:T(8,128)S(1)}, f32[8,128]{1,0:T(8,128)S(1)}, u32[]{:S(2)}, u32[]{:S(2)}) %collective-permute-start.84) | collective-permute-done | bytes 4128 | tf_op jit(solution)/shard_map/ppermute | solution.py:904
  (377 shorter events, 138.2 us)
Async XLA Ops:
  7.2 118.2 %all-gather.3.cloned.1.call-start = ((), (), s32[]{:S(2)}) async-start(), calls=%async_computation | async-start | bytes 4718592 | tf_op jit(solution)/shard_map/all_gather | solution.py:1070
  7.2 30.7 %collective-permute-start.7 = (bf16[512,1024]{1,0:T(8,128)(2,1)}, bf16[512,1024]{1,0:T(8,128)(2,1)S(1)}, u32[]{:S(2)}, u32[]{:S(2)}) collective-permute-start(bf16[512,1024]{1,0:T(8,128)(2,1)} %tok_ref.5), channel_id=1, source_target_pairs={{0,8},{8,0},{16,24},{24,16},{1,9},{9,1},{17,25},{25,17},{2,10},{10... | collective-permute-start | bytes 3145736 | tf_op jit(solution)/shard_map/ppermute | solution.py:904
  8.8 16.3 %collective-permute-start.2 = (bf16[224,1024]{1,0:T(8,128)(2,1)S(1)}, bf16[224,1024]{1,0:T(8,128)(2,1)}, u32[]{:S(2)}, u32[]{:S(2)}) collective-permute-start(bf16[224,1024]{1,0:T(8,128)(2,1)S(1)} %slice.51), channel_id=1, source_target_pairs={{0,16},{8,24},{16,0},{24,8},{1,17},{9,25},{17,1},{25,9},{2,18},{10... | collective-permute-start | bytes 1376264 | tf_op jit(solution)/shard_map/ppermute | solution.py:904
  17.5 24.6 %collective-permute-start.6 = (bf16[288,1024]{1,0:T(8,128)(2,1)S(1)}, bf16[288,1024]{1,0:T(8,128)(2,1)}, u32[]{:S(2)}, u32[]{:S(2)}) collective-permute-start(bf16[288,1024]{1,0:T(8,128)(2,1)S(1)} %slice.52), channel_id=1, source_target_pairs={{0,16},{8,24},{16,0},{24,8},{1,17},{9,25},{17,1},{25,9},{2,18},{10... | collective-permute-start | bytes 1769480 | tf_op jit(solution)/shard_map/ppermute | solution.py:904
  27.2 14.9 %collective-permute-start.5 = (s32[1]{0:T(128)}, s32[1]{0:T(128)}, u32[]{:S(2)}, u32[]{:S(2)}) collective-permute-start(s32[1]{0:T(128)} %param.14), channel_id=1, source_target_pairs={{0,16},{8,24},{16,0},{24,8},{1,17},{9,25},{17,1},{25,9},{2,18},{10... | collective-permute-start | bytes 20 | tf_op jit(solution)/shard_map/ppermute | solution.py:904
  53.9 34.1 %collective-permute-start.14 = (bf16[512,1024]{1,0:T(8,128)(2,1)S(1)}, bf16[512,1024]{1,0:T(8,128)(2,1)S(1)}, u32[]{:S(2)}, u32[]{:S(2)}) collective-permute-start(bf16[512,1024]{1,0:T(8,128)(2,1)S(1)} %multiply_convert_fusion.refs_4_), channel_id=1, source_target_pairs={{0,16},{8,24},{16,0},{24,8},{1,17},{9,25},{17,1},{25,9},{2,18},{10... | collective-permute-start | bytes 3145736 | tf_op jit(solution)/shard_map/ppermute | solution.py:904
  58.4 63.5 %collective-permute-start.13 = (bf16[512,1024]{1,0:T(8,128)(2,1)S(1)}, bf16[512,1024]{1,0:T(8,128)(2,1)}, u32[]{:S(2)}, u32[]{:S(2)}) collective-permute-start(bf16[512,1024]{1,0:T(8,128)(2,1)S(1)} %multiply_convert_fusion.refs_4_), channel_id=1, source_target_pairs={{0,8},{8,0},{16,24},{24,16},{1,9},{9,1},{17,25},{25,17},{2,10},{10... | collective-permute-start | bytes 3145736 | tf_op jit(solution)/shard_map/ppermute | solution.py:904
  78.9 15.1 %collective-permute-start.22 = (bf16[1024,256]{1,0:T(8,128)(2,1)}, bf16[1024,256]{1,0:T(8,128)(2,1)}, u32[]{:S(2)}, u32[]{:S(2)}) collective-permute-start(bf16[1024,256]{1,0:T(8,128)(2,1)} %get-tuple-element.177.refs_4_.refs_2_), channel_id=1, source_target_pairs={{0,16},{8,24},{16,0},{24,8},{1,17},{9,25},{17,1},{25,9},{2,18},{10... | collective-permute-start | bytes 1572872 | tf_op jit(solution)/shard_map/ppermute | solution.py:904
  80.4 30.8 %collective-permute-start.21 = (bf16[1024,256]{1,0:T(8,128)(2,1)}, bf16[1024,256]{1,0:T(8,128)(2,1)}, u32[]{:S(2)}, u32[]{:S(2)}) collective-permute-start(bf16[1024,256]{1,0:T(8,128)(2,1)} %get-tuple-element.177.refs_4_.refs_2_), channel_id=1, source_target_pairs={{0,8},{8,0},{16,24},{24,16},{1,9},{9,1},{17,25},{25,17},{2,10},{10... | collective-permute-start | bytes 1572872 | tf_op jit(solution)/shard_map/ppermute | solution.py:904
  94.0 17.2 %collective-permute-start.23 = (bf16[1024,256]{1,0:T(8,128)(2,1)}, bf16[1024,256]{1,0:T(8,128)(2,1)S(1)}, u32[]{:S(2)}, u32[]{:S(2)}) collective-permute-start(bf16[1024,256]{1,0:T(8,128)(2,1)} %collective-permute-done.22.refs_6_.refs_4_), channel_id=1, source_target_pairs={{0,8},{8,0},{16,24},{24,16},{1,9},{9,1},{17,25},{25,17},{2,10},{10... | collective-permute-start | bytes 1572872 | tf_op jit(solution)/shard_map/ppermute | solution.py:904
  107.4 36.4 %collective-permute-start.15 = (bf16[512,1024]{1,0:T(8,128)(2,1)S(1)}, bf16[512,1024]{1,0:T(8,128)(2,1)S(1)}, u32[]{:S(2)}, u32[]{:S(2)}) collective-permute-start(bf16[512,1024]{1,0:T(8,128)(2,1)S(1)} %collective-permute-done.14.refs_5_), channel_id=1, source_target_pairs={{0,8},{8,0},{16,24},{24,16},{1,9},{9,1},{17,25},{25,17},{2,10},{10... | collective-permute-start | bytes 3145736 | tf_op jit(solution)/shard_map/ppermute | solution.py:904
  120.5 21.5 %collective-permute-start.27 = (bf16[256,1024]{1,0:T(8,128)(2,1)}, bf16[256,1024]{1,0:T(8,128)(2,1)}, u32[]{:S(2)}, u32[]{:S(2)}) collective-permute-start(bf16[256,1024]{1,0:T(8,128)(2,1)} %get-tuple-element.183.refs_0_), channel_id=1, source_target_pairs={{0,16},{8,24},{16,0},{24,8},{1,17},{9,25},{17,1},{25,9},{2,18},{10... | collective-permute-start | bytes 1572872 | tf_op jit(solution)/shard_map/ppermute | solution.py:904
  122.0 35.6 %collective-permute-start.26 = (bf16[256,1024]{1,0:T(8,128)(2,1)}, bf16[256,1024]{1,0:T(8,128)(2,1)S(1)}, u32[]{:S(2)}, u32[]{:S(2)}) collective-permute-start(bf16[256,1024]{1,0:T(8,128)(2,1)} %get-tuple-element.184.refs_1_), channel_id=1, source_target_pairs={{0,16},{8,24},{16,0},{24,8},{1,17},{9,25},{17,1},{25,9},{2,18},{10... | collective-permute-start | bytes 1572872 | tf_op jit(solution)/shard_map/ppermute | solution.py:904
  160.4 17.0 %collective-permute-start.47 = (bf16[256,1024]{1,0:T(8,128)(2,1)S(1)}, bf16[256,1024]{1,0:T(8,128)(2,1)S(1)}, u32[]{:S(2)}, u32[]{:S(2)}) collective-permute-start(bf16[256,1024]{1,0:T(8,128)(2,1)S(1)} %add_convert_fusion.12), channel_id=1, source_target_pairs={{0,16},{8,24},{16,0},{24,8},{1,17},{9,25},{17,1},{25,9},{2,18},{10... | collective-permute-start | bytes 1572872 | tf_op jit(solution)/shard_map/ppermute | solution.py:904
  174.9 18.0 %collective-permute-start.48 = (bf16[128,1024]{1,0:T(8,128)(2,1)S(1)}, bf16[128,1024]{1,0:T(8,128)(2,1)S(1)}, u32[]{:S(2)}, u32[]{:S(2)}) collective-permute-start(bf16[128,1024]{1,0:T(8,128)(2,1)S(1)} %copy-done.67), channel_id=1, source_target_pairs={{0,8},{8,0},{16,24},{24,16},{1,9},{9,1},{17,25},{25,17},{2,10},{10... | collective-permute-start | bytes 786440 | tf_op jit(solution)/shard_map/ppermute | solution.py:904
  175.1 18.4 %collective-permute-start.49 = (bf16[128,1024]{1,0:T(8,128)(2,1)S(1)}, bf16[128,1024]{1,0:T(8,128)(2,1)S(1)}, u32[]{:S(2)}, u32[]{:S(2)}) collective-permute-start(bf16[128,1024]{1,0:T(8,128)(2,1)S(1)} %copy-done.66), channel_id=1, source_target_pairs={{0,8},{8,0},{16,24},{24,16},{1,9},{9,1},{17,25},{25,17},{2,10},{10... | collective-permute-start | bytes 786440 | tf_op jit(solution)/shard_map/ppermute | solution.py:904
  175.4 24.6 %collective-permute-start.45 = (bf16[128,1024]{1,0:T(8,128)(2,1)S(1)}, bf16[128,1024]{1,0:T(8,128)(2,1)S(1)}, u32[]{:S(2)}, u32[]{:S(2)}) collective-permute-start(bf16[128,1024]{1,0:T(8,128)(2,1)S(1)} %copy-done.65), channel_id=1, source_target_pairs={{0,8},{8,0},{16,24},{24,16},{1,9},{9,1},{17,25},{25,17},{2,10},{10... | collective-permute-start | bytes 786440 | tf_op jit(solution)/shard_map/ppermute | solution.py:904
  175.6 24.4 %collective-permute-start.46 = (bf16[128,1024]{1,0:T(8,128)(2,1)S(1)}, bf16[128,1024]{1,0:T(8,128)(2,1)S(1)}, u32[]{:S(2)}, u32[]{:S(2)}) collective-permute-start(bf16[128,1024]{1,0:T(8,128)(2,1)S(1)} %copy-done.64), channel_id=1, source_target_pairs={{0,8},{8,0},{16,24},{24,16},{1,9},{9,1},{17,25},{25,17},{2,10},{10... | collective-permute-start | bytes 786440 | tf_op jit(solution)/shard_map/ppermute | solution.py:904
  177.3 22.7 %collective-permute-start.44 = (bf16[256,1024]{1,0:T(8,128)(2,1)S(1)}, bf16[256,1024]{1,0:T(8,128)(2,1)S(1)}, u32[]{:S(2)}, u32[]{:S(2)}) collective-permute-start(bf16[256,1024]{1,0:T(8,128)(2,1)S(1)} %add_convert_fusion.11), channel_id=1, source_target_pairs={{0,16},{8,24},{16,0},{24,8},{1,17},{9,25},{17,1},{25,9},{2,18},{10... | collective-permute-start | bytes 1572872 | tf_op jit(solution)/shard_map/ppermute | solution.py:904
  192.9 14.8 %collective-permute-start.53 = (bf16[128,2048]{1,0:T(8,128)(2,1)S(1)}, bf16[128,2048]{1,0:T(8,128)(2,1)S(1)}, u32[]{:S(2)}, u32[]{:S(2)}) collective-permute-start(bf16[128,2048]{1,0:T(8,128)(2,1)S(1)} %pad_maximum_fusion.1), channel_id=1, source_target_pairs={{2,0},{4,2},{6,4},{7,6},{5,7},{3,5},{1,3},{0,1},{9,8},{8,10},{10,1... | collective-permute-start | bytes 1572872 | tf_op jit(solution)/shard_map/ppermute | solution.py:898
  193.5 14.2 %collective-permute-start.52 = (bf16[128,2048]{1,0:T(8,128)(2,1)S(1)}, bf16[128,2048]{1,0:T(8,128)(2,1)S(1)}, u32[]{:S(2)}, u32[]{:S(2)}) collective-permute-start(bf16[128,2048]{1,0:T(8,128)(2,1)S(1)} %pad_maximum_fusion), channel_id=1, source_target_pairs={{0,2},{2,4},{4,6},{6,7},{7,5},{5,3},{3,1},{1,0},{8,9},{10,8},{12,1... | collective-permute-start | bytes 1572872 | tf_op jit(solution)/shard_map/ppermute | solution.py:898
  207.8 14.5 %collective-permute-start.57 = (bf16[128,2048]{1,0:T(8,128)(2,1)S(1)}, bf16[128,2048]{1,0:T(8,128)(2,1)S(1)}, u32[]{:S(2)}, u32[]{:S(2)}) collective-permute-start(bf16[128,2048]{1,0:T(8,128)(2,1)S(1)} %add_convert_fusion.9), channel_id=1, source_target_pairs={{2,0},{4,2},{6,4},{7,6},{5,7},{3,5},{1,3},{0,1},{9,8},{8,10},{10,1... | collective-permute-start | bytes 1572872 | tf_op jit(solution)/shard_map/ppermute | solution.py:898
  208.6 13.8 %collective-permute-start.56 = (bf16[128,2048]{1,0:T(8,128)(2,1)S(1)}, bf16[128,2048]{1,0:T(8,128)(2,1)S(1)}, u32[]{:S(2)}, u32[]{:S(2)}) collective-permute-start(bf16[128,2048]{1,0:T(8,128)(2,1)S(1)} %add_convert_fusion.10), channel_id=1, source_target_pairs={{0,2},{2,4},{4,6},{6,7},{7,5},{5,3},{3,1},{1,0},{8,9},{10,8},{12,1... | collective-permute-start | bytes 1572872 | tf_op jit(solution)/shard_map/ppermute | solution.py:898
  222.6 14.8 %collective-permute-start.61 = (bf16[128,2048]{1,0:T(8,128)(2,1)S(1)}, bf16[128,2048]{1,0:T(8,128)(2,1)S(1)}, u32[]{:S(2)}, u32[]{:S(2)}) collective-permute-start(bf16[128,2048]{1,0:T(8,128)(2,1)S(1)} %add_convert_fusion.6), channel_id=1, source_target_pairs={{2,0},{4,2},{6,4},{7,6},{5,7},{3,5},{1,3},{0,1},{9,8},{8,10},{10,1... | collective-permute-start | bytes 1572872 | tf_op jit(solution)/shard_map/ppermute | solution.py:898
  223.3 14.0 %collective-permute-start.60 = (bf16[128,2048]{1,0:T(8,128)(2,1)S(1)}, bf16[128,2048]{1,0:T(8,128)(2,1)S(1)}, u32[]{:S(2)}, u32[]{:S(2)}) collective-permute-start(bf16[128,2048]{1,0:T(8,128)(2,1)S(1)} %add_convert_fusion.7), channel_id=1, source_target_pairs={{0,2},{2,4},{4,6},{6,7},{7,5},{5,3},{3,1},{1,0},{8,9},{10,8},{12,1... | collective-permute-start | bytes 1572872 | tf_op jit(solution)/shard_map/ppermute | solution.py:898
  257.3 13.5 %collective-permute-start.65 = (bf16[256,1024]{1,0:T(8,128)(2,1)S(1)}, bf16[256,1024]{1,0:T(8,128)(2,1)S(1)}, u32[]{:S(2)}, u32[]{:S(2)}) collective-permute-start(bf16[256,1024]{1,0:T(8,128)(2,1)S(1)} %get-tuple-element.332), channel_id=1, source_target_pairs={{0,16},{8,24},{16,0},{24,8},{1,17},{9,25},{17,1},{25,9},{2,18},{10... | collective-permute-start | bytes 1572872 | tf_op jit(solution)/shard_map/ppermute | solution.py:904
  266.2 15.7 %collective-permute-start.64 = (bf16[128,1280]{1,0:T(8,128)(2,1)}, bf16[128,1280]{1,0:T(8,128)(2,1)}, u32[]{:S(2)}, u32[]{:S(2)}) collective-permute-start(bf16[128,1280]{1,0:T(8,128)(2,1)} %pad_maximum_fusion.3), channel_id=1, source_target_pairs={{2,0},{4,2},{6,4},{7,6},{5,7},{3,5},{1,3},{0,1},{9,8},{8,10},{10,1... | collective-permute-start | bytes 983048 | tf_op jit(solution)/shard_map/ppermute | solution.py:898
  267.7 14.2 %collective-permute-start.63 = (bf16[128,1280]{1,0:T(8,128)(2,1)}, bf16[128,1280]{1,0:T(8,128)(2,1)}, u32[]{:S(2)}, u32[]{:S(2)}) collective-permute-start(bf16[128,1280]{1,0:T(8,128)(2,1)} %pad_maximum_fusion.2), channel_id=1, source_target_pairs={{0,2},{2,4},{4,6},{6,7},{7,5},{5,3},{3,1},{1,0},{8,9},{10,8},{12,1... | collective-permute-start | bytes 983048 | tf_op jit(solution)/shard_map/ppermute | solution.py:898
  283.4 15.1 %collective-permute-start.70 = (bf16[256,1024]{1,0:T(8,128)(2,1)}, bf16[256,1024]{1,0:T(8,128)(2,1)}, u32[]{:S(2)}, u32[]{:S(2)}) collective-permute-start(bf16[256,1024]{1,0:T(8,128)(2,1)} %get-tuple-element.275), channel_id=1, source_target_pairs={{0,16},{8,24},{16,0},{24,8},{1,17},{9,25},{17,1},{25,9},{2,18},{10... | collective-permute-start | bytes 1572872 | tf_op jit(solution)/shard_map/ppermute | solution.py:904
  291.1 30.9 %collective-permute-start.77 = (bf16[512,1024]{1,0:T(8,128)(2,1)}, bf16[512,1024]{1,0:T(8,128)(2,1)S(1)}, u32[]{:S(2)}, u32[]{:S(2)}) collective-permute-start(bf16[512,1024]{1,0:T(8,128)(2,1)} %get-tuple-element.287), channel_id=1, source_target_pairs={{0,8},{8,0},{16,24},{24,16},{1,9},{9,1},{17,25},{25,17},{2,10},{10... | collective-permute-start | bytes 3145736 | tf_op jit(solution)/shard_map/ppermute | solution.py:904
  302.6 14.3 %collective-permute-start.73 = (bf16[128,1280]{1,0:T(8,128)(2,1)}, bf16[128,1280]{1,0:T(8,128)(2,1)}, u32[]{:S(2)}, u32[]{:S(2)}) collective-permute-start(bf16[128,1280]{1,0:T(8,128)(2,1)} %add_convert_fusion.15), channel_id=1, source_target_pairs={{2,0},{4,2},{6,4},{7,6},{5,7},{3,5},{1,3},{0,1},{9,8},{8,10},{10,1... | collective-permute-start | bytes 983048 | tf_op jit(solution)/shard_map/ppermute | solution.py:898
  306.6 16.6 %collective-permute-start.79 = (bf16[256,1024]{1,0:T(8,128)(2,1)S(1)}, bf16[256,1024]{1,0:T(8,128)(2,1)S(1)}, u32[]{:S(2)}, u32[]{:S(2)}) collective-permute-start(bf16[256,1024]{1,0:T(8,128)(2,1)S(1)} %add_convert_fusion.3), channel_id=1, source_target_pairs={{0,16},{8,24},{16,0},{24,8},{1,17},{9,25},{17,1},{25,9},{2,18},{10... | collective-permute-start | bytes 1572872 | tf_op jit(solution)/shard_map/ppermute | solution.py:904
  (132 other events, 792.9 us)
Sparse Core Ops, SparseCore 0:
  51.8 73.5 all-gather.2

commit v4 on v3

--- a/solution.py
+++ b/solution.py
@@ -1080,7 +1080,7 @@
     tiles = bias_tiles(n, small, buckets, heads)
     atts, probs = [None] * 4, [None] * 4
     for r in (3, 2, 1, 0):
-        length = {2: [grad_ffn[2]], 0: grad_ffn[1:]}.get(r, [])
+        length = {2: [grad_ffn[2]], 0: [grad_ffn[1]]}.get(r, [])
         length = after(lengths_all[r], *length) if length else lengths_all[r]
         atts[r], probs[r] = attn_fwd(length, packed, tiles, r)
     wouts = [wout, at.swap(wout, 1), wout_far, at.swap(after(wout_far, atts[1]), 1)]
@@ -1191,13 +1191,12 @@
         next(turns)
         sent = turns.send([p_back[1], smalls])
         p0 = after(p0, *sent)
-        up_full, down_full = join_ffn(n, ffn_all, quarter)
     grad_tokens = ln1_last(tokens, xhats[0], grad_middle, small, p0, p_near, *p_back)
 
     outs = [o0, at.swap(o1, 1), jnp.concatenate(out_back, axis=0)]
     if at.rings:
         next(turns)
-        sent = turns.send([grad_tokens, up_full])
+        sent = turns.send([grad_tokens])
         smalls, outs[0] = after(smalls, *sent), after(o0, *sent)
         pick = lambda i: lax.dynamic_index_in_dim(smalls, i, 0, keepdims=False)
         z_parts = [pick(at.z)] + [
@@ -1222,11 +1221,11 @@
         smalls = [jnp.pad(g, ((0, 0), (0, 0), (0, TILE - g.shape[2]))) for g in smalls]
         smalls = jnp.concatenate(smalls + [jnp.zeros((wide, 3, TILE), f32)], axis=1)
         smalls = lax.psum_scatter(smalls, "wide", scatter_dimension=0, tiled=True)[0]
-    smalls = smalls + at.swap(smalls, 2)
+    ffn_all[0] = after(ffn_all[0], attn_own)
+    up_full, down_full = join_ffn(n, ffn_all, quarter)
+    smalls = smalls + after(at.swap(smalls, 2), up_full)
     smalls = smalls + at.swap(smalls, 1)
 
-    if not at.rings:
-        up_full, down_full = join_ffn(n, ffn_all, quarter)
     qkv_full, out_full = join_attn(n, at.all_narrow(attn_own), model)
 
     return (

time: 354 us -> 351 us (level)
    unnamed x148 -> x154, local copies, waits for them, and re-layouts: 9.76 us -> 9.92 us
  transfers between devices with their start and end apart: 90 -> 90, of which waited for: 30 -> 31; matrix products, arithmetic and copies ran while one was open for 14% -> 14% of each run, Pallas kernels for 41% -> 41%
where the time goes in v4:
time: 351 us; the launch traced here: 345 us
  Pallas kernels  153 us (44%)
  starting transfers between devices  59.2 us (17%)
  waiting for transfers between devices  58.1 us (17%)
  matrix products  22.3 us (6%)
  local copies, waits for them, and re-layouts  19.9 us (6%)
  other arithmetic  16.6 us (5%)
  between operations  15.7 us (4%)
    pallas_call x3, Pallas kernels, ffn(): pl.pallas_call(functools.partial(ffn_kernel, len(norms), places, start, c...  37.6 us
    ppermute x64, starting transfers between devices, swap(): return lax.ppermute(x, 'narrow', [(i, i ^ bit) for i in range(self.narrow)])  31.6 us
    ppermute x64, waiting for transfers between devices, swap(): return lax.ppermute(x, 'narrow', [(i, i ^ bit) for i in range(self.narrow)])  26.9 us
    ppermute x21, waiting for transfers between devices, ring(): return lax.ppermute(x, ('narrow', 'wide'), pairs)  23.2 us
    dot_general x5, matrix products, dot(): return lax.dot_general(a, b, (dims, ((), ())), preferred_element_type=f32)  22.3 us
    ppermute x21, starting transfers between devices, ring(): return lax.ppermute(x, ('narrow', 'wide'), pairs)  22.1 us
    pallas_call x4, Pallas kernels, attn_bwd(): pl.pallas_call(attn_bwd_kernel, grid=(steps,), in_specs=[pl.BlockSpec((sl...  18.9 us
    pallas_call x4, Pallas kernels, attn_fwd(): pl.pallas_call(attn_fwd_kernel, grid=(heads // 2,), in_specs=[pl.BlockSpe...  17 us
  transfers between devices with their start and end apart: 90, of which 31 were waited for; matrix products, arithmetic and copies ran while one was open for 14% of the time, Pallas kernels for 41%

profile of v4, /device:TPU:0, one launch (start us, length us, event | category | flops | bytes accessed | tf_op | source)
XLA Modules:
  0.0 345.2 jit_solution(7016833850096129152)
XLA Ops:
  19.8 5.3 %collective-permute-done.refs_2_.refs_6_ = bf16[128,1152]{1,0:T(8,128)(2,1)S(1)} collective-permute-done((bf16[128,1152]{1,0:T(8,128)(2,1)}, bf16[128,1152]{1,0:T(8,128)(2,1)S(1)}, u32[]{:S(2)}, u32[]{:S(2)}) %collective-permute-start) | collective-permute-done | bytes 294944 | tf_op jit(solution)/shard_map/ppermute | solution.py:898
  27.3 6.7 %collective-permute-done.3.refs_4_.refs_8_ = bf16[128,1152]{1,0:T(8,128)(2,1)S(1)} collective-permute-done((bf16[128,1152]{1,0:T(8,128)(2,1)S(1)}, bf16[128,1152]{1,0:T(8,128)(2,1)S(1)}, u32[]{:S(2)}, u32[]{:S(2)}) %collective-permute-start.3) | collective-permute-done | bytes 294944 | tf_op jit(solution)/shard_map/ppermute | solution.py:898
  34.7 3.3 xhat.4.refs_0_.x0_ref.xhat_ref
  38.9 3.2 xhat.5.refs_1_.x1_ref
  44.2 7.1 %collective-permute-done.8.refs_6_.refs_10_ = bf16[128,1152]{1,0:T(8,128)(2,1)S(1)} collective-permute-done((bf16[128,1152]{1,0:T(8,128)(2,1)S(1)}, bf16[128,1152]{1,0:T(8,128)(2,1)S(1)}, u32[]{:S(2)}, u32[]{:S(2)}) %collective-permute-start.8) | collective-permute-done | bytes 294944 | tf_op jit(solution)/shard_map/ppermute | solution.py:898
  60.1 3.2 xhat.7.refs_3_.x1_ref
  63.3 3.1 xhat.6.refs_2_.x0_ref
  67.9 11.1 %qkv.1 = (bf16[2048,1024]{1,0:T(8,128)(2,1)}, bf16[2048,768]{1,0:T(8,128)(2,1)}, bf16[1024,768]{1,0:T(8,128)(2,1)}, bf16[1024,256]{1,0:T(8,128)(2,1)}) custom-call(s32[8]{0:T(128)} %stack.53.where_ref, f32[8,1024]{1,0:T(8,128)} %small_rows.1.small_ref, f32[512,1024]{1,0:T(8,128)} %xhat.4.refs_0_.x0_ref.xhat_ref, f32[512,1024]{1,0:T(8,128)} %xhat.5.refs_1_.x1_ref, ...), custom_call_target="tpu_custom_call" | custom-call | flops 402500000 | tf_op jit(solution)/shard_map/qkv/pallas_call | solution.py:246
  83.4 4.3 %attn_fwd.7 = (bf16[512,256]{1,0:T(8,128)(2,1)}, bf16[4,512,512]{2,1,0:T(8,128)(2,1)}) custom-call(s32[1]{0:T(128)} %collective-permute-done.11.len_ref, bf16[2048,768]{1,0:T(8,128)(2,1)} %get-tuple-element.173.qkv_ref, f32[4,4,128,128]{3,2,1,0:T(8,128)} %bias_tiles.1.tiles_ref), custom_call_target="tpu_custom_call" | custom-call | flops 517500000 | tf_op jit(solution)/shard_map/attn_fwd/pallas_call | solution.py:346
  88.1 4.4 %attn_fwd.5 = (bf16[512,256]{1,0:T(8,128)(2,1)}, bf16[4,512,512]{2,1,0:T(8,128)(2,1)}) custom-call(s32[1]{0:T(128)} %collective-permute-done.10.len_ref, bf16[2048,768]{1,0:T(8,128)(2,1)} %get-tuple-element.173.qkv_ref, f32[4,4,128,128]{3,2,1,0:T(8,128)} %bias_tiles.1.tiles_ref), custom_call_target="tpu_custom_call" | custom-call | flops 517500000 | tf_op jit(solution)/shard_map/attn_fwd/pallas_call | solution.py:346
  94.1 4.4 %attn_fwd.6 = (bf16[512,256]{1,0:T(8,128)(2,1)}, bf16[4,512,512]{2,1,0:T(8,128)(2,1)}) custom-call(s32[1]{0:T(128)} %collective-permute-done.5.len_ref, bf16[2048,768]{1,0:T(8,128)(2,1)} %get-tuple-element.173.qkv_ref, f32[4,4,128,128]{3,2,1,0:T(8,128)} %bias_tiles.1.tiles_ref), custom_call_target="tpu_custom_call" | custom-call | flops 517500000 | tf_op jit(solution)/shard_map/attn_fwd/pallas_call | solution.py:346
  100.4 6.9 %collective-permute-done.18.refs_2_ = bf16[512,256]{1,0:T(8,128)(2,1)S(1)} collective-permute-done((bf16[512,256]{1,0:T(8,128)(2,1)}, bf16[512,256]{1,0:T(8,128)(2,1)S(1)}, u32[]{:S(2)}, u32[]{:S(2)}) %collective-permute-start.18) | collective-permute-done | bytes 262176 | tf_op jit(solution)/shard_map/ppermute | solution.py:904
  107.4 3.9 %attn_fwd.4 = (bf16[512,256]{1,0:T(8,128)(2,1)}, bf16[4,512,512]{2,1,0:T(8,128)(2,1)}) custom-call(s32[1]{0:T(128)} %copy.64.len_ref, bf16[2048,768]{1,0:T(8,128)(2,1)} %get-tuple-element.173.qkv_ref, f32[4,4,128,128]{3,2,1,0:T(8,128)} %bias_tiles.1.tiles_ref), custom_call_target="tpu_custom_call" | custom-call | flops 517500000 | tf_op jit(solution)/shard_map/attn_fwd/pallas_call | solution.py:346
  112.2 3.9 %out_ln2.2 = (f32[512,1024]{1,0:T(8,128)}, bf16[512,1024]{1,0:T(8,128)(2,1)}, bf16[256,1024]{1,0:T(8,128)(2,1)}) custom-call(s32[1]{0:T(128)} %bitcast.n_ref, s32[1]{0:T(128)} %copy.64.len_ref, bf16[512,1024]{1,0:T(8,128)(2,1)} %tok_ref.5, f32[8,1024]{1,0:T(8,128)} %small_rows.1.small_ref, bf16[512,256]{1,0:T(8,128)(2,1)} %get-tuple-element.174.refs_0_.att_ref, ...), custom_call_target="tpu_custom_call" | custom-call | flops 71875000 | tf_op jit(solution)/shard_map/out_ln2/pallas_call | solution.py:510
  116.1 3.9 %out_ln2.3 = (f32[512,1024]{1,0:T(8,128)}, bf16[512,1024]{1,0:T(8,128)(2,1)}, bf16[256,1024]{1,0:T(8,128)(2,1)}) custom-call(s32[1]{0:T(128)} %bitcast.n_ref, s32[1]{0:T(128)} %copy.64.len_ref, bf16[512,1024]{1,0:T(8,128)(2,1)} %tok_ref.5, f32[8,1024]{1,0:T(8,128)} %small_rows.1.small_ref, ...), custom_call_target="tpu_custom_call", output_to_operand_aliasing={{0}: (12, {}), {1}: (13, {})} | custom-call | flops 71875000 | tf_op jit(solution)/shard_map/out_ln2/pallas_call | solution.py:510
  125.8 16.6 %ffn.3 = (f32[512,1024]{1,0:T(8,128)}, f32[512,1024]{1,0:T(8,128)}, bf16[512,1024]{1,0:T(8,128)(2,1)}, bf16[128,1024]{1,0:T(8,128)(2,1)}, bf16[128,1024]{1,0:T(8...) custom-call(bf16[8,2,128,1024]{3,2,1,0:T(8,128)(2,1)} %bitcast.118, ...), custom_call_target="tpu_custom_call" | custom-call | flops 215624992 | tf_op jit(solution)/shard_map/ffn/pallas_call | solution.py:701
  146.3 10.5 %ffn.4 = (f32[256,1024]{1,0:T(8,128)}, f32[256,1024]{1,0:T(8,128)}, bf16[256,1024]{1,0:T(8,128)(2,1)}, bf16[64,1024]{1,0:T(8,128)(2,1)}, bf16[64,1024]{1,0:T(8,1...) custom-call(bf16[8,2,128,1024]{3,2,1,0:T(8,128)(2,1)} %bitcast.119, ...), custom_call_target="tpu_custom_call", output_to_operand_aliasing={{7}: (8, {}), {8}: (9, {}), {9}: (10, {}), {10}: (11, {})} | custom-call | flops 143750000 | tf_op jit(solution)/shard_map/ffn/pallas_call | solution.py:701
  163.0 10.5 %ffn.5 = (f32[256,1024]{1,0:T(8,128)}, f32[256,1024]{1,0:T(8,128)}, bf16[256,1024]{1,0:T(8,128)(2,1)}, bf16[64,1024]{1,0:T(8,128)(2,1)}, bf16[64,1024]{1,0:T(8,1...) custom-call(bf16[8,2,128,1024]{3,2,1,0:T(8,128)(2,1)} %bitcast.120, ...), custom_call_target="tpu_custom_call", output_to_operand_aliasing={{7}: (8, {}), {8}: (9, {}), {9}: (10, {}), {10}: (11, {})} | custom-call | flops 143750000 | tf_op jit(solution)/shard_map/ffn/pallas_call | solution.py:701
  178.2 8.2 %convolution_convert_fusion.1 = bf16[1024,1024]{1,0:T(8,128)(2,1)S(1)} fusion(bf16[2048,1024]{1,0:T(8,128)(2,1)} %get-tuple-element.226, bf16[2048,1024]{1,0:T(8,128)(2,1)} %get-tuple-element.228), kind=kOutput, calls=%fused_computation.5 | convolution fusion | flops 4296015872 | bytes 10485760 | tf_op jit(solution)/shard_map/dot_general | solution.py:32
  186.4 5.0 %convolution_convert_fusion = bf16[1024,1024]{1,0:T(8,128)(2,1)S(1)} fusion(bf16[2048,1024]{1,0:T(8,128)(2,1)S(1)} %copy-done.2, bf16[2048,1024]{1,0:T(8,128)(2,1)S(1)} %copy-done.1), kind=kOutput, calls=%fused_computation.4 | convolution fusion | flops 4296015872 | bytes 10485760 | tf_op jit(solution)/shard_map/dot_general | solution.py:32
  195.2 5.1 %ln2_back.2 = (f32[512,1024]{1,0:T(8,128)}, bf16[512,512]{1,0:T(8,128)(2,1)}, bf16[512,512]{1,0:T(8,128)(2,1)}, bf16[512,256]{1,0:T(8,128)(2,1)}, bf16[512,256]{...) custom-call(s32[1]{0:T(128)} %bitcast.n_ref, s32[1]{0:T(128)} %copy.64.len_ref, ...), custom_call_target="tpu_custom_call" | custom-call | flops 5750000128 | tf_op jit(solution)/shard_map/ln2_back/pallas_call | solution.py:569
  201.2 5.2 %ln2_back.3 = (f32[512,1024]{1,0:T(8,128)}, bf16[512,512]{1,0:T(8,128)(2,1)}, bf16[512,512]{1,0:T(8,128)(2,1)}, bf16[512,256]{1,0:T(8,128)(2,1)}, bf16[512,256]{...) custom-call(s32[1]{0:T(128)} %bitcast.n_ref, ...), custom_call_target="tpu_custom_call", output_to_operand_aliasing={{0}: (13, {}), {1}: (14, {}), {2}: (15, {}), {3}: (16, {}),... | custom-call | flops 5750000128 | tf_op jit(solution)/shard_map/ln2_back/pallas_call | solution.py:569
  210.3 4.7 %attn_bwd.4 = (bf16[2048,768]{1,0:T(8,128)(2,1)}, f32[2,2,512]{2,1,0:T(2,128)}) custom-call(bf16[2048,768]{1,0:T(8,128)(2,1)} %get-tuple-element.173.qkv_ref, bf16[512,256]{1,0:T(8,128)(2,1)} %get-tuple-element.234.ga_ref, bf16[512,256]{1,0:T(8,128)(2,1)} %get-tuple-element.174.refs_0_.att_ref, bf16[4,512,512]{2,1,0:T(8,128)(2,1)} %get-tuple-element.235.p_ref), custom_call_target="tpu_custom_call" | custom-call | flops 1150000000 | tf_op jit(solution)/shard_map/attn_bwd/pallas_call | solution.py:431
  227.5 5.0 %attn_bwd.5 = (bf16[2048,768]{1,0:T(8,128)(2,1)}, f32[2,2,512]{2,1,0:T(2,128)}) custom-call(bf16[2048,768]{1,0:T(8,128)(2,1)} %get-tuple-element.173.qkv_ref, bf16[512,256]{1,0:T(8,128)(2,1)} %copy-done.48, bf16[512,256]{1,0:T(8,128)(2,1)} %get-tuple-element.177.att_ref, ...), custom_call_target="tpu_custom_call", output_to_operand_aliasing={{0}: (4, {})} | custom-call | flops 1150000000 | tf_op jit(solution)/shard_map/attn_bwd/pallas_call | solution.py:431
  232.8 4.6 %attn_bwd.6 = (bf16[2048,768]{1,0:T(8,128)(2,1)}, f32[2,2,512]{2,1,0:T(2,128)}) custom-call(bf16[2048,768]{1,0:T(8,128)(2,1)} %get-tuple-element.173.qkv_ref, bf16[512,256]{1,0:T(8,128)(2,1)} %copy-done.47, bf16[512,256]{1,0:T(8,128)(2,1)} %get-tuple-element.178.att_ref, ...), custom_call_target="tpu_custom_call", output_to_operand_aliasing={{0}: (4, {})} | custom-call | flops 1150000000 | tf_op jit(solution)/shard_map/attn_bwd/pallas_call | solution.py:431
  238.7 7.3 %ln1_back.2 = (bf16[512,1024]{1,0:T(8,128)(2,1)}, bf16[512,1024]{1,0:T(8,128)(2,1)}, f32[2,1024]{1,0:T(2,128)}) custom-call(bf16[2048,768]{1,0:T(8,128)(2,1)} %get-tuple-element.254.gp_ref.refs_0_, bf16[1024,768]{1,0:T(8,128)(2,1)} %get-tuple-element.255.wq_ref, f32[512,1024]{1,0:T(8,128)} %xhat.6.refs_2_.x0_ref, f32[512,1024]{1,0:T(8,128)} %xhat.7.refs_3_.x1_ref), custom_call_target="tpu_custom_call" | custom-call | flops 575000000 | tf_op jit(solution)/shard_map/ln1_back/pallas_call | solution.py:291
  250.3 4.6 %attn_bwd.7 = (bf16[2048,768]{1,0:T(8,128)(2,1)}, f32[2,2,512]{2,1,0:T(2,128)}) custom-call(bf16[2048,768]{1,0:T(8,128)(2,1)} %get-tuple-element.173.qkv_ref, bf16[512,256]{1,0:T(8,128)(2,1)} %copy-done.49, bf16[512,256]{1,0:T(8,128)(2,1)} %get-tuple-element.175.att_ref, ...), custom_call_target="tpu_custom_call", output_to_operand_aliasing={{0}: (4, {})} | custom-call | flops 1150000000 | tf_op jit(solution)/shard_map/attn_bwd/pallas_call | solution.py:431
  258.8 6.7 %convolution_convert_fusion.2 = bf16[1024,768]{1,0:T(8,128)(2,1)S(1)} fusion(bf16[2048,1024]{1,0:T(8,128)(2,1)} %get-tuple-element.188, bf16[2048,768]{1,0:T(8,128)(2,1)} %get-tuple-element.261.gp_ref), kind=kOutput, calls=%fused_computation.6 | convolution fusion | flops 3222011904 | bytes 8912896 | tf_op jit(solution)/shard_map/dot_general | solution.py:32
  272.4 7.8 %ln1_back.3 = (f32[512,1024]{1,0:T(8,128)}, bf16[512,1024]{1,0:T(8,128)(2,1)}, f32[2,1024]{1,0:T(2,128)}) custom-call(bf16[2048,768]{1,0:T(8,128)(2,1)} %get-tuple-element.261.gp_ref, bf16[1024,768]{1,0:T(8,128)(2,1)} %get-tuple-element.255.wq_ref, f32[512,1024]{1,0:T(8,128)} %xhat.4.refs_0_.x0_ref.xhat_ref, f32[512,1024]{1,0:T(8,128)} %xhat.5.refs_1_.x1_ref), custom_call_target="tpu_custom_call" | custom-call | flops 5750000128 | tf_op jit(solution)/shard_map/ln1_back/pallas_call | solution.py:291
  289.9 5.2 %collective-permute-done.71 = f32[4,8,128]{2,1,0:T(8,128)S(1)} collective-permute-done((f32[4,8,128]{2,1,0:T(8,128)}, f32[4,8,128]{2,1,0:T(8,128)S(1)}, u32[]{:S(2)}, u32[]{:S(2)}) %collective-permute-start.71) | collective-permute-done | bytes 16416 | tf_op jit(solution)/shard_map/ppermute | solution.py:911
  302.1 5.8 %ln1_last.1 = f32[512,1024]{1,0:T(8,128)} custom-call(bf16[512,1024]{1,0:T(8,128)(2,1)} %tok_ref.5, f32[512,1024]{1,0:T(8,128)} %xhat.4.refs_0_.x0_ref.xhat_ref, f32[512,1024]{1,0:T(8,128)} %get-tuple-element.282.gmid_ref, f32[8,1024]{1,0:T(8,128)} %small_rows.1.small_ref, f32[512,1024]{1,0:T(8,128)} %get-tuple-element.284.p0_ref, ...), custom_call_target="tpu_custom_call" | custom-call | flops 287500000 | tf_op jit(solution)/shard_map/ln1_last/pallas_call | solution.py:472
  324.9 3.9 %join_ffn.1 = (f32[128,4096]{1,0:T(8,128)}, f32[512,1024]{1,0:T(8,128)}) custom-call(s32[1]{0:T(128)} %bitcast.n_ref, bf16[128,2048]{1,0:T(8,128)(2,1)} %copy-done.8, bf16[128,2048]{1,0:T(8,128)(2,1)} %copy-done.27, bf16[128,2048]{1,0:T(8,128)(2,1)} %copy-done.24, bf16[128,2048]{1,0:T(8,128)(2,1)} %copy-done.30), custom_call_target="tpu_custom_call" | custom-call | flops 230000000 | tf_op jit(solution)/shard_map/join_ffn/pallas_call | solution.py:820
  (383 shorter events, 138.2 us)
Async XLA Ops:
  7.2 118.6 %all-gather.3.cloned.1.call-start = ((), (), s32[]{:S(2)}) async-start(), calls=%async_computation | async-start | bytes 4718592 | tf_op jit(solution)/shard_map/all_gather | solution.py:1070
  7.2 30.7 %collective-permute-start.7 = (bf16[512,1024]{1,0:T(8,128)(2,1)}, bf16[512,1024]{1,0:T(8,128)(2,1)S(1)}, u32[]{:S(2)}, u32[]{:S(2)}) collective-permute-start(bf16[512,1024]{1,0:T(8,128)(2,1)} %tok_ref.5), channel_id=1, source_target_pairs={{0,8},{8,0},{16,24},{24,16},{1,9},{9,1},{17,25},{25,17},{2,10},{10... | collective-permute-start | bytes 3145736 | tf_op jit(solution)/shard_map/ppermute | solution.py:904
  8.8 16.4 %collective-permute-start.2 = (bf16[224,1024]{1,0:T(8,128)(2,1)S(1)}, bf16[224,1024]{1,0:T(8,128)(2,1)}, u32[]{:S(2)}, u32[]{:S(2)}) collective-permute-start(bf16[224,1024]{1,0:T(8,128)(2,1)S(1)} %slice.51), channel_id=1, source_target_pairs={{0,16},{8,24},{16,0},{24,8},{1,17},{9,25},{17,1},{25,9},{2,18},{10... | collective-permute-start | bytes 1376264 | tf_op jit(solution)/shard_map/ppermute | solution.py:904
  17.5 24.6 %collective-permute-start.6 = (bf16[288,1024]{1,0:T(8,128)(2,1)S(1)}, bf16[288,1024]{1,0:T(8,128)(2,1)}, u32[]{:S(2)}, u32[]{:S(2)}) collective-permute-start(bf16[288,1024]{1,0:T(8,128)(2,1)S(1)} %slice.52), channel_id=1, source_target_pairs={{0,16},{8,24},{16,0},{24,8},{1,17},{9,25},{17,1},{25,9},{2,18},{10... | collective-permute-start | bytes 1769480 | tf_op jit(solution)/shard_map/ppermute | solution.py:904
  27.2 14.9 %collective-permute-start.5 = (s32[1]{0:T(128)}, s32[1]{0:T(128)}, u32[]{:S(2)}, u32[]{:S(2)}) collective-permute-start(s32[1]{0:T(128)} %param.14), channel_id=1, source_target_pairs={{0,16},{8,24},{16,0},{24,8},{1,17},{9,25},{17,1},{25,9},{2,18},{10... | collective-permute-start | bytes 20 | tf_op jit(solution)/shard_map/ppermute | solution.py:904
  53.9 34.2 %collective-permute-start.17 = (bf16[512,1024]{1,0:T(8,128)(2,1)S(1)}, bf16[512,1024]{1,0:T(8,128)(2,1)S(1)}, u32[]{:S(2)}, u32[]{:S(2)}) collective-permute-start(bf16[512,1024]{1,0:T(8,128)(2,1)S(1)} %multiply_convert_fusion.refs_4_), channel_id=1, source_target_pairs={{0,16},{8,24},{16,0},{24,8},{1,17},{9,25},{17,1},{25,9},{2,18},{10... | collective-permute-start | bytes 3145736 | tf_op jit(solution)/shard_map/ppermute | solution.py:904
  58.5 63.7 %collective-permute-start.13 = (bf16[512,1024]{1,0:T(8,128)(2,1)S(1)}, bf16[512,1024]{1,0:T(8,128)(2,1)}, u32[]{:S(2)}, u32[]{:S(2)}) collective-permute-start(bf16[512,1024]{1,0:T(8,128)(2,1)S(1)} %multiply_convert_fusion.refs_4_), channel_id=1, source_target_pairs={{0,8},{8,0},{16,24},{24,16},{1,9},{9,1},{17,25},{25,17},{2,10},{10... | collective-permute-start | bytes 3145736 | tf_op jit(solution)/shard_map/ppermute | solution.py:904
  79.0 15.1 %collective-permute-start.21 = (bf16[1024,256]{1,0:T(8,128)(2,1)}, bf16[1024,256]{1,0:T(8,128)(2,1)}, u32[]{:S(2)}, u32[]{:S(2)}) collective-permute-start(bf16[1024,256]{1,0:T(8,128)(2,1)} %get-tuple-element.179.refs_4_.refs_2_), channel_id=1, source_target_pairs={{0,16},{8,24},{16,0},{24,8},{1,17},{9,25},{17,1},{25,9},{2,18},{10... | collective-permute-start | bytes 1572872 | tf_op jit(solution)/shard_map/ppermute | solution.py:904
  80.8 30.5 %collective-permute-start.20 = (bf16[1024,256]{1,0:T(8,128)(2,1)}, bf16[1024,256]{1,0:T(8,128)(2,1)}, u32[]{:S(2)}, u32[]{:S(2)}) collective-permute-start(bf16[1024,256]{1,0:T(8,128)(2,1)} %get-tuple-element.179.refs_4_.refs_2_), channel_id=1, source_target_pairs={{0,8},{8,0},{16,24},{24,16},{1,9},{9,1},{17,25},{25,17},{2,10},{10... | collective-permute-start | bytes 1572872 | tf_op jit(solution)/shard_map/ppermute | solution.py:904
  94.1 17.2 %collective-permute-start.22 = (bf16[1024,256]{1,0:T(8,128)(2,1)}, bf16[1024,256]{1,0:T(8,128)(2,1)S(1)}, u32[]{:S(2)}, u32[]{:S(2)}) collective-permute-start(bf16[1024,256]{1,0:T(8,128)(2,1)} %collective-permute-done.21.refs_6_.refs_4_), channel_id=1, source_target_pairs={{0,8},{8,0},{16,24},{24,16},{1,9},{9,1},{17,25},{25,17},{2,10},{10... | collective-permute-start | bytes 1572872 | tf_op jit(solution)/shard_map/ppermute | solution.py:904
  107.4 36.8 %collective-permute-start.31 = (bf16[512,1024]{1,0:T(8,128)(2,1)S(1)}, bf16[512,1024]{1,0:T(8,128)(2,1)S(1)}, u32[]{:S(2)}, u32[]{:S(2)}) collective-permute-start(bf16[512,1024]{1,0:T(8,128)(2,1)S(1)} %collective-permute-done.17.refs_5_), channel_id=1, source_target_pairs={{0,8},{8,0},{16,24},{24,16},{1,9},{9,1},{17,25},{25,17},{2,10},{10... | collective-permute-start | bytes 3145736 | tf_op jit(solution)/shard_map/ppermute | solution.py:904
  120.5 21.9 %collective-permute-start.26 = (bf16[256,1024]{1,0:T(8,128)(2,1)}, bf16[256,1024]{1,0:T(8,128)(2,1)}, u32[]{:S(2)}, u32[]{:S(2)}) collective-permute-start(bf16[256,1024]{1,0:T(8,128)(2,1)} %get-tuple-element.185.refs_0_), channel_id=1, source_target_pairs={{0,16},{8,24},{16,0},{24,8},{1,17},{9,25},{17,1},{25,9},{2,18},{10... | collective-permute-start | bytes 1572872 | tf_op jit(solution)/shard_map/ppermute | solution.py:904
  122.2 35.7 %collective-permute-start.25 = (bf16[256,1024]{1,0:T(8,128)(2,1)}, bf16[256,1024]{1,0:T(8,128)(2,1)S(1)}, u32[]{:S(2)}, u32[]{:S(2)}) collective-permute-start(bf16[256,1024]{1,0:T(8,128)(2,1)} %get-tuple-element.186.refs_1_), channel_id=1, source_target_pairs={{0,16},{8,24},{16,0},{24,8},{1,17},{9,25},{17,1},{25,9},{2,18},{10... | collective-permute-start | bytes 1572872 | tf_op jit(solution)/shard_map/ppermute | solution.py:904
  160.6 16.9 %collective-permute-start.47 = (bf16[256,1024]{1,0:T(8,128)(2,1)S(1)}, bf16[256,1024]{1,0:T(8,128)(2,1)S(1)}, u32[]{:S(2)}, u32[]{:S(2)}) collective-permute-start(bf16[256,1024]{1,0:T(8,128)(2,1)S(1)} %add_convert_fusion.12), channel_id=1, source_target_pairs={{0,16},{8,24},{16,0},{24,8},{1,17},{9,25},{17,1},{25,9},{2,18},{10... | collective-permute-start | bytes 1572872 | tf_op jit(solution)/shard_map/ppermute | solution.py:904
  175.1 17.9 %collective-permute-start.48 = (bf16[128,1024]{1,0:T(8,128)(2,1)S(1)}, bf16[128,1024]{1,0:T(8,128)(2,1)S(1)}, u32[]{:S(2)}, u32[]{:S(2)}) collective-permute-start(bf16[128,1024]{1,0:T(8,128)(2,1)S(1)} %copy-done.70), channel_id=1, source_target_pairs={{0,8},{8,0},{16,24},{24,16},{1,9},{9,1},{17,25},{25,17},{2,10},{10... | collective-permute-start | bytes 786440 | tf_op jit(solution)/shard_map/ppermute | solution.py:904
  175.3 18.4 %collective-permute-start.49 = (bf16[128,1024]{1,0:T(8,128)(2,1)S(1)}, bf16[128,1024]{1,0:T(8,128)(2,1)S(1)}, u32[]{:S(2)}, u32[]{:S(2)}) collective-permute-start(bf16[128,1024]{1,0:T(8,128)(2,1)S(1)} %copy-done.69), channel_id=1, source_target_pairs={{0,8},{8,0},{16,24},{24,16},{1,9},{9,1},{17,25},{25,17},{2,10},{10... | collective-permute-start | bytes 786440 | tf_op jit(solution)/shard_map/ppermute | solution.py:904
  175.7 24.6 %collective-permute-start.45 = (bf16[128,1024]{1,0:T(8,128)(2,1)S(1)}, bf16[128,1024]{1,0:T(8,128)(2,1)S(1)}, u32[]{:S(2)}, u32[]{:S(2)}) collective-permute-start(bf16[128,1024]{1,0:T(8,128)(2,1)S(1)} %copy-done.68), channel_id=1, source_target_pairs={{0,8},{8,0},{16,24},{24,16},{1,9},{9,1},{17,25},{25,17},{2,10},{10... | collective-permute-start | bytes 786440 | tf_op jit(solution)/shard_map/ppermute | solution.py:904
  175.8 24.4 %collective-permute-start.46 = (bf16[128,1024]{1,0:T(8,128)(2,1)S(1)}, bf16[128,1024]{1,0:T(8,128)(2,1)S(1)}, u32[]{:S(2)}, u32[]{:S(2)}) collective-permute-start(bf16[128,1024]{1,0:T(8,128)(2,1)S(1)} %copy-done.67), channel_id=1, source_target_pairs={{0,8},{8,0},{16,24},{24,16},{1,9},{9,1},{17,25},{25,17},{2,10},{10... | collective-permute-start | bytes 786440 | tf_op jit(solution)/shard_map/ppermute | solution.py:904
  177.6 22.7 %collective-permute-start.44 = (bf16[256,1024]{1,0:T(8,128)(2,1)S(1)}, bf16[256,1024]{1,0:T(8,128)(2,1)S(1)}, u32[]{:S(2)}, u32[]{:S(2)}) collective-permute-start(bf16[256,1024]{1,0:T(8,128)(2,1)S(1)} %add_convert_fusion.11), channel_id=1, source_target_pairs={{0,16},{8,24},{16,0},{24,8},{1,17},{9,25},{17,1},{25,9},{2,18},{10... | collective-permute-start | bytes 1572872 | tf_op jit(solution)/shard_map/ppermute | solution.py:904
  193.1 14.8 %collective-permute-start.53 = (bf16[128,2048]{1,0:T(8,128)(2,1)S(1)}, bf16[128,2048]{1,0:T(8,128)(2,1)S(1)}, u32[]{:S(2)}, u32[]{:S(2)}) collective-permute-start(bf16[128,2048]{1,0:T(8,128)(2,1)S(1)} %pad_maximum_fusion.1), channel_id=1, source_target_pairs={{2,0},{4,2},{6,4},{7,6},{5,7},{3,5},{1,3},{0,1},{9,8},{8,10},{10,1... | collective-permute-start | bytes 1572872 | tf_op jit(solution)/shard_map/ppermute | solution.py:898
  193.7 14.2 %collective-permute-start.52 = (bf16[128,2048]{1,0:T(8,128)(2,1)S(1)}, bf16[128,2048]{1,0:T(8,128)(2,1)S(1)}, u32[]{:S(2)}, u32[]{:S(2)}) collective-permute-start(bf16[128,2048]{1,0:T(8,128)(2,1)S(1)} %pad_maximum_fusion), channel_id=1, source_target_pairs={{0,2},{2,4},{4,6},{6,7},{7,5},{5,3},{3,1},{1,0},{8,9},{10,8},{12,1... | collective-permute-start | bytes 1572872 | tf_op jit(solution)/shard_map/ppermute | solution.py:898
  208.1 14.5 %collective-permute-start.57 = (bf16[128,2048]{1,0:T(8,128)(2,1)S(1)}, bf16[128,2048]{1,0:T(8,128)(2,1)S(1)}, u32[]{:S(2)}, u32[]{:S(2)}) collective-permute-start(bf16[128,2048]{1,0:T(8,128)(2,1)S(1)} %add_convert_fusion.9), channel_id=1, source_target_pairs={{2,0},{4,2},{6,4},{7,6},{5,7},{3,5},{1,3},{0,1},{9,8},{8,10},{10,1... | collective-permute-start | bytes 1572872 | tf_op jit(solution)/shard_map/ppermute | solution.py:898
  208.8 13.8 %collective-permute-start.56 = (bf16[128,2048]{1,0:T(8,128)(2,1)S(1)}, bf16[128,2048]{1,0:T(8,128)(2,1)S(1)}, u32[]{:S(2)}, u32[]{:S(2)}) collective-permute-start(bf16[128,2048]{1,0:T(8,128)(2,1)S(1)} %add_convert_fusion.10), channel_id=1, source_target_pairs={{0,2},{2,4},{4,6},{6,7},{7,5},{5,3},{3,1},{1,0},{8,9},{10,8},{12,1... | collective-permute-start | bytes 1572872 | tf_op jit(solution)/shard_map/ppermute | solution.py:898
  222.8 14.8 %collective-permute-start.61 = (bf16[128,2048]{1,0:T(8,128)(2,1)S(1)}, bf16[128,2048]{1,0:T(8,128)(2,1)S(1)}, u32[]{:S(2)}, u32[]{:S(2)}) collective-permute-start(bf16[128,2048]{1,0:T(8,128)(2,1)S(1)} %add_convert_fusion.6), channel_id=1, source_target_pairs={{2,0},{4,2},{6,4},{7,6},{5,7},{3,5},{1,3},{0,1},{9,8},{8,10},{10,1... | collective-permute-start | bytes 1572872 | tf_op jit(solution)/shard_map/ppermute | solution.py:898
  223.5 14.0 %collective-permute-start.60 = (bf16[128,2048]{1,0:T(8,128)(2,1)S(1)}, bf16[128,2048]{1,0:T(8,128)(2,1)S(1)}, u32[]{:S(2)}, u32[]{:S(2)}) collective-permute-start(bf16[128,2048]{1,0:T(8,128)(2,1)S(1)} %add_convert_fusion.7), channel_id=1, source_target_pairs={{0,2},{2,4},{4,6},{6,7},{7,5},{5,3},{3,1},{1,0},{8,9},{10,8},{12,1... | collective-permute-start | bytes 1572872 | tf_op jit(solution)/shard_map/ppermute | solution.py:898
  225.2 13.5 %collective-permute-start.59 = (bf16[256,1024]{1,0:T(8,128)(2,1)S(1)}, bf16[256,1024]{1,0:T(8,128)(2,1)S(1)}, u32[]{:S(2)}, u32[]{:S(2)}) collective-permute-start(bf16[256,1024]{1,0:T(8,128)(2,1)S(1)} %add_convert_fusion.8), channel_id=1, source_target_pairs={{0,16},{8,24},{16,0},{24,8},{1,17},{9,25},{17,1},{25,9},{2,18},{10... | collective-permute-start | bytes 1572872 | tf_op jit(solution)/shard_map/ppermute | solution.py:904
  257.5 13.6 %collective-permute-start.65 = (bf16[256,1024]{1,0:T(8,128)(2,1)S(1)}, bf16[256,1024]{1,0:T(8,128)(2,1)}, u32[]{:S(2)}, u32[]{:S(2)}) collective-permute-start(bf16[256,1024]{1,0:T(8,128)(2,1)S(1)} %get-tuple-element.336), channel_id=1, source_target_pairs={{0,16},{8,24},{16,0},{24,8},{1,17},{9,25},{17,1},{25,9},{2,18},{10... | collective-permute-start | bytes 1572872 | tf_op jit(solution)/shard_map/ppermute | solution.py:904
  266.4 15.8 %collective-permute-start.64 = (bf16[128,1280]{1,0:T(8,128)(2,1)}, bf16[128,1280]{1,0:T(8,128)(2,1)}, u32[]{:S(2)}, u32[]{:S(2)}) collective-permute-start(bf16[128,1280]{1,0:T(8,128)(2,1)} %pad_maximum_fusion.3), channel_id=1, source_target_pairs={{2,0},{4,2},{6,4},{7,6},{5,7},{3,5},{1,3},{0,1},{9,8},{8,10},{10,1... | collective-permute-start | bytes 983048 | tf_op jit(solution)/shard_map/ppermute | solution.py:898
  267.9 14.3 %collective-permute-start.63 = (bf16[128,1280]{1,0:T(8,128)(2,1)}, bf16[128,1280]{1,0:T(8,128)(2,1)}, u32[]{:S(2)}, u32[]{:S(2)}) collective-permute-start(bf16[128,1280]{1,0:T(8,128)(2,1)} %pad_maximum_fusion.2), channel_id=1, source_target_pairs={{0,2},{2,4},{4,6},{6,7},{7,5},{5,3},{3,1},{1,0},{8,9},{10,8},{12,1... | collective-permute-start | bytes 983048 | tf_op jit(solution)/shard_map/ppermute | solution.py:898
  289.9 20.8 %collective-permute-start.75 = (bf16[512,1024]{1,0:T(8,128)(2,1)}, bf16[512,1024]{1,0:T(8,128)(2,1)S(1)}, u32[]{:S(2)}, u32[]{:S(2)}) collective-permute-start(bf16[512,1024]{1,0:T(8,128)(2,1)} %get-tuple-element.288), channel_id=1, source_target_pairs={{0,8},{8,0},{16,24},{24,16},{1,9},{9,1},{17,25},{25,17},{2,10},{10... | collective-permute-start | bytes 3145736 | tf_op jit(solution)/shard_map/ppermute | solution.py:904
  301.3 22.0 %collective-permute-start.83 = (bf16[128,2048]{1,0:T(8,128)(2,1)S(1)}, bf16[128,2048]{1,0:T(8,128)(2,1)S(1)}, u32[]{:S(2)}, u32[]{:S(2)}) collective-permute-start(bf16[128,2048]{1,0:T(8,128)(2,1)S(1)} %add_convert_fusion.4.refs_0_), channel_id=1, source_target_pairs={{0,8},{8,0},{16,24},{24,16},{1,9},{9,1},{17,25},{25,17},{2,10},{10... | collective-permute-start | bytes 1572872 | tf_op jit(solution)/shard_map/ppermute | solution.py:904
  301.4 14.4 %collective-permute-start.77 = (bf16[256,1024]{1,0:T(8,128)(2,1)S(1)}, bf16[256,1024]{1,0:T(8,128)(2,1)}, u32[]{:S(2)}, u32[]{:S(2)}) collective-permute-start(bf16[256,1024]{1,0:T(8,128)(2,1)S(1)} %add_convert_fusion.3), channel_id=1, source_target_pairs={{0,16},{8,24},{16,0},{24,8},{1,17},{9,25},{17,1},{25,9},{2,18},{10... | collective-permute-start | bytes 1572872 | tf_op jit(solution)/shard_map/ppermute | solution.py:904
  (135 other events, 837.5 us)
Sparse Core Ops, SparseCore 0:
  51.9 73.8 all-gather.2

commit v5 on v4

--- a/solution.py
+++ b/solution.py
@@ -1080,7 +1080,7 @@
     tiles = bias_tiles(n, small, buckets, heads)
     atts, probs = [None] * 4, [None] * 4
     for r in (3, 2, 1, 0):
-        length = {2: [grad_ffn[2]], 0: [grad_ffn[1]]}.get(r, [])
+        length = {1: [grad_ffn[2]], 0: [grad_ffn[1]]}.get(r, [])
         length = after(lengths_all[r], *length) if length else lengths_all[r]
         atts[r], probs[r] = attn_fwd(length, packed, tiles, r)
     wouts = [wout, at.swap(wout, 1), wout_far, at.swap(after(wout_far, atts[1]), 1)]

time: 351 us -> 351 us (level)
  no operation moved by 1% of the time
where the time goes in v5:
time: 351 us; the launch traced here: 345 us
  Pallas kernels  153 us (44%)
  starting transfers between devices  59.3 us (17%)
  waiting for transfers between devices  58.1 us (17%)
  matrix products  22.3 us (6%)
  local copies, waits for them, and re-layouts  19.9 us (6%)
  other arithmetic  16.6 us (5%)
  between operations  15.7 us (4%)
    pallas_call x3, Pallas kernels, ffn(): pl.pallas_call(functools.partial(ffn_kernel, len(norms), places, start, c...  37.6 us
    ppermute x64, starting transfers between devices, swap(): return lax.ppermute(x, 'narrow', [(i, i ^ bit) for i in range(self.narrow)])  31.6 us
    ppermute x64, waiting for transfers between devices, swap(): return lax.ppermute(x, 'narrow', [(i, i ^ bit) for i in range(self.narrow)])  26.9 us
    ppermute x21, waiting for transfers between devices, ring(): return lax.ppermute(x, ('narrow', 'wide'), pairs)  23.2 us
    dot_general x5, matrix products, dot(): return lax.dot_general(a, b, (dims, ((), ())), preferred_element_type=f32)  22.3 us
    ppermute x21, starting transfers between devices, ring(): return lax.ppermute(x, ('narrow', 'wide'), pairs)  22.1 us
    pallas_call x4, Pallas kernels, attn_bwd(): pl.pallas_call(attn_bwd_kernel, grid=(steps,), in_specs=[pl.BlockSpec((sl...  18.9 us
    pallas_call x4, Pallas kernels, attn_fwd(): pl.pallas_call(attn_fwd_kernel, grid=(heads // 2,), in_specs=[pl.BlockSpe...  17 us
  transfers between devices with their start and end apart: 90, of which 31 were waited for; matrix products, arithmetic and copies ran while one was open for 14% of the time, Pallas kernels for 41%

profile of v5, /device:TPU:0, one launch (start us, length us, event | category | flops | bytes accessed | tf_op | source)
XLA Modules:
  0.0 345.2 jit_solution(1561287572572687386)
XLA Ops:
  19.8 5.3 %collective-permute-done.refs_2_.refs_6_ = bf16[128,1152]{1,0:T(8,128)(2,1)S(1)} collective-permute-done((bf16[128,1152]{1,0:T(8,128)(2,1)}, bf16[128,1152]{1,0:T(8,128)(2,1)S(1)}, u32[]{:S(2)}, u32[]{:S(2)}) %collective-permute-start) | collective-permute-done | bytes 294944 | tf_op jit(solution)/shard_map/ppermute | solution.py:898
  27.3 6.7 %collective-permute-done.3.refs_4_.refs_8_ = bf16[128,1152]{1,0:T(8,128)(2,1)S(1)} collective-permute-done((bf16[128,1152]{1,0:T(8,128)(2,1)S(1)}, bf16[128,1152]{1,0:T(8,128)(2,1)S(1)}, u32[]{:S(2)}, u32[]{:S(2)}) %collective-permute-start.3) | collective-permute-done | bytes 294944 | tf_op jit(solution)/shard_map/ppermute | solution.py:898
  34.7 3.3 xhat.4.refs_0_.x0_ref.xhat_ref
  38.9 3.2 xhat.5.refs_1_.x1_ref
  44.2 7.1 %collective-permute-done.8.refs_6_.refs_10_ = bf16[128,1152]{1,0:T(8,128)(2,1)S(1)} collective-permute-done((bf16[128,1152]{1,0:T(8,128)(2,1)S(1)}, bf16[128,1152]{1,0:T(8,128)(2,1)S(1)}, u32[]{:S(2)}, u32[]{:S(2)}) %collective-permute-start.8) | collective-permute-done | bytes 294944 | tf_op jit(solution)/shard_map/ppermute | solution.py:898
  60.1 3.2 xhat.7.refs_3_.x1_ref
  63.3 3.1 xhat.6.refs_2_.x0_ref
  67.9 11.1 %qkv.1 = (bf16[2048,1024]{1,0:T(8,128)(2,1)}, bf16[2048,768]{1,0:T(8,128)(2,1)}, bf16[1024,768]{1,0:T(8,128)(2,1)}, bf16[1024,256]{1,0:T(8,128)(2,1)}) custom-call(s32[8]{0:T(128)} %stack.53.where_ref, f32[8,1024]{1,0:T(8,128)} %small_rows.1.small_ref, f32[512,1024]{1,0:T(8,128)} %xhat.4.refs_0_.x0_ref.xhat_ref, f32[512,1024]{1,0:T(8,128)} %xhat.5.refs_1_.x1_ref, ...), custom_call_target="tpu_custom_call" | custom-call | flops 402500000 | tf_op jit(solution)/shard_map/qkv/pallas_call | solution.py:246
  83.4 4.3 %attn_fwd.7 = (bf16[512,256]{1,0:T(8,128)(2,1)}, bf16[4,512,512]{2,1,0:T(8,128)(2,1)}) custom-call(s32[1]{0:T(128)} %collective-permute-done.11.len_ref, bf16[2048,768]{1,0:T(8,128)(2,1)} %get-tuple-element.173.qkv_ref, f32[4,4,128,128]{3,2,1,0:T(8,128)} %bias_tiles.1.tiles_ref), custom_call_target="tpu_custom_call" | custom-call | flops 517500000 | tf_op jit(solution)/shard_map/attn_fwd/pallas_call | solution.py:346
  88.1 4.4 %attn_fwd.5 = (bf16[512,256]{1,0:T(8,128)(2,1)}, bf16[4,512,512]{2,1,0:T(8,128)(2,1)}) custom-call(s32[1]{0:T(128)} %collective-permute-done.10.len_ref, bf16[2048,768]{1,0:T(8,128)(2,1)} %get-tuple-element.173.qkv_ref, f32[4,4,128,128]{3,2,1,0:T(8,128)} %bias_tiles.1.tiles_ref), custom_call_target="tpu_custom_call" | custom-call | flops 517500000 | tf_op jit(solution)/shard_map/attn_fwd/pallas_call | solution.py:346
  94.1 4.4 %attn_fwd.6 = (bf16[512,256]{1,0:T(8,128)(2,1)}, bf16[4,512,512]{2,1,0:T(8,128)(2,1)}) custom-call(s32[1]{0:T(128)} %collective-permute-done.5.len_ref, bf16[2048,768]{1,0:T(8,128)(2,1)} %get-tuple-element.173.qkv_ref, f32[4,4,128,128]{3,2,1,0:T(8,128)} %bias_tiles.1.tiles_ref), custom_call_target="tpu_custom_call" | custom-call | flops 517500000 | tf_op jit(solution)/shard_map/attn_fwd/pallas_call | solution.py:346
  100.4 6.9 %collective-permute-done.18.refs_2_ = bf16[512,256]{1,0:T(8,128)(2,1)S(1)} collective-permute-done((bf16[512,256]{1,0:T(8,128)(2,1)}, bf16[512,256]{1,0:T(8,128)(2,1)S(1)}, u32[]{:S(2)}, u32[]{:S(2)}) %collective-permute-start.18) | collective-permute-done | bytes 262176 | tf_op jit(solution)/shard_map/ppermute | solution.py:904
  107.4 3.9 %attn_fwd.4 = (bf16[512,256]{1,0:T(8,128)(2,1)}, bf16[4,512,512]{2,1,0:T(8,128)(2,1)}) custom-call(s32[1]{0:T(128)} %copy.64.len_ref, bf16[2048,768]{1,0:T(8,128)(2,1)} %get-tuple-element.173.qkv_ref, f32[4,4,128,128]{3,2,1,0:T(8,128)} %bias_tiles.1.tiles_ref), custom_call_target="tpu_custom_call" | custom-call | flops 517500000 | tf_op jit(solution)/shard_map/attn_fwd/pallas_call | solution.py:346
  112.2 3.9 %out_ln2.2 = (f32[512,1024]{1,0:T(8,128)}, bf16[512,1024]{1,0:T(8,128)(2,1)}, bf16[256,1024]{1,0:T(8,128)(2,1)}) custom-call(s32[1]{0:T(128)} %bitcast.n_ref, s32[1]{0:T(128)} %copy.64.len_ref, bf16[512,1024]{1,0:T(8,128)(2,1)} %tok_ref.5, f32[8,1024]{1,0:T(8,128)} %small_rows.1.small_ref, bf16[512,256]{1,0:T(8,128)(2,1)} %get-tuple-element.174.refs_0_.att_ref, ...), custom_call_target="tpu_custom_call" | custom-call | flops 71875000 | tf_op jit(solution)/shard_map/out_ln2/pallas_call | solution.py:510
  116.1 3.9 %out_ln2.3 = (f32[512,1024]{1,0:T(8,128)}, bf16[512,1024]{1,0:T(8,128)(2,1)}, bf16[256,1024]{1,0:T(8,128)(2,1)}) custom-call(s32[1]{0:T(128)} %bitcast.n_ref, s32[1]{0:T(128)} %copy.64.len_ref, bf16[512,1024]{1,0:T(8,128)(2,1)} %tok_ref.5, f32[8,1024]{1,0:T(8,128)} %small_rows.1.small_ref, ...), custom_call_target="tpu_custom_call", output_to_operand_aliasing={{0}: (12, {}), {1}: (13, {})} | custom-call | flops 71875000 | tf_op jit(solution)/shard_map/out_ln2/pallas_call | solution.py:510
  125.8 16.6 %ffn.3 = (f32[512,1024]{1,0:T(8,128)}, f32[512,1024]{1,0:T(8,128)}, bf16[512,1024]{1,0:T(8,128)(2,1)}, bf16[128,1024]{1,0:T(8,128)(2,1)}, bf16[128,1024]{1,0:T(8...) custom-call(bf16[8,2,128,1024]{3,2,1,0:T(8,128)(2,1)} %bitcast.118, ...), custom_call_target="tpu_custom_call" | custom-call | flops 215624992 | tf_op jit(solution)/shard_map/ffn/pallas_call | solution.py:701
  146.3 10.5 %ffn.4 = (f32[256,1024]{1,0:T(8,128)}, f32[256,1024]{1,0:T(8,128)}, bf16[256,1024]{1,0:T(8,128)(2,1)}, bf16[64,1024]{1,0:T(8,128)(2,1)}, bf16[64,1024]{1,0:T(8,1...) custom-call(bf16[8,2,128,1024]{3,2,1,0:T(8,128)(2,1)} %bitcast.119, ...), custom_call_target="tpu_custom_call", output_to_operand_aliasing={{7}: (8, {}), {8}: (9, {}), {9}: (10, {}), {10}: (11, {})} | custom-call | flops 143750000 | tf_op jit(solution)/shard_map/ffn/pallas_call | solution.py:701
  163.0 10.5 %ffn.5 = (f32[256,1024]{1,0:T(8,128)}, f32[256,1024]{1,0:T(8,128)}, bf16[256,1024]{1,0:T(8,128)(2,1)}, bf16[64,1024]{1,0:T(8,128)(2,1)}, bf16[64,1024]{1,0:T(8,1...) custom-call(bf16[8,2,128,1024]{3,2,1,0:T(8,128)(2,1)} %bitcast.120, ...), custom_call_target="tpu_custom_call", output_to_operand_aliasing={{7}: (8, {}), {8}: (9, {}), {9}: (10, {}), {10}: (11, {})} | custom-call | flops 143750000 | tf_op jit(solution)/shard_map/ffn/pallas_call | solution.py:701
  178.2 8.2 %convolution_convert_fusion.1 = bf16[1024,1024]{1,0:T(8,128)(2,1)S(1)} fusion(bf16[2048,1024]{1,0:T(8,128)(2,1)} %get-tuple-element.226, bf16[2048,1024]{1,0:T(8,128)(2,1)} %get-tuple-element.228), kind=kOutput, calls=%fused_computation.5 | convolution fusion | flops 4296015872 | bytes 10485760 | tf_op jit(solution)/shard_map/dot_general | solution.py:32
  186.4 5.0 %convolution_convert_fusion = bf16[1024,1024]{1,0:T(8,128)(2,1)S(1)} fusion(bf16[2048,1024]{1,0:T(8,128)(2,1)S(1)} %copy-done.2, bf16[2048,1024]{1,0:T(8,128)(2,1)S(1)} %copy-done.1), kind=kOutput, calls=%fused_computation.4 | convolution fusion | flops 4296015872 | bytes 10485760 | tf_op jit(solution)/shard_map/dot_general | solution.py:32
  195.2 5.1 %ln2_back.2 = (f32[512,1024]{1,0:T(8,128)}, bf16[512,512]{1,0:T(8,128)(2,1)}, bf16[512,512]{1,0:T(8,128)(2,1)}, bf16[512,256]{1,0:T(8,128)(2,1)}, bf16[512,256]{...) custom-call(s32[1]{0:T(128)} %bitcast.n_ref, s32[1]{0:T(128)} %copy.64.len_ref, ...), custom_call_target="tpu_custom_call" | custom-call | flops 5750000128 | tf_op jit(solution)/shard_map/ln2_back/pallas_call | solution.py:569
  201.2 5.2 %ln2_back.3 = (f32[512,1024]{1,0:T(8,128)}, bf16[512,512]{1,0:T(8,128)(2,1)}, bf16[512,512]{1,0:T(8,128)(2,1)}, bf16[512,256]{1,0:T(8,128)(2,1)}, bf16[512,256]{...) custom-call(s32[1]{0:T(128)} %bitcast.n_ref, ...), custom_call_target="tpu_custom_call", output_to_operand_aliasing={{0}: (13, {}), {1}: (14, {}), {2}: (15, {}), {3}: (16, {}),... | custom-call | flops 5750000128 | tf_op jit(solution)/shard_map/ln2_back/pallas_call | solution.py:569
  210.3 4.7 %attn_bwd.4 = (bf16[2048,768]{1,0:T(8,128)(2,1)}, f32[2,2,512]{2,1,0:T(2,128)}) custom-call(bf16[2048,768]{1,0:T(8,128)(2,1)} %get-tuple-element.173.qkv_ref, bf16[512,256]{1,0:T(8,128)(2,1)} %get-tuple-element.234.ga_ref, bf16[512,256]{1,0:T(8,128)(2,1)} %get-tuple-element.174.refs_0_.att_ref, bf16[4,512,512]{2,1,0:T(8,128)(2,1)} %get-tuple-element.235.p_ref), custom_call_target="tpu_custom_call" | custom-call | flops 1150000000 | tf_op jit(solution)/shard_map/attn_bwd/pallas_call | solution.py:431
  227.5 5.0 %attn_bwd.5 = (bf16[2048,768]{1,0:T(8,128)(2,1)}, f32[2,2,512]{2,1,0:T(2,128)}) custom-call(bf16[2048,768]{1,0:T(8,128)(2,1)} %get-tuple-element.173.qkv_ref, bf16[512,256]{1,0:T(8,128)(2,1)} %copy-done.48, bf16[512,256]{1,0:T(8,128)(2,1)} %get-tuple-element.177.att_ref, ...), custom_call_target="tpu_custom_call", output_to_operand_aliasing={{0}: (4, {})} | custom-call | flops 1150000000 | tf_op jit(solution)/shard_map/attn_bwd/pallas_call | solution.py:431
  232.8 4.6 %attn_bwd.6 = (bf16[2048,768]{1,0:T(8,128)(2,1)}, f32[2,2,512]{2,1,0:T(2,128)}) custom-call(bf16[2048,768]{1,0:T(8,128)(2,1)} %get-tuple-element.173.qkv_ref, bf16[512,256]{1,0:T(8,128)(2,1)} %copy-done.47, bf16[512,256]{1,0:T(8,128)(2,1)} %get-tuple-element.178.att_ref, ...), custom_call_target="tpu_custom_call", output_to_operand_aliasing={{0}: (4, {})} | custom-call | flops 1150000000 | tf_op jit(solution)/shard_map/attn_bwd/pallas_call | solution.py:431
  238.7 7.3 %ln1_back.2 = (bf16[512,1024]{1,0:T(8,128)(2,1)}, bf16[512,1024]{1,0:T(8,128)(2,1)}, f32[2,1024]{1,0:T(2,128)}) custom-call(bf16[2048,768]{1,0:T(8,128)(2,1)} %get-tuple-element.254.gp_ref.refs_0_, bf16[1024,768]{1,0:T(8,128)(2,1)} %get-tuple-element.255.wq_ref, f32[512,1024]{1,0:T(8,128)} %xhat.6.refs_2_.x0_ref, f32[512,1024]{1,0:T(8,128)} %xhat.7.refs_3_.x1_ref), custom_call_target="tpu_custom_call" | custom-call | flops 575000000 | tf_op jit(solution)/shard_map/ln1_back/pallas_call | solution.py:291
  250.3 4.6 %attn_bwd.7 = (bf16[2048,768]{1,0:T(8,128)(2,1)}, f32[2,2,512]{2,1,0:T(2,128)}) custom-call(bf16[2048,768]{1,0:T(8,128)(2,1)} %get-tuple-element.173.qkv_ref, bf16[512,256]{1,0:T(8,128)(2,1)} %copy-done.49, bf16[512,256]{1,0:T(8,128)(2,1)} %get-tuple-element.176.att_ref, ...), custom_call_target="tpu_custom_call", output_to_operand_aliasing={{0}: (4, {})} | custom-call | flops 1150000000 | tf_op jit(solution)/shard_map/attn_bwd/pallas_call | solution.py:431
  258.8 6.7 %convolution_convert_fusion.2 = bf16[1024,768]{1,0:T(8,128)(2,1)S(1)} fusion(bf16[2048,1024]{1,0:T(8,128)(2,1)} %get-tuple-element.188, bf16[2048,768]{1,0:T(8,128)(2,1)} %get-tuple-element.261.gp_ref), kind=kOutput, calls=%fused_computation.6 | convolution fusion | flops 3222011904 | bytes 8912896 | tf_op jit(solution)/shard_map/dot_general | solution.py:32
  272.4 7.8 %ln1_back.3 = (f32[512,1024]{1,0:T(8,128)}, bf16[512,1024]{1,0:T(8,128)(2,1)}, f32[2,1024]{1,0:T(2,128)}) custom-call(bf16[2048,768]{1,0:T(8,128)(2,1)} %get-tuple-element.261.gp_ref, bf16[1024,768]{1,0:T(8,128)(2,1)} %get-tuple-element.255.wq_ref, f32[512,1024]{1,0:T(8,128)} %xhat.4.refs_0_.x0_ref.xhat_ref, f32[512,1024]{1,0:T(8,128)} %xhat.5.refs_1_.x1_ref), custom_call_target="tpu_custom_call" | custom-call | flops 5750000128 | tf_op jit(solution)/shard_map/ln1_back/pallas_call | solution.py:291
  289.9 5.2 %collective-permute-done.71 = f32[4,8,128]{2,1,0:T(8,128)S(1)} collective-permute-done((f32[4,8,128]{2,1,0:T(8,128)}, f32[4,8,128]{2,1,0:T(8,128)S(1)}, u32[]{:S(2)}, u32[]{:S(2)}) %collective-permute-start.71) | collective-permute-done | bytes 16416 | tf_op jit(solution)/shard_map/ppermute | solution.py:911
  302.1 5.8 %ln1_last.1 = f32[512,1024]{1,0:T(8,128)} custom-call(bf16[512,1024]{1,0:T(8,128)(2,1)} %tok_ref.5, f32[512,1024]{1,0:T(8,128)} %xhat.4.refs_0_.x0_ref.xhat_ref, f32[512,1024]{1,0:T(8,128)} %get-tuple-element.282.gmid_ref, f32[8,1024]{1,0:T(8,128)} %small_rows.1.small_ref, f32[512,1024]{1,0:T(8,128)} %get-tuple-element.284.p0_ref, ...), custom_call_target="tpu_custom_call" | custom-call | flops 287500000 | tf_op jit(solution)/shard_map/ln1_last/pallas_call | solution.py:472
  324.9 3.9 %join_ffn.1 = (f32[128,4096]{1,0:T(8,128)}, f32[512,1024]{1,0:T(8,128)}) custom-call(s32[1]{0:T(128)} %bitcast.n_ref, bf16[128,2048]{1,0:T(8,128)(2,1)} %copy-done.8, bf16[128,2048]{1,0:T(8,128)(2,1)} %copy-done.27, bf16[128,2048]{1,0:T(8,128)(2,1)} %copy-done.24, bf16[128,2048]{1,0:T(8,128)(2,1)} %copy-done.30), custom_call_target="tpu_custom_call" | custom-call | flops 230000000 | tf_op jit(solution)/shard_map/join_ffn/pallas_call | solution.py:820
  (383 shorter events, 138.2 us)
Async XLA Ops:
  7.2 118.6 %all-gather.3.cloned.1.call-start = ((), (), s32[]{:S(2)}) async-start(), calls=%async_computation | async-start | bytes 4718592 | tf_op jit(solution)/shard_map/all_gather | solution.py:1070
  7.2 30.7 %collective-permute-start.7 = (bf16[512,1024]{1,0:T(8,128)(2,1)}, bf16[512,1024]{1,0:T(8,128)(2,1)S(1)}, u32[]{:S(2)}, u32[]{:S(2)}) collective-permute-start(bf16[512,1024]{1,0:T(8,128)(2,1)} %tok_ref.5), channel_id=1, source_target_pairs={{0,8},{8,0},{16,24},{24,16},{1,9},{9,1},{17,25},{25,17},{2,10},{10... | collective-permute-start | bytes 3145736 | tf_op jit(solution)/shard_map/ppermute | solution.py:904
  8.8 16.4 %collective-permute-start.2 = (bf16[224,1024]{1,0:T(8,128)(2,1)S(1)}, bf16[224,1024]{1,0:T(8,128)(2,1)}, u32[]{:S(2)}, u32[]{:S(2)}) collective-permute-start(bf16[224,1024]{1,0:T(8,128)(2,1)S(1)} %slice.51), channel_id=1, source_target_pairs={{0,16},{8,24},{16,0},{24,8},{1,17},{9,25},{17,1},{25,9},{2,18},{10... | collective-permute-start | bytes 1376264 | tf_op jit(solution)/shard_map/ppermute | solution.py:904
  17.5 24.6 %collective-permute-start.6 = (bf16[288,1024]{1,0:T(8,128)(2,1)S(1)}, bf16[288,1024]{1,0:T(8,128)(2,1)}, u32[]{:S(2)}, u32[]{:S(2)}) collective-permute-start(bf16[288,1024]{1,0:T(8,128)(2,1)S(1)} %slice.52), channel_id=1, source_target_pairs={{0,16},{8,24},{16,0},{24,8},{1,17},{9,25},{17,1},{25,9},{2,18},{10... | collective-permute-start | bytes 1769480 | tf_op jit(solution)/shard_map/ppermute | solution.py:904
  27.2 14.9 %collective-permute-start.5 = (s32[1]{0:T(128)}, s32[1]{0:T(128)}, u32[]{:S(2)}, u32[]{:S(2)}) collective-permute-start(s32[1]{0:T(128)} %param.14), channel_id=1, source_target_pairs={{0,16},{8,24},{16,0},{24,8},{1,17},{9,25},{17,1},{25,9},{2,18},{10... | collective-permute-start | bytes 20 | tf_op jit(solution)/shard_map/ppermute | solution.py:904
  53.9 33.8 %collective-permute-start.16 = (bf16[512,1024]{1,0:T(8,128)(2,1)S(1)}, bf16[512,1024]{1,0:T(8,128)(2,1)S(1)}, u32[]{:S(2)}, u32[]{:S(2)}) collective-permute-start(bf16[512,1024]{1,0:T(8,128)(2,1)S(1)} %multiply_convert_fusion.refs_4_), channel_id=1, source_target_pairs={{0,16},{8,24},{16,0},{24,8},{1,17},{9,25},{17,1},{25,9},{2,18},{10... | collective-permute-start | bytes 3145736 | tf_op jit(solution)/shard_map/ppermute | solution.py:904
  58.5 63.7 %collective-permute-start.13 = (bf16[512,1024]{1,0:T(8,128)(2,1)S(1)}, bf16[512,1024]{1,0:T(8,128)(2,1)}, u32[]{:S(2)}, u32[]{:S(2)}) collective-permute-start(bf16[512,1024]{1,0:T(8,128)(2,1)S(1)} %multiply_convert_fusion.refs_4_), channel_id=1, source_target_pairs={{0,8},{8,0},{16,24},{24,16},{1,9},{9,1},{17,25},{25,17},{2,10},{10... | collective-permute-start | bytes 3145736 | tf_op jit(solution)/shard_map/ppermute | solution.py:904
  79.0 15.1 %collective-permute-start.21 = (bf16[1024,256]{1,0:T(8,128)(2,1)}, bf16[1024,256]{1,0:T(8,128)(2,1)}, u32[]{:S(2)}, u32[]{:S(2)}) collective-permute-start(bf16[1024,256]{1,0:T(8,128)(2,1)} %get-tuple-element.179.refs_4_.refs_2_), channel_id=1, source_target_pairs={{0,16},{8,24},{16,0},{24,8},{1,17},{9,25},{17,1},{25,9},{2,18},{10... | collective-permute-start | bytes 1572872 | tf_op jit(solution)/shard_map/ppermute | solution.py:904
  80.8 30.5 %collective-permute-start.20 = (bf16[1024,256]{1,0:T(8,128)(2,1)}, bf16[1024,256]{1,0:T(8,128)(2,1)}, u32[]{:S(2)}, u32[]{:S(2)}) collective-permute-start(bf16[1024,256]{1,0:T(8,128)(2,1)} %get-tuple-element.179.refs_4_.refs_2_), channel_id=1, source_target_pairs={{0,8},{8,0},{16,24},{24,16},{1,9},{9,1},{17,25},{25,17},{2,10},{10... | collective-permute-start | bytes 1572872 | tf_op jit(solution)/shard_map/ppermute | solution.py:904
  94.1 17.2 %collective-permute-start.22 = (bf16[1024,256]{1,0:T(8,128)(2,1)}, bf16[1024,256]{1,0:T(8,128)(2,1)S(1)}, u32[]{:S(2)}, u32[]{:S(2)}) collective-permute-start(bf16[1024,256]{1,0:T(8,128)(2,1)} %collective-permute-done.21.refs_6_.refs_4_), channel_id=1, source_target_pairs={{0,8},{8,0},{16,24},{24,16},{1,9},{9,1},{17,25},{25,17},{2,10},{10... | collective-permute-start | bytes 1572872 | tf_op jit(solution)/shard_map/ppermute | solution.py:904
  107.4 36.8 %collective-permute-start.31 = (bf16[512,1024]{1,0:T(8,128)(2,1)S(1)}, bf16[512,1024]{1,0:T(8,128)(2,1)S(1)}, u32[]{:S(2)}, u32[]{:S(2)}) collective-permute-start(bf16[512,1024]{1,0:T(8,128)(2,1)S(1)} %collective-permute-done.16.refs_5_), channel_id=1, source_target_pairs={{0,8},{8,0},{16,24},{24,16},{1,9},{9,1},{17,25},{25,17},{2,10},{10... | collective-permute-start | bytes 3145736 | tf_op jit(solution)/shard_map/ppermute | solution.py:904
  120.5 21.9 %collective-permute-start.26 = (bf16[256,1024]{1,0:T(8,128)(2,1)}, bf16[256,1024]{1,0:T(8,128)(2,1)}, u32[]{:S(2)}, u32[]{:S(2)}) collective-permute-start(bf16[256,1024]{1,0:T(8,128)(2,1)} %get-tuple-element.185.refs_0_), channel_id=1, source_target_pairs={{0,16},{8,24},{16,0},{24,8},{1,17},{9,25},{17,1},{25,9},{2,18},{10... | collective-permute-start | bytes 1572872 | tf_op jit(solution)/shard_map/ppermute | solution.py:904
  122.2 35.7 %collective-permute-start.25 = (bf16[256,1024]{1,0:T(8,128)(2,1)}, bf16[256,1024]{1,0:T(8,128)(2,1)S(1)}, u32[]{:S(2)}, u32[]{:S(2)}) collective-permute-start(bf16[256,1024]{1,0:T(8,128)(2,1)} %get-tuple-element.186.refs_1_), channel_id=1, source_target_pairs={{0,16},{8,24},{16,0},{24,8},{1,17},{9,25},{17,1},{25,9},{2,18},{10... | collective-permute-start | bytes 1572872 | tf_op jit(solution)/shard_map/ppermute | solution.py:904
  160.6 16.9 %collective-permute-start.47 = (bf16[256,1024]{1,0:T(8,128)(2,1)S(1)}, bf16[256,1024]{1,0:T(8,128)(2,1)S(1)}, u32[]{:S(2)}, u32[]{:S(2)}) collective-permute-start(bf16[256,1024]{1,0:T(8,128)(2,1)S(1)} %add_convert_fusion.12), channel_id=1, source_target_pairs={{0,16},{8,24},{16,0},{24,8},{1,17},{9,25},{17,1},{25,9},{2,18},{10... | collective-permute-start | bytes 1572872 | tf_op jit(solution)/shard_map/ppermute | solution.py:904
  175.1 17.9 %collective-permute-start.48 = (bf16[128,1024]{1,0:T(8,128)(2,1)S(1)}, bf16[128,1024]{1,0:T(8,128)(2,1)S(1)}, u32[]{:S(2)}, u32[]{:S(2)}) collective-permute-start(bf16[128,1024]{1,0:T(8,128)(2,1)S(1)} %copy-done.70), channel_id=1, source_target_pairs={{0,8},{8,0},{16,24},{24,16},{1,9},{9,1},{17,25},{25,17},{2,10},{10... | collective-permute-start | bytes 786440 | tf_op jit(solution)/shard_map/ppermute | solution.py:904
  175.3 18.4 %collective-permute-start.49 = (bf16[128,1024]{1,0:T(8,128)(2,1)S(1)}, bf16[128,1024]{1,0:T(8,128)(2,1)S(1)}, u32[]{:S(2)}, u32[]{:S(2)}) collective-permute-start(bf16[128,1024]{1,0:T(8,128)(2,1)S(1)} %copy-done.69), channel_id=1, source_target_pairs={{0,8},{8,0},{16,24},{24,16},{1,9},{9,1},{17,25},{25,17},{2,10},{10... | collective-permute-start | bytes 786440 | tf_op jit(solution)/shard_map/ppermute | solution.py:904
  175.7 24.6 %collective-permute-start.45 = (bf16[128,1024]{1,0:T(8,128)(2,1)S(1)}, bf16[128,1024]{1,0:T(8,128)(2,1)S(1)}, u32[]{:S(2)}, u32[]{:S(2)}) collective-permute-start(bf16[128,1024]{1,0:T(8,128)(2,1)S(1)} %copy-done.68), channel_id=1, source_target_pairs={{0,8},{8,0},{16,24},{24,16},{1,9},{9,1},{17,25},{25,17},{2,10},{10... | collective-permute-start | bytes 786440 | tf_op jit(solution)/shard_map/ppermute | solution.py:904
  175.8 24.4 %collective-permute-start.46 = (bf16[128,1024]{1,0:T(8,128)(2,1)S(1)}, bf16[128,1024]{1,0:T(8,128)(2,1)S(1)}, u32[]{:S(2)}, u32[]{:S(2)}) collective-permute-start(bf16[128,1024]{1,0:T(8,128)(2,1)S(1)} %copy-done.67), channel_id=1, source_target_pairs={{0,8},{8,0},{16,24},{24,16},{1,9},{9,1},{17,25},{25,17},{2,10},{10... | collective-permute-start | bytes 786440 | tf_op jit(solution)/shard_map/ppermute | solution.py:904
  177.6 22.7 %collective-permute-start.44 = (bf16[256,1024]{1,0:T(8,128)(2,1)S(1)}, bf16[256,1024]{1,0:T(8,128)(2,1)S(1)}, u32[]{:S(2)}, u32[]{:S(2)}) collective-permute-start(bf16[256,1024]{1,0:T(8,128)(2,1)S(1)} %add_convert_fusion.11), channel_id=1, source_target_pairs={{0,16},{8,24},{16,0},{24,8},{1,17},{9,25},{17,1},{25,9},{2,18},{10... | collective-permute-start | bytes 1572872 | tf_op jit(solution)/shard_map/ppermute | solution.py:904
  193.1 14.8 %collective-permute-start.53 = (bf16[128,2048]{1,0:T(8,128)(2,1)S(1)}, bf16[128,2048]{1,0:T(8,128)(2,1)S(1)}, u32[]{:S(2)}, u32[]{:S(2)}) collective-permute-start(bf16[128,2048]{1,0:T(8,128)(2,1)S(1)} %pad_maximum_fusion.1), channel_id=1, source_target_pairs={{2,0},{4,2},{6,4},{7,6},{5,7},{3,5},{1,3},{0,1},{9,8},{8,10},{10,1... | collective-permute-start | bytes 1572872 | tf_op jit(solution)/shard_map/ppermute | solution.py:898
  193.7 14.2 %collective-permute-start.52 = (bf16[128,2048]{1,0:T(8,128)(2,1)S(1)}, bf16[128,2048]{1,0:T(8,128)(2,1)S(1)}, u32[]{:S(2)}, u32[]{:S(2)}) collective-permute-start(bf16[128,2048]{1,0:T(8,128)(2,1)S(1)} %pad_maximum_fusion), channel_id=1, source_target_pairs={{0,2},{2,4},{4,6},{6,7},{7,5},{5,3},{3,1},{1,0},{8,9},{10,8},{12,1... | collective-permute-start | bytes 1572872 | tf_op jit(solution)/shard_map/ppermute | solution.py:898
  208.1 14.5 %collective-permute-start.57 = (bf16[128,2048]{1,0:T(8,128)(2,1)S(1)}, bf16[128,2048]{1,0:T(8,128)(2,1)S(1)}, u32[]{:S(2)}, u32[]{:S(2)}) collective-permute-start(bf16[128,2048]{1,0:T(8,128)(2,1)S(1)} %add_convert_fusion.9), channel_id=1, source_target_pairs={{2,0},{4,2},{6,4},{7,6},{5,7},{3,5},{1,3},{0,1},{9,8},{8,10},{10,1... | collective-permute-start | bytes 1572872 | tf_op jit(solution)/shard_map/ppermute | solution.py:898
  208.8 13.8 %collective-permute-start.56 = (bf16[128,2048]{1,0:T(8,128)(2,1)S(1)}, bf16[128,2048]{1,0:T(8,128)(2,1)S(1)}, u32[]{:S(2)}, u32[]{:S(2)}) collective-permute-start(bf16[128,2048]{1,0:T(8,128)(2,1)S(1)} %add_convert_fusion.10), channel_id=1, source_target_pairs={{0,2},{2,4},{4,6},{6,7},{7,5},{5,3},{3,1},{1,0},{8,9},{10,8},{12,1... | collective-permute-start | bytes 1572872 | tf_op jit(solution)/shard_map/ppermute | solution.py:898
  222.8 14.8 %collective-permute-start.61 = (bf16[128,2048]{1,0:T(8,128)(2,1)S(1)}, bf16[128,2048]{1,0:T(8,128)(2,1)S(1)}, u32[]{:S(2)}, u32[]{:S(2)}) collective-permute-start(bf16[128,2048]{1,0:T(8,128)(2,1)S(1)} %add_convert_fusion.6), channel_id=1, source_target_pairs={{2,0},{4,2},{6,4},{7,6},{5,7},{3,5},{1,3},{0,1},{9,8},{8,10},{10,1... | collective-permute-start | bytes 1572872 | tf_op jit(solution)/shard_map/ppermute | solution.py:898
  223.5 14.0 %collective-permute-start.60 = (bf16[128,2048]{1,0:T(8,128)(2,1)S(1)}, bf16[128,2048]{1,0:T(8,128)(2,1)S(1)}, u32[]{:S(2)}, u32[]{:S(2)}) collective-permute-start(bf16[128,2048]{1,0:T(8,128)(2,1)S(1)} %add_convert_fusion.7), channel_id=1, source_target_pairs={{0,2},{2,4},{4,6},{6,7},{7,5},{5,3},{3,1},{1,0},{8,9},{10,8},{12,1... | collective-permute-start | bytes 1572872 | tf_op jit(solution)/shard_map/ppermute | solution.py:898
  225.2 13.5 %collective-permute-start.59 = (bf16[256,1024]{1,0:T(8,128)(2,1)S(1)}, bf16[256,1024]{1,0:T(8,128)(2,1)S(1)}, u32[]{:S(2)}, u32[]{:S(2)}) collective-permute-start(bf16[256,1024]{1,0:T(8,128)(2,1)S(1)} %add_convert_fusion.8), channel_id=1, source_target_pairs={{0,16},{8,24},{16,0},{24,8},{1,17},{9,25},{17,1},{25,9},{2,18},{10... | collective-permute-start | bytes 1572872 | tf_op jit(solution)/shard_map/ppermute | solution.py:904
  257.5 13.6 %collective-permute-start.65 = (bf16[256,1024]{1,0:T(8,128)(2,1)S(1)}, bf16[256,1024]{1,0:T(8,128)(2,1)}, u32[]{:S(2)}, u32[]{:S(2)}) collective-permute-start(bf16[256,1024]{1,0:T(8,128)(2,1)S(1)} %get-tuple-element.336), channel_id=1, source_target_pairs={{0,16},{8,24},{16,0},{24,8},{1,17},{9,25},{17,1},{25,9},{2,18},{10... | collective-permute-start | bytes 1572872 | tf_op jit(solution)/shard_map/ppermute | solution.py:904
  266.4 15.8 %collective-permute-start.64 = (bf16[128,1280]{1,0:T(8,128)(2,1)}, bf16[128,1280]{1,0:T(8,128)(2,1)}, u32[]{:S(2)}, u32[]{:S(2)}) collective-permute-start(bf16[128,1280]{1,0:T(8,128)(2,1)} %pad_maximum_fusion.3), channel_id=1, source_target_pairs={{2,0},{4,2},{6,4},{7,6},{5,7},{3,5},{1,3},{0,1},{9,8},{8,10},{10,1... | collective-permute-start | bytes 983048 | tf_op jit(solution)/shard_map/ppermute | solution.py:898
  267.9 14.3 %collective-permute-start.63 = (bf16[128,1280]{1,0:T(8,128)(2,1)}, bf16[128,1280]{1,0:T(8,128)(2,1)}, u32[]{:S(2)}, u32[]{:S(2)}) collective-permute-start(bf16[128,1280]{1,0:T(8,128)(2,1)} %pad_maximum_fusion.2), channel_id=1, source_target_pairs={{0,2},{2,4},{4,6},{6,7},{7,5},{5,3},{3,1},{1,0},{8,9},{10,8},{12,1... | collective-permute-start | bytes 983048 | tf_op jit(solution)/shard_map/ppermute | solution.py:898
  289.9 20.8 %collective-permute-start.75 = (bf16[512,1024]{1,0:T(8,128)(2,1)}, bf16[512,1024]{1,0:T(8,128)(2,1)S(1)}, u32[]{:S(2)}, u32[]{:S(2)}) collective-permute-start(bf16[512,1024]{1,0:T(8,128)(2,1)} %get-tuple-element.288), channel_id=1, source_target_pairs={{0,8},{8,0},{16,24},{24,16},{1,9},{9,1},{17,25},{25,17},{2,10},{10... | collective-permute-start | bytes 3145736 | tf_op jit(solution)/shard_map/ppermute | solution.py:904
  301.3 22.0 %collective-permute-start.83 = (bf16[128,2048]{1,0:T(8,128)(2,1)S(1)}, bf16[128,2048]{1,0:T(8,128)(2,1)S(1)}, u32[]{:S(2)}, u32[]{:S(2)}) collective-permute-start(bf16[128,2048]{1,0:T(8,128)(2,1)S(1)} %add_convert_fusion.4.refs_0_), channel_id=1, source_target_pairs={{0,8},{8,0},{16,24},{24,16},{1,9},{9,1},{17,25},{25,17},{2,10},{10... | collective-permute-start | bytes 1572872 | tf_op jit(solution)/shard_map/ppermute | solution.py:904
  301.4 14.4 %collective-permute-start.77 = (bf16[256,1024]{1,0:T(8,128)(2,1)S(1)}, bf16[256,1024]{1,0:T(8,128)(2,1)}, u32[]{:S(2)}, u32[]{:S(2)}) collective-permute-start(bf16[256,1024]{1,0:T(8,128)(2,1)S(1)} %add_convert_fusion.3), channel_id=1, source_target_pairs={{0,16},{8,24},{16,0},{24,8},{1,17},{9,25},{17,1},{25,9},{2,18},{10... | collective-permute-start | bytes 1572872 | tf_op jit(solution)/shard_map/ppermute | solution.py:904
  (135 other events, 837.9 us)
Sparse Core Ops, SparseCore 0:
  51.9 73.8 all-gather.2
